TPU v7x, 768 devices: a whole 4x8x12 slice. The times are simulated.
768 devices in a mesh: gx: 32 (over z_lo, x, core), gy: 24 (over z_hi, y).
Axes of the slice: x: 4, y: 8, z: 12 (z_hi: 3, z_lo: 4; z = z_hi * 4 + z_lo), core: 2. Of those that a mesh axis runs over, the one named last changes fastest.
Arguments:
- start: float32 [19, 64, 192, 128], P(None, 'gx', 'gy'), may hold values from -6 to 6
- adjoint: float32 [19, 64, 192, 128], P(None, 'gx', 'gy'), may hold values from -6 to 6
- solid: int32 [64, 192, 128], P('gx', 'gy'), may hold values 0 or 1
- w_in: float32 [64, 19], replicated, may hold values from -1.25 to 1.25
- b_in: float32 [64], replicated, may hold values from -3 to 3
- w_out: float32 [19, 64], replicated, may hold values from -0.75 to 0.75
- b_out: float32 [19], replicated, may hold values from -1.5 to 1.5
Outputs:
- final_state: float32 [19, 64, 192, 128], P(None, 'gx', 'gy')
- grad_start: float32 [19, 64, 192, 128], P(None, 'gx', 'gy')
- grad_w_in: float32 [64, 19], replicated
- grad_b_in: float32 [64], replicated
- grad_w_out: float32 [19, 64], replicated
- grad_b_out: float32 [19], replicated
All inputs are finite; a program needn't handle non-finite values. No bound on the sum of `solid` on one device may be relied on, other than what follows from the above.
Results may differ from a plain program's by a relative error of at most 0.00016.
Values sent between devices are 32-bit elements; how exact they have to be, the bound alone decides.
No kernel may reach another device: no remote copies, remote signals or barrier semaphores. Data moves between devices by JAX's collectives and lax.ppermute only.
A program may use at most 32 MiB of HBM per device.

v0:
```python
import math

import jax
import jax.numpy as jnp
from jax import lax
from jax.sharding import PartitionSpec as P

STEPS = 3


velocities = (
    (0, 0, 0),
    (1, 0, 0),
    (-1, 0, 0),
    (0, 1, 0),
    (0, -1, 0),
    (0, 0, 1),
    (0, 0, -1),
    (1, 1, 0),
    (-1, -1, 0),
    (1, -1, 0),
    (-1, 1, 0),
    (1, 0, 1),
    (-1, 0, -1),
    (1, 0, -1),
    (-1, 0, 1),
    (0, 1, 1),
    (0, -1, -1),
    (0, 1, -1),
    (0, -1, 1),
)
opposite = (0, 2, 1, 4, 3, 6, 5, 8, 7, 10, 9, 12, 11, 14, 13, 16, 15, 18, 17)


def padded_2(x, sides, width):
    for axis, dim in sides:
        count, length = (lax.axis_size(axis), x.shape[dim])
        up = [(i, (i + 1) % count) for i in range(count)]
        down = [(j, i) for i, j in up]
        last = lax.slice_in_dim(x, length - width, length, axis=dim)
        first = lax.slice_in_dim(x, 0, width, axis=dim)
        before = lax.ppermute(last, axis, up)
        after = lax.ppermute(first, axis, down)
        x = jnp.concatenate([before, x, after], axis=dim)
    return x


def activate(state, w_in, b_in):
    flat = state.reshape(state.shape[0], -1)
    return jnp.tanh(jnp.dot(w_in, flat, precision=lax.Precision.HIGHEST) + b_in[:, None])


def collide(state, fluid, w_in, b_in, w_out, b_out):
    hidden_units = activate(state, w_in, b_in)
    change = jnp.dot(w_out, hidden_units, precision=lax.Precision.HIGHEST) + b_out[:, None]
    return state + fluid * change.reshape(state.shape)


def transport(post_state, orient):
    width_x = post_state.shape[1]
    width_y = post_state.shape[2]
    padded = padded_2(post_state, (("gx", 1), ("gy", 2)), 1)
    shifted = []
    for number in range(19):
        step_x = orient * velocities[number][0]
        step_y = orient * velocities[number][1]
        portion = padded[
            number, 1 - step_x : 1 - step_x + width_x, 1 - step_y : 1 - step_y + width_y, :
        ]
        shifted.append(jnp.roll(portion, orient * velocities[number][2], axis=2))
    return jnp.stack(shifted)


def reflect(field, solid):
    reflected = jnp.stack([field[other] for other in opposite])
    return jnp.where(solid[None] == 1, reflected, field)


def on_device(start, adjoint, solid, w_in, b_in, w_out, b_out):
    fluid = (1 - solid).astype(jnp.float32)[None]

    def advance(state):
        return reflect(transport(collide(state, fluid, w_in, b_in, w_out, b_out), 1), solid)

    states = [start]
    current = start
    for section in range(STEPS):
        current = advance(current)
    final_state = current
    current = start
    for section in range(STEPS - 1):
        current = advance(current)
        states.append(current)
    grad_state = adjoint
    sum_w_in = jnp.zeros(w_in.shape, jnp.float32)
    sum_b_in = jnp.zeros(b_in.shape, jnp.float32)
    sum_w_out = jnp.zeros(w_out.shape, jnp.float32)
    sum_b_out = jnp.zeros(b_out.shape, jnp.float32)
    contract = (((1,), (1,)), ((), ()))
    for section in reversed(range(STEPS)):
        state = states[section]
        grad_moved = reflect(grad_state, solid)
        grad_post = transport(grad_moved, -1)
        hidden_units = activate(state, w_in, b_in)
        grad_change = (fluid * grad_post).reshape(grad_post.shape[0], -1)
        sum_w_out = sum_w_out + lax.dot_general(
            grad_change, hidden_units, contract, precision=lax.Precision.HIGHEST
        )
        sum_b_out = sum_b_out + jnp.sum(grad_change, axis=1)
        grad_hidden = jnp.dot(w_out.T, grad_change, precision=lax.Precision.HIGHEST)
        grad_pre = grad_hidden * (1.0 - hidden_units * hidden_units)
        flat_state = state.reshape(state.shape[0], -1)
        sum_w_in = sum_w_in + lax.dot_general(
            grad_pre, flat_state, contract, precision=lax.Precision.HIGHEST
        )
        sum_b_in = sum_b_in + jnp.sum(grad_pre, axis=1)
        grad_state = grad_post + jnp.dot(w_in.T, grad_pre, precision=lax.Precision.HIGHEST).reshape(
            grad_post.shape
        )
    total_w_in, total_b_in, total_w_out, total_b_out = lax.psum(
        (sum_w_in, sum_b_in, sum_w_out, sum_b_out), ("gx", "gy")
    )
    cells_total = start.size // start.shape[0] * lax.axis_size("gx") * lax.axis_size("gy")
    factor = 1.0 / math.sqrt(cells_total)
    return (
        final_state,
        grad_state,
        total_w_in * factor,
        total_b_in * factor,
        total_w_out * factor,
        total_b_out * factor,
    )


def solution(mesh):
    return jax.shard_map(
        on_device,
        mesh=mesh,
        in_specs=(
            P(None, "gx", "gy", None),
            P(None, "gx", "gy", None),
            P("gx", "gy", None),
            P(),
            P(),
            P(),
            P(),
        ),
        out_specs=(P(None, "gx", "gy", None), P(None, "gx", "gy", None), P(), P(), P(), P()),
        check_vma=False,
    )
```

profile of v0, /device:TPU:1, one launch (start us, length us, event | category | flops | bytes accessed | tf_op | source)
XLA Modules:
  0.0 307.4 jit_solution(4867559433967294881)
XLA Ops:
  0.6 0.7 fusion.45
  1.4 0.9 pad.558
  2.4 0.6 copy-done.5
  3.0 0.6 fusion
  4.2 0.9 copy-done.3
  5.1 12.6 %collective-permute-start = (f32[19,1,8,128]{3,2,1,0:T(8,128)S(1)}, f32[19,1,8,128]{3,2,1,0:T(8,128)S(1)}, u32[]{:S(2)}, u32[]{:S(2)}) collective-permute-start(f32[19,1,8,128]{3,2,1,0:T(8,128)S(1)} %get-tuple-element.325), channel_id=1, source_target_pairs={{24,0},{48,24},{72,48},{96,72},{120,96},{144,120},{168,144},{192,1... | collective-permute-start | bytes 233480 | tf_op jit(solution)/shard_map/ppermute | solution.py:43
  17.7 1.9 collective-permute-start.1
  20.1 1.0 collective-permute-done.1
  21.1 12.4 %collective-permute-start.2 = (f32[19,4,1,128]{3,2,1,0:T(1,128)S(1)}, f32[19,4,1,128]{3,2,1,0:T(1,128)S(1)}, u32[]{:S(2)}, u32[]{:S(2)}) collective-permute-start(f32[19,4,1,128]{3,2,1,0:T(1,128)S(1)} %get-tuple-element.267), channel_id=1, source_target_pairs={{1,0},{2,1},{3,2},{4,3},{5,4},{6,5},{7,6},{8,7},{9,8},{10,9},{11,1... | collective-permute-start | bytes 116744 | tf_op jit(solution)/shard_map/ppermute | solution.py:43
  33.5 1.9 collective-permute-start.3
  35.4 8.8 %collective-permute-done.3 = f32[19,4,1,128]{3,2,1,0:T(1,128)S(1)} collective-permute-done((f32[19,4,1,128]{3,2,1,0:T(1,128)S(1)}, f32[19,4,1,128]{3,2,1,0:T(1,128)S(1)}, u32[]{:S(2)}, u32[]{:S(2)}) %collective-permute-start.3) | collective-permute-done | bytes 38944 | tf_op jit(solution)/shard_map/ppermute | solution.py:42
  46.4 0.6 fusion.1
  47.6 3.3 %collective-permute-start.13 = (f32[19,1,8,128]{3,2,1,0:T(8,128)S(1)}, f32[19,1,8,128]{3,2,1,0:T(8,128)S(1)}, u32[]{:S(2)}, u32[]{:S(2)}) collective-permute-start(f32[19,1,8,128]{3,2,1,0:T(8,128)S(1)} %get-tuple-element.309), channel_id=1, source_target_pairs={{0,24},{24,48},{48,72},{72,96},{96,120},{120,144},{144,168},{168,1... | collective-permute-start | bytes 233480 | tf_op jit(solution)/shard_map/ppermute | solution.py:42
  51.0 8.9 %collective-permute-start.12 = (f32[19,1,8,128]{3,2,1,0:T(8,128)S(1)}, f32[19,1,8,128]{3,2,1,0:T(8,128)S(1)}, u32[]{:S(2)}, u32[]{:S(2)}) collective-permute-start(f32[19,1,8,128]{3,2,1,0:T(8,128)S(1)} %get-tuple-element.310), channel_id=1, source_target_pairs={{24,0},{48,24},{72,48},{96,72},{120,96},{144,120},{168,144},{192,1... | collective-permute-start | bytes 233480 | tf_op jit(solution)/shard_map/ppermute | solution.py:43
  59.9 0.6 fusion.50
  60.5 7.5 %collective-permute-start.4 = (f32[19,1,8,128]{3,2,1,0:T(8,128)S(1)}, f32[19,1,8,128]{3,2,1,0:T(8,128)S(1)}, u32[]{:S(2)}, u32[]{:S(2)}) collective-permute-start(f32[19,1,8,128]{3,2,1,0:T(8,128)S(1)} %get-tuple-element.319), channel_id=1, source_target_pairs={{24,0},{48,24},{72,48},{96,72},{120,96},{144,120},{168,144},{192,1... | collective-permute-start | bytes 233480 | tf_op jit(solution)/shard_map/ppermute | solution.py:43
  68.0 1.9 collective-permute-start.5
  70.3 1.9 collective-permute-start.15
  72.2 9.4 %collective-permute-start.14 = (f32[19,4,1,128]{3,2,1,0:T(1,128)S(1)}, f32[19,4,1,128]{3,2,1,0:T(1,128)S(1)}, u32[]{:S(2)}, u32[]{:S(2)}) collective-permute-start(f32[19,4,1,128]{3,2,1,0:T(1,128)S(1)} %get-tuple-element.262), channel_id=1, source_target_pairs={{1,0},{2,1},{3,2},{4,3},{5,4},{6,5},{7,6},{8,7},{9,8},{10,9},{11,1... | collective-permute-start | bytes 116744 | tf_op jit(solution)/shard_map/ppermute | solution.py:43
  81.7 1.9 collective-permute-start.6
  83.6 3.4 %collective-permute-start.7 = (f32[19,4,1,128]{3,2,1,0:T(1,128)S(1)}, f32[19,4,1,128]{3,2,1,0:T(1,128)S(1)}, u32[]{:S(2)}, u32[]{:S(2)}) collective-permute-start(f32[19,4,1,128]{3,2,1,0:T(1,128)S(1)} %get-tuple-element.266), channel_id=1, source_target_pairs={{0,1},{1,2},{2,3},{3,4},{4,5},{5,6},{6,7},{7,8},{8,9},{9,10},{10,1... | collective-permute-start | bytes 116744 | tf_op jit(solution)/shard_map/ppermute | solution.py:42
  87.0 0.6 constant_dynamic-update-slice_fusion.150
  87.6 0.6 constant_dynamic-update-slice_fusion.149
  88.3 6.1 %collective-permute-done.7 = f32[19,4,1,128]{3,2,1,0:T(1,128)S(1)} collective-permute-done((f32[19,4,1,128]{3,2,1,0:T(1,128)S(1)}, f32[19,4,1,128]{3,2,1,0:T(1,128)S(1)}, u32[]{:S(2)}, u32[]{:S(2)}) %collective-permute-start.7) | collective-permute-done | bytes 38944 | tf_op jit(solution)/shard_map/ppermute | solution.py:42
  95.8 0.6 constant_dynamic-update-slice_fusion.148
  97.9 0.7 constant_dynamic-update-slice_fusion.146
  98.6 0.7 constant_dynamic-update-slice_fusion.145
  99.3 0.6 constant_dynamic-update-slice_fusion.144
  99.9 0.6 constant_dynamic-update-slice_fusion.143
  101.1 0.6 fusion.30
  102.9 0.6 fusion.2
  105.6 1.1 fusion.8
  106.8 1.3 fusion.56
  109.3 0.7 copy-done.26
  110.0 0.6 constant_dynamic-update-slice_fusion.53
  112.5 0.6 constant_dynamic-update-slice_fusion.49
  115.0 0.6 constant_dynamic-update-slice_fusion.45
  116.4 0.6 constant_dynamic-update-slice_fusion.43
  119.8 1.9 collective-permute-start.17
  121.8 4.1 %collective-permute-start.16 = (f32[19,1,8,128]{3,2,1,0:T(8,128)S(1)}, f32[19,1,8,128]{3,2,1,0:T(8,128)S(1)}, u32[]{:S(2)}, u32[]{:S(2)}) collective-permute-start(f32[19,1,8,128]{3,2,1,0:T(8,128)S(1)} %get-tuple-element.304), channel_id=1, source_target_pairs={{24,0},{48,24},{72,48},{96,72},{120,96},{144,120},{168,144},{192,1... | collective-permute-start | bytes 233480 | tf_op jit(solution)/shard_map/ppermute | solution.py:43
  125.9 0.6 constant_dynamic-update-slice_fusion.38
  126.7 0.8 collective-permute-done.16
  127.5 1.9 collective-permute-start.19
  129.5 9.6 %collective-permute-start.18 = (f32[19,4,1,128]{3,2,1,0:T(1,128)S(1)}, f32[19,4,1,128]{3,2,1,0:T(1,128)S(1)}, u32[]{:S(2)}, u32[]{:S(2)}) collective-permute-start(f32[19,4,1,128]{3,2,1,0:T(1,128)S(1)} %get-tuple-element.260), channel_id=1, source_target_pairs={{1,0},{2,1},{3,2},{4,3},{5,4},{6,5},{7,6},{8,7},{9,8},{10,9},{11,1... | collective-permute-start | bytes 116744 | tf_op jit(solution)/shard_map/ppermute | solution.py:43
  139.1 0.9 collective-permute-done.18
  141.7 0.8 fusion.57
  143.2 0.7 copy-done.2
  144.0 0.7 copy-done.31
  145.9 2.9 collective-permute-start.21
  148.8 8.0 %collective-permute-start.20 = (f32[19,1,8,128]{3,2,1,0:T(8,128)S(1)}, f32[19,1,8,128]{3,2,1,0:T(8,128)S(1)}, u32[]{:S(2)}, u32[]{:S(2)}) collective-permute-start(f32[19,1,8,128]{3,2,1,0:T(8,128)S(1)} %get-tuple-element.298), channel_id=1, source_target_pairs={{24,0},{48,24},{72,48},{96,72},{120,96},{144,120},{168,144},{192,1... | collective-permute-start | bytes 233480 | tf_op jit(solution)/shard_map/ppermute | solution.py:43
  156.9 7.5 %collective-permute-start.8 = (f32[19,1,8,128]{3,2,1,0:T(8,128)S(1)}, f32[19,1,8,128]{3,2,1,0:T(8,128)S(1)}, u32[]{:S(2)}, u32[]{:S(2)}) collective-permute-start(f32[19,1,8,128]{3,2,1,0:T(8,128)S(1)} %get-tuple-element.313), channel_id=1, source_target_pairs={{24,0},{48,24},{72,48},{96,72},{120,96},{144,120},{168,144},{192,1... | collective-permute-start | bytes 233480 | tf_op jit(solution)/shard_map/ppermute | solution.py:43
  164.4 1.9 collective-permute-start.9
  166.6 1.9 collective-permute-start.23
  168.5 10.0 %collective-permute-start.22 = (f32[19,4,1,128]{3,2,1,0:T(1,128)S(1)}, f32[19,4,1,128]{3,2,1,0:T(1,128)S(1)}, u32[]{:S(2)}, u32[]{:S(2)}) collective-permute-start(f32[19,4,1,128]{3,2,1,0:T(1,128)S(1)} %get-tuple-element.258), channel_id=1, source_target_pairs={{1,0},{2,1},{3,2},{4,3},{5,4},{6,5},{7,6},{8,7},{9,8},{10,9},{11,1... | collective-permute-start | bytes 116744 | tf_op jit(solution)/shard_map/ppermute | solution.py:43
  178.6 3.4 %collective-permute-start.10 = (f32[19,4,1,128]{3,2,1,0:T(1,128)S(1)}, f32[19,4,1,128]{3,2,1,0:T(1,128)S(1)}, u32[]{:S(2)}, u32[]{:S(2)}) collective-permute-start(f32[19,4,1,128]{3,2,1,0:T(1,128)S(1)} %get-tuple-element.263), channel_id=1, source_target_pairs={{1,0},{2,1},{3,2},{4,3},{5,4},{6,5},{7,6},{8,7},{9,8},{10,9},{11,1... | collective-permute-start | bytes 116744 | tf_op jit(solution)/shard_map/ppermute | solution.py:43
  182.0 1.9 collective-permute-start.11
  185.7 0.8 fusion.55
  186.4 6.3 %collective-permute-done.11 = f32[19,4,1,128]{3,2,1,0:T(1,128)S(1)} collective-permute-done((f32[19,4,1,128]{3,2,1,0:T(1,128)S(1)}, f32[19,4,1,128]{3,2,1,0:T(1,128)S(1)}, u32[]{:S(2)}, u32[]{:S(2)}) %collective-permute-start.11) | collective-permute-done | bytes 38944 | tf_op jit(solution)/shard_map/ppermute | solution.py:42
  196.4 0.6 copy-done.47
  197.1 106.7 %all-reduce = (f32[64,19]{0,1:T(8,128)S(1)}, f32[64]{0:T(128)S(1)}, f32[19,64]{1,0:T(8,128)S(1)}, f32[19]{0:T(128)S(1)}) all-reduce(f32[64,19]{0,1:T(8,128)S(1)} %convolution_add_fusion.8, f32[64]{0:T(128)S(1)} %add_add_fusion.1, f32[19,64]{1,0:T(8,128)S(1)} %convolution_add_fusion.6, ...), channel_id=1, replica_groups=mesh['gx'=32,'gy'=24] {'gx','gy'}, use_global_device_ids=true, to_apply=%region_0.1 | all-reduce | flops 2515 | bytes 20120 | tf_op jit(solution)/shard_map/psum | solution.py:120
  303.7 0.6 broadcast_multiply_fusion.1
  305.4 0.6 broadcast_multiply_fusion
  306.1 0.7 broadcast_select_fusion.9
  306.7 0.7 bitcast_add_fusion
  (426 shorter events, 29.5 us)
Async XLA Ops:
  0.6 3.0 copy-start
  2.3 0.7 copy-start.5
  4.1 0.9 copy-start.3
  5.1 14.5 %copy-start.24 = (s32[2,8,128]{2,1,0:T(8,128)S(1)}, s32[2,8,128]{2,1,0:T(8,128)}, u32[]{:S(2)}) copy-start(s32[2,8,128]{2,1,0:T(8,128)} %param.9) | copy-start | bytes 24580
  5.1 14.6 %copy-start.4 = (f32[19,2,8,128]{3,2,1,0:T(8,128)S(1)}, f32[19,2,8,128]{3,2,1,0:T(8,128)}, u32[]{:S(2)}) copy-start(f32[19,2,8,128]{3,2,1,0:T(8,128)} %param.8) | copy-start | bytes 466948
  5.1 14.9 %collective-permute-start = (f32[19,1,8,128]{3,2,1,0:T(8,128)S(1)}, f32[19,1,8,128]{3,2,1,0:T(8,128)S(1)}, u32[]{:S(2)}, u32[]{:S(2)}) collective-permute-start(f32[19,1,8,128]{3,2,1,0:T(8,128)S(1)} %get-tuple-element.325), channel_id=1, source_target_pairs={{24,0},{48,24},{72,48},{96,72},{120,96},{144,120},{168,144},{192,1... | collective-permute-start | bytes 233480 | tf_op jit(solution)/shard_map/ppermute | solution.py:43
  17.7 3.4 %collective-permute-start.1 = (f32[19,1,8,128]{3,2,1,0:T(8,128)S(1)}, f32[19,1,8,128]{3,2,1,0:T(8,128)S(1)}, u32[]{:S(2)}, u32[]{:S(2)}) collective-permute-start(f32[19,1,8,128]{3,2,1,0:T(8,128)S(1)} %get-tuple-element.326), channel_id=1, source_target_pairs={{0,24},{24,48},{48,72},{72,96},{96,120},{120,144},{144,168},{168,1... | collective-permute-start | bytes 233480 | tf_op jit(solution)/shard_map/ppermute | solution.py:42
  19.6 26.8 %copy-start.28 = (pred[2048]{0:T(1024)(128)(4,1)}, pred[2048]{0:T(1024)(128)(4,1)S(1)}, u32[]{:S(2)}) copy-start(pred[2048]{0:T(1024)(128)(4,1)S(1)} %fusion.87) | copy-start | bytes 6148
  19.9 27.6 %copy-start.25 = (pred[2,8,128]{2,1,0:T(8,128)(4,1)}, pred[2,8,128]{2,1,0:T(8,128)(4,1)S(1)}, u32[]{:S(2)}) copy-start(pred[2,8,128]{2,1,0:T(8,128)(4,1)S(1)} %broadcast_compare_fusion) | copy-start | bytes 6148
  21.1 23.2 %collective-permute-start.2 = (f32[19,4,1,128]{3,2,1,0:T(1,128)S(1)}, f32[19,4,1,128]{3,2,1,0:T(1,128)S(1)}, u32[]{:S(2)}, u32[]{:S(2)}) collective-permute-start(f32[19,4,1,128]{3,2,1,0:T(1,128)S(1)} %get-tuple-element.267), channel_id=1, source_target_pairs={{1,0},{2,1},{3,2},{4,3},{5,4},{6,5},{7,6},{8,7},{9,8},{10,9},{11,1... | collective-permute-start | bytes 116744 | tf_op jit(solution)/shard_map/ppermute | solution.py:43
  33.5 10.7 %collective-permute-start.3 = (f32[19,4,1,128]{3,2,1,0:T(1,128)S(1)}, f32[19,4,1,128]{3,2,1,0:T(1,128)S(1)}, u32[]{:S(2)}, u32[]{:S(2)}) collective-permute-start(f32[19,4,1,128]{3,2,1,0:T(1,128)S(1)} %get-tuple-element.268), channel_id=1, source_target_pairs={{0,1},{1,2},{2,3},{3,4},{4,5},{5,6},{6,7},{7,8},{8,9},{9,10},{10,1... | collective-permute-start | bytes 116744 | tf_op jit(solution)/shard_map/ppermute | solution.py:42
  47.6 22.6 %collective-permute-start.13 = (f32[19,1,8,128]{3,2,1,0:T(8,128)S(1)}, f32[19,1,8,128]{3,2,1,0:T(8,128)S(1)}, u32[]{:S(2)}, u32[]{:S(2)}) collective-permute-start(f32[19,1,8,128]{3,2,1,0:T(8,128)S(1)} %get-tuple-element.309), channel_id=1, source_target_pairs={{0,24},{24,48},{48,72},{72,96},{96,120},{120,144},{144,168},{168,1... | collective-permute-start | bytes 233480 | tf_op jit(solution)/shard_map/ppermute | solution.py:42
  51.0 19.3 %collective-permute-start.12 = (f32[19,1,8,128]{3,2,1,0:T(8,128)S(1)}, f32[19,1,8,128]{3,2,1,0:T(8,128)S(1)}, u32[]{:S(2)}, u32[]{:S(2)}) collective-permute-start(f32[19,1,8,128]{3,2,1,0:T(8,128)S(1)} %get-tuple-element.310), channel_id=1, source_target_pairs={{24,0},{48,24},{72,48},{96,72},{120,96},{144,120},{168,144},{192,1... | collective-permute-start | bytes 233480 | tf_op jit(solution)/shard_map/ppermute | solution.py:43
  60.5 21.2 %collective-permute-start.4 = (f32[19,1,8,128]{3,2,1,0:T(8,128)S(1)}, f32[19,1,8,128]{3,2,1,0:T(8,128)S(1)}, u32[]{:S(2)}, u32[]{:S(2)}) collective-permute-start(f32[19,1,8,128]{3,2,1,0:T(8,128)S(1)} %get-tuple-element.319), channel_id=1, source_target_pairs={{24,0},{48,24},{72,48},{96,72},{120,96},{144,120},{168,144},{192,1... | collective-permute-start | bytes 233480 | tf_op jit(solution)/shard_map/ppermute | solution.py:43
  68.0 13.6 %collective-permute-start.5 = (f32[19,1,8,128]{3,2,1,0:T(8,128)S(1)}, f32[19,1,8,128]{3,2,1,0:T(8,128)S(1)}, u32[]{:S(2)}, u32[]{:S(2)}) collective-permute-start(f32[19,1,8,128]{3,2,1,0:T(8,128)S(1)} %get-tuple-element.320), channel_id=1, source_target_pairs={{0,24},{24,48},{48,72},{72,96},{96,120},{120,144},{144,168},{168,1... | collective-permute-start | bytes 233480 | tf_op jit(solution)/shard_map/ppermute | solution.py:42
  70.3 27.0 %collective-permute-start.15 = (f32[19,4,1,128]{3,2,1,0:T(1,128)S(1)}, f32[19,4,1,128]{3,2,1,0:T(1,128)S(1)}, u32[]{:S(2)}, u32[]{:S(2)}) collective-permute-start(f32[19,4,1,128]{3,2,1,0:T(1,128)S(1)} %get-tuple-element.261), channel_id=1, source_target_pairs={{0,1},{1,2},{2,3},{3,4},{4,5},{5,6},{6,7},{7,8},{8,9},{9,10},{10,1... | collective-permute-start | bytes 116744 | tf_op jit(solution)/shard_map/ppermute | solution.py:42
  72.2 23.5 %collective-permute-start.14 = (f32[19,4,1,128]{3,2,1,0:T(1,128)S(1)}, f32[19,4,1,128]{3,2,1,0:T(1,128)S(1)}, u32[]{:S(2)}, u32[]{:S(2)}) collective-permute-start(f32[19,4,1,128]{3,2,1,0:T(1,128)S(1)} %get-tuple-element.262), channel_id=1, source_target_pairs={{1,0},{2,1},{3,2},{4,3},{5,4},{6,5},{7,6},{8,7},{9,8},{10,9},{11,1... | collective-permute-start | bytes 116744 | tf_op jit(solution)/shard_map/ppermute | solution.py:43
  81.7 12.7 %collective-permute-start.6 = (f32[19,4,1,128]{3,2,1,0:T(1,128)S(1)}, f32[19,4,1,128]{3,2,1,0:T(1,128)S(1)}, u32[]{:S(2)}, u32[]{:S(2)}) collective-permute-start(f32[19,4,1,128]{3,2,1,0:T(1,128)S(1)} %get-tuple-element.265), channel_id=1, source_target_pairs={{1,0},{2,1},{3,2},{4,3},{5,4},{6,5},{7,6},{8,7},{9,8},{10,9},{11,1... | collective-permute-start | bytes 116744 | tf_op jit(solution)/shard_map/ppermute | solution.py:43
  83.6 10.7 %collective-permute-start.7 = (f32[19,4,1,128]{3,2,1,0:T(1,128)S(1)}, f32[19,4,1,128]{3,2,1,0:T(1,128)S(1)}, u32[]{:S(2)}, u32[]{:S(2)}) collective-permute-start(f32[19,4,1,128]{3,2,1,0:T(1,128)S(1)} %get-tuple-element.266), channel_id=1, source_target_pairs={{0,1},{1,2},{2,3},{3,4},{4,5},{5,6},{6,7},{7,8},{8,9},{9,10},{10,1... | collective-permute-start | bytes 116744 | tf_op jit(solution)/shard_map/ppermute | solution.py:42
  88.3 6.1 %copy-start.1 = (f32[19,2,8,128]{3,2,1,0:T(8,128)}, f32[19,2,8,128]{3,2,1,0:T(8,128)S(1)}, u32[]{:S(2)}) copy-start(f32[19,2,8,128]{3,2,1,0:T(8,128)S(1)} %constant_dynamic-update-slice_fusion.54) | copy-start | bytes 466948
  94.6 2.2 copy-start.6
  95.2 1.5 copy-start.8
  95.3 1.4 copy-start.12
  95.4 1.4 copy-start.10
  95.5 1.3 copy-start.18
  95.5 1.2 copy-start.16
  95.6 1.2 copy-start.20
  95.7 1.1 copy-start.14
  104.5 0.7 copy-start.35
  104.5 0.7 copy-start.41
  104.5 0.7 copy-start.42
  104.6 0.7 copy-start.36
  104.6 0.7 copy-start.37
  104.6 0.7 copy-start.38
  104.6 0.7 copy-start.39
  104.6 0.8 copy-start.40
  104.6 0.8 copy-start.34
  104.6 0.8 copy-start.33
  104.6 0.8 copy-start.32
  109.3 0.7 copy-start.26
  110.6 0.7 copy-start.7
  114.3 0.7 copy-start.13
  115.0 0.7 copy-start.9
  115.7 0.7 copy-start.19
  116.4 0.7 copy-start.11
  117.1 0.7 copy-start.21
  117.8 0.7 copy-start.17
  118.5 0.7 copy-start.23
  119.2 6.6 %copy-start.15 = (f32[2,8,128]{2,1,0:T(8,128)S(1)}, f32[2,8,128]{2,1,0:T(8,128)}, u32[]{:S(2)}) copy-start(f32[2,8,128]{2,1,0:T(8,128)} %copy-done.14) | copy-start | bytes 24580
  119.8 6.8 %collective-permute-start.17 = (f32[19,1,8,128]{3,2,1,0:T(8,128)S(1)}, f32[19,1,8,128]{3,2,1,0:T(8,128)S(1)}, u32[]{:S(2)}, u32[]{:S(2)}) collective-permute-start(f32[19,1,8,128]{3,2,1,0:T(8,128)S(1)} %get-tuple-element.303), channel_id=1, source_target_pairs={{0,24},{24,48},{48,72},{72,96},{96,120},{120,144},{144,168},{168,1... | collective-permute-start | bytes 233480 | tf_op jit(solution)/shard_map/ppermute | solution.py:42
  121.8 5.7 %collective-permute-start.16 = (f32[19,1,8,128]{3,2,1,0:T(8,128)S(1)}, f32[19,1,8,128]{3,2,1,0:T(8,128)S(1)}, u32[]{:S(2)}, u32[]{:S(2)}) collective-permute-start(f32[19,1,8,128]{3,2,1,0:T(8,128)S(1)} %get-tuple-element.304), channel_id=1, source_target_pairs={{24,0},{48,24},{72,48},{96,72},{120,96},{144,120},{168,144},{192,1... | collective-permute-start | bytes 233480 | tf_op jit(solution)/shard_map/ppermute | solution.py:43
  127.5 12.5 %collective-permute-start.19 = (f32[19,4,1,128]{3,2,1,0:T(1,128)S(1)}, f32[19,4,1,128]{3,2,1,0:T(1,128)S(1)}, u32[]{:S(2)}, u32[]{:S(2)}) collective-permute-start(f32[19,4,1,128]{3,2,1,0:T(1,128)S(1)} %get-tuple-element.259), channel_id=1, source_target_pairs={{0,1},{1,2},{2,3},{3,4},{4,5},{5,6},{6,7},{7,8},{8,9},{9,10},{10,1... | collective-permute-start | bytes 116744 | tf_op jit(solution)/shard_map/ppermute | solution.py:42
  129.5 10.5 %collective-permute-start.18 = (f32[19,4,1,128]{3,2,1,0:T(1,128)S(1)}, f32[19,4,1,128]{3,2,1,0:T(1,128)S(1)}, u32[]{:S(2)}, u32[]{:S(2)}) collective-permute-start(f32[19,4,1,128]{3,2,1,0:T(1,128)S(1)} %get-tuple-element.260), channel_id=1, source_target_pairs={{1,0},{2,1},{3,2},{4,3},{5,4},{6,5},{7,6},{8,7},{9,8},{10,9},{11,1... | collective-permute-start | bytes 116744 | tf_op jit(solution)/shard_map/ppermute | solution.py:43
  143.0 0.9 copy-start.2
  144.0 0.7 copy-start.31
  145.9 20.6 %collective-permute-start.21 = (f32[19,1,8,128]{3,2,1,0:T(8,128)S(1)}, f32[19,1,8,128]{3,2,1,0:T(8,128)S(1)}, u32[]{:S(2)}, u32[]{:S(2)}) collective-permute-start(f32[19,1,8,128]{3,2,1,0:T(8,128)S(1)} %get-tuple-element.297), channel_id=1, source_target_pairs={{0,24},{24,48},{48,72},{72,96},{96,120},{120,144},{144,168},{168,1... | collective-permute-start | bytes 233480 | tf_op jit(solution)/shard_map/ppermute | solution.py:42
  148.8 17.7 %collective-permute-start.20 = (f32[19,1,8,128]{3,2,1,0:T(8,128)S(1)}, f32[19,1,8,128]{3,2,1,0:T(8,128)S(1)}, u32[]{:S(2)}, u32[]{:S(2)}) collective-permute-start(f32[19,1,8,128]{3,2,1,0:T(8,128)S(1)} %get-tuple-element.298), channel_id=1, source_target_pairs={{24,0},{48,24},{72,48},{96,72},{120,96},{144,120},{168,144},{192,1... | collective-permute-start | bytes 233480 | tf_op jit(solution)/shard_map/ppermute | solution.py:43
  156.9 21.6 %collective-permute-start.8 = (f32[19,1,8,128]{3,2,1,0:T(8,128)S(1)}, f32[19,1,8,128]{3,2,1,0:T(8,128)S(1)}, u32[]{:S(2)}, u32[]{:S(2)}) collective-permute-start(f32[19,1,8,128]{3,2,1,0:T(8,128)S(1)} %get-tuple-element.313), channel_id=1, source_target_pairs={{24,0},{48,24},{72,48},{96,72},{120,96},{144,120},{168,144},{192,1... | collective-permute-start | bytes 233480 | tf_op jit(solution)/shard_map/ppermute | solution.py:43
  164.4 14.0 %collective-permute-start.9 = (f32[19,1,8,128]{3,2,1,0:T(8,128)S(1)}, f32[19,1,8,128]{3,2,1,0:T(8,128)S(1)}, u32[]{:S(2)}, u32[]{:S(2)}) collective-permute-start(f32[19,1,8,128]{3,2,1,0:T(8,128)S(1)} %get-tuple-element.314), channel_id=1, source_target_pairs={{0,24},{24,48},{48,72},{72,96},{96,120},{120,144},{144,168},{168,1... | collective-permute-start | bytes 233480 | tf_op jit(solution)/shard_map/ppermute | solution.py:42
  166.6 17.4 %collective-permute-start.23 = (f32[19,4,1,128]{3,2,1,0:T(1,128)S(1)}, f32[19,4,1,128]{3,2,1,0:T(1,128)S(1)}, u32[]{:S(2)}, u32[]{:S(2)}) collective-permute-start(f32[19,4,1,128]{3,2,1,0:T(1,128)S(1)} %get-tuple-element.257), channel_id=1, source_target_pairs={{0,1},{1,2},{2,3},{3,4},{4,5},{5,6},{6,7},{7,8},{8,9},{9,10},{10,1... | collective-permute-start | bytes 116744 | tf_op jit(solution)/shard_map/ppermute | solution.py:42
  168.5 15.4 %collective-permute-start.22 = (f32[19,4,1,128]{3,2,1,0:T(1,128)S(1)}, f32[19,4,1,128]{3,2,1,0:T(1,128)S(1)}, u32[]{:S(2)}, u32[]{:S(2)}) collective-permute-start(f32[19,4,1,128]{3,2,1,0:T(1,128)S(1)} %get-tuple-element.258), channel_id=1, source_target_pairs={{1,0},{2,1},{3,2},{4,3},{5,4},{6,5},{7,6},{8,7},{9,8},{10,9},{11,1... | collective-permute-start | bytes 116744 | tf_op jit(solution)/shard_map/ppermute | solution.py:43
  178.6 14.4 %collective-permute-start.10 = (f32[19,4,1,128]{3,2,1,0:T(1,128)S(1)}, f32[19,4,1,128]{3,2,1,0:T(1,128)S(1)}, u32[]{:S(2)}, u32[]{:S(2)}) collective-permute-start(f32[19,4,1,128]{3,2,1,0:T(1,128)S(1)} %get-tuple-element.263), channel_id=1, source_target_pairs={{1,0},{2,1},{3,2},{4,3},{5,4},{6,5},{7,6},{8,7},{9,8},{10,9},{11,1... | collective-permute-start | bytes 116744 | tf_op jit(solution)/shard_map/ppermute | solution.py:43
  182.0 10.7 %collective-permute-start.11 = (f32[19,4,1,128]{3,2,1,0:T(1,128)S(1)}, f32[19,4,1,128]{3,2,1,0:T(1,128)S(1)}, u32[]{:S(2)}, u32[]{:S(2)}) collective-permute-start(f32[19,4,1,128]{3,2,1,0:T(1,128)S(1)} %get-tuple-element.264), channel_id=1, source_target_pairs={{0,1},{1,2},{2,3},{3,4},{4,5},{5,6},{6,7},{7,8},{8,9},{9,10},{10,1... | collective-permute-start | bytes 116744 | tf_op jit(solution)/shard_map/ppermute | solution.py:42
  305.4 0.7 copy-start.27
  (8 other events, 5.2 us)
where the time goes:
time: 309 us; the launch traced here: 307 us
  starting transfers between devices  122 us (39%)
  blocking collectives  107 us (35%)
  local copies, waits for them, and re-layouts  24.9 us (8%)
  waiting for transfers between devices  24 us (8%)
  other arithmetic  16.3 us (5%)
  matrix products  11 us (4%)
    psum x1, blocking collectives, on_device(): lax.psum((sum_w_in, sum_b_in, sum_w_out, sum_b_out), ('gx', 'gy'))  107 us
    ppermute x12, starting transfers between devices, padded_2(): after = lax.ppermute(first, axis, down)  95.3 us
    ppermute x12, starting transfers between devices, padded_2(): before = lax.ppermute(last, axis, up)  26.8 us
    ppermute x12, waiting for transfers between devices, padded_2(): before = lax.ppermute(last, axis, up)  22.2 us
    unnamed x203, local copies, waits for them, and re-layouts  17.4 us
    unnamed x94, other arithmetic  9.36 us
  transfers between devices with their start and end apart: 24, of which 6 were waited for; matrix products, arithmetic and copies ran while one was open for 3% of the time, Pallas kernels for 0%

commit v1 on v0

v1 whole, which is shorter than its diff:
```python
import functools
import math

import jax
import jax.numpy as jnp
from jax import lax
from jax.experimental import pallas as pl
from jax.experimental.pallas import tpu as pltpu
from jax.sharding import PartitionSpec as P

Q = 19
HID = 64
T = 24
ONE = 19
W = 128

velocities = (
    (0, 0, 0),
    (1, 0, 0),
    (-1, 0, 0),
    (0, 1, 0),
    (0, -1, 0),
    (0, 0, 1),
    (0, 0, -1),
    (1, 1, 0),
    (-1, -1, 0),
    (1, -1, 0),
    (-1, 1, 0),
    (1, 0, 1),
    (-1, 0, -1),
    (1, 0, -1),
    (-1, 0, 1),
    (0, 1, 1),
    (0, -1, -1),
    (0, 1, -1),
    (0, -1, 1),
)
opposite = (0, 2, 1, 4, 3, 6, 5, 8, 7, 10, 9, 12, 11, 14, 13, 16, 15, 18, 17)

order = tuple(sorted(range(Q), key=lambda k: -velocities[k][0]))
place = {k: i for i, k in enumerate(order)}
UNITS = 2 * Q + 1
SOLID = 2 * Q


def y_pieces(way):
    pieces = []
    for plane in range(2):
        for k in range(Q):
            pieces.append((plane, place[k], 3 + way * velocities[k][1]))
        for k in range(Q):
            pieces.append((plane, Q + place[k], 2 - way * velocities[k][1]))
        pieces.append((plane, SOLID, 3))
    return pieces


Y_ROWS = 200


def split(a):
    high = a.astype(jnp.bfloat16).astype(jnp.float32)
    return high, a - high


def stack3(high, low):
    parts = [high, low, high]
    if (3 * high.shape[0]) % 16:
        parts.append(jnp.zeros((8, high.shape[1]), jnp.float32))
    return jnp.concatenate(parts, axis=0).astype(jnp.bfloat16)


def weights3(a):
    high, low = split(a)
    parts = [high, high, low]
    if (3 * a.shape[1]) % 16:
        parts.append(jnp.zeros((a.shape[0], 8), jnp.float32))
    return jnp.concatenate(parts, axis=1)


def mm(a, b):
    return lax.dot_general(a, b, (((1,), (0,)), ((), ())), preferred_element_type=jnp.float32)


def mm_t(a, b):
    return lax.dot_general(a, b, (((1,), (1,)), ((), ())), preferred_element_type=jnp.float32)


def load_rows(ref, plane, first, count):
    return jnp.concatenate(
        [ref[plane, (first + i) * T : (first + i + 1) * T, :] for i in range(count)], axis=1
    )


def store_rows(ref, plane, first, count, value):
    for i in range(count):
        ref[plane, (first + i) * T : (first + i + 1) * T, :] = value[:, i * W : (i + 1) * W]


def get8(ref, plane, first, k):
    return ref[plane, pl.ds(first * T + k, 8, stride=T), :]


def put8(ref, plane, first, k, value):
    ref[plane, pl.ds(first * T + k, 8, stride=T), :] = value


def z_shift(value, step):
    if step == 0:
        return value
    return pltpu.roll(value, step % W, axis=1)


def pad_tile():
    row = lax.broadcasted_iota(jnp.int32, (8, W), 0)
    return jnp.where(row == ONE - 16, 1.0, 0.0).astype(jnp.float32)


def pad_rows(ref, plane, first, count):
    tile = pad_tile()
    for i in range(count):
        ref[plane, (first + i) * T + 16 : (first + i + 1) * T, :] = tile


def chunks(count, size):
    return [(i, min(size, count - i)) for i in range(0, count, size)]


def first_kernel(
    start, adjoint, solid, w_in, b_in, w_out, b_out,
    z, to_up, to_down, w1x, w2x, w2tx, w1tx, b2b,
    s0, p1, sq,
):
    sq[...] = jnp.zeros((128, 128), jnp.float32)
    sq[0:HID, 0:Q] = w_in[...]
    a1t = sq[...].T
    sq[...] = a1t
    sq[ONE : ONE + 1, 0:HID] = b_in[...]
    a1t = sq[0:T, 0:HID]
    a1 = sq[...].T[0:HID, 0:T]
    sq[...] = jnp.zeros((128, 128), jnp.float32)
    sq[0:Q, 0:HID] = w_out[...]
    a2 = sq[0:T, 0:HID]
    a2t = sq[...].T[0:HID, 0:T]
    sq[...] = jnp.zeros((128, 128), jnp.float32)
    sq[0:1, 0:Q] = b_out[...]
    b2 = jnp.broadcast_to(sq[...].T[0:T, 0:1], (T, W))
    w1 = weights3(a1)
    w2 = weights3(a2)
    w1x[...] = w1
    w2x[...] = w2
    w2tx[...] = weights3(a2t)
    w1tx[...] = weights3(a1t)
    b2b[...] = b2
    w1 = w1.astype(jnp.bfloat16)
    w2 = w2.astype(jnp.bfloat16)
    for plane in range(2):
        pad_rows(s0, plane, 0, 8)
        for k in range(Q):
            put8(s0, plane, 0, k, start[k, plane])
        sol = solid[plane].astype(jnp.float32)
        z[plane, SOLID, 4:12, :] = sol
        mask = sol > 0.5
        for k in range(Q):
            z[plane, Q + place[k], 4:12, :] = jnp.where(
                mask, adjoint[opposite[k], plane], adjoint[k, plane]
            )
    for plane in range(2):
        for first, count in chunks(8, 4):
            state = load_rows(s0, plane, first, count)
            hidden = jnp.tanh(mm(w1, stack3(*split(state))))
            change = mm(w2, stack3(*split(hidden)))
            for i in range(count):
                y = first + i
                fluid = 1.0 - solid[plane, y : y + 1, :].astype(jnp.float32)
                p1[plane, y * T : (y + 1) * T, :] = state[:, i * W : (i + 1) * W] + fluid * (
                    change[:, i * W : (i + 1) * W] + b2
                )
    for plane in range(2):
        for k in range(Q):
            z[plane, place[k], 4:12, :] = get8(p1, plane, 0, k)
    for ref, way in ((to_up, 1), (to_down, -1)):
        at = 0
        for plane, unit, rows in y_pieces(way):
            begin = 12 - rows if way == 1 else 4
            ref[at : at + rows, :] = z[plane, unit, begin : begin + rows, :]
            at += rows
        ref[at:, :] = jnp.zeros((Y_ROWS - at, W), jnp.float32)


def second_kernel(z_in, from_below, from_above, z, to_right, to_left):
    z[...] = z_in[...]
    for ref, way in ((from_below, 1), (from_above, -1)):
        at = 0
        for plane, unit, rows in y_pieces(way):
            begin = 4 - rows if way == 1 else 12
            z[plane, unit, begin : begin + rows, :] = ref[at : at + rows, :]
            at += rows
    for at, (plane, unit) in enumerate(far_units(1)):
        to_right[at] = z[plane, unit]
    for at, (plane, unit) in enumerate(far_units(-1)):
        to_left[at] = z[plane, unit]


def far_runs(way):
    if way == 1:
        return ((5, 0, 0), (14, 1, 0), (5, 1, Q + 14), (1, 1, SOLID))
    return ((5, 1, 14), (14, 0, 5), (5, 0, Q), (1, 0, SOLID))


def far_units(way):
    return [(plane, first + i) for count, plane, first in far_runs(way) for i in range(count)]


FAR = 25


PLANES = 10
ROWS = 16


def third_kernel(
    scale,
    start, z_own, z_left, z_right, f_left, f_right, w1x, w2x, w2tx, w1tx, b2b,
    final, grad, sums,
    zs, s0, s1, p2, s2, p3, gp, g, acc1, acc2, sems,
):
    copies = [(z_left, zs.at[2:4]), (z_own, zs.at[4:6]), (z_right, zs.at[6:8])]
    for ref, way, base in ((f_left, 1, 0), (f_right, -1, 8)):
        at = 0
        for count, plane, first in far_runs(way):
            copies.append((ref.at[at : at + count], zs.at[base + plane, first : first + count]))
            at += count
    copies = [pltpu.make_async_copy(a, b, sems.at[i]) for i, (a, b) in enumerate(copies)]
    for copy in copies:
        copy.start()

    w1 = w1x[...].astype(jnp.bfloat16)
    w2 = w2x[...].astype(jnp.bfloat16)
    w2t = w2tx[...].astype(jnp.bfloat16)
    w1t = w1tx[...].astype(jnp.bfloat16)
    b2 = b2b[...]
    acc1[...] = jnp.zeros(acc1.shape, jnp.float32)
    acc2[...] = jnp.zeros(acc2.shape, jnp.float32)
    tile = pad_tile()

    def init_pads(ref, planes, first, count):
        for plane in range(planes):
            pad_rows(ref, plane, first, count)

    init_pads(s0, 2, 0, 8)
    for plane in range(2):
        for k in range(Q):
            put8(s0, plane, 0, k, start[k, plane])
    for ref, planes in ((s1, 8), (s2, 6)):
        for plane in range(planes):
            pad_rows(ref, plane, 0, ROWS)
    for plane in range(6):
        for i in range(ROWS):
            gp[plane, i * T + 16 : (i + 1) * T, :] = jnp.zeros((8, W), jnp.float32)

    for copy in copies:
        copy.wait()

    def fluid_rows(x, y):
        return 1.0 - zs[x, SOLID, y : y + 1, :]

    def forward_hidden(state_parts):
        return jnp.tanh(mm(w1, stack3(*state_parts)))

    def collide(p_ref, p_plane, zx, first, count, state, hidden_parts):
        change = mm(w2, stack3(*hidden_parts))
        for i in range(count):
            y = first + i
            p_ref[p_plane, y * T : (y + 1) * T, :] = state[:, i * W : (i + 1) * W] + fluid_rows(
                zx, y
            ) * (change[:, i * W : (i + 1) * W] + b2)

    def backward(own, zx, first, count, state_parts, hidden, hidden_parts, grad_post):
        change = jnp.concatenate(
            [
                fluid_rows(zx, first + i) * grad_post[:, i * W : (i + 1) * W]
                for i in range(count)
            ],
            axis=1,
        )
        change_parts = split(change)
        grad_hidden = mm(w2t, stack3(*change_parts))
        grad_pre = grad_hidden * (1.0 - hidden * hidden)
        pre_parts = split(grad_pre)
        back = grad_post + mm(w1t, stack3(*pre_parts))
        low = max(first, 4)
        high = min(first + count, 12)

        if own and high > low:
            part = slice((low - first) * W, (high - first) * W)
            left = jnp.concatenate([a[:, part] for a in state_parts], axis=0)
            right = jnp.concatenate([a[:, part] for a in pre_parts + change_parts], axis=0)
            acc1[...] += mm_t(left.astype(jnp.bfloat16), right.astype(jnp.bfloat16))
            left = jnp.concatenate([a[:, part] for a in change_parts], axis=0)
            right = jnp.concatenate([a[:, part] for a in hidden_parts], axis=0)
            acc2[...] += mm_t(left.astype(jnp.bfloat16), right.astype(jnp.bfloat16))
        return back

    def over_planes(halo, body):
        if halo:
            lax.fori_loop(
                0,
                2 * halo,
                lambda i, c: body(False, jnp.where(i < halo, i, i + 2), c),
                0,
            )
        lax.fori_loop(0, 2, lambda i, c: body(True, i + halo, c), 0)

    def reflect(values, mask):
        return [jnp.where(mask, values[opposite[k]], values[k]) for k in range(Q)]

    def stage1(j, carry):
        zx = j + 1
        for y in (1, 7):
            moved = []
            for k in range(Q):
                cx, cy, cz = velocities[k]
                moved.append(z_shift(zs[zx - cx, place[k], y - cy : y - cy + 8, :], cz))
            moved = reflect(moved, zs[zx, SOLID, y : y + 8, :] > 0.5)
            for k in range(Q):
                put8(s1, j, y, k, moved[k])
        for first, count in chunks(14, 4):
            first += 1
            state = load_rows(s1, j, first, count)
            hidden = forward_hidden(split(state))
            collide(p2, j, zx, first, count, state, split(hidden))
        return carry

    lax.fori_loop(0, 8, stage1, 0)

    def stage2(own, j, carry):
        zx = j + 2
        for y in (2, 6):
            moved = []
            for k in range(Q):
                cx, cy, cz = velocities[k]
                moved.append(z_shift(get8(p2, j + 1 - cx, y - cy, k), cz))
            moved = reflect(moved, zs[zx, SOLID, y : y + 8, :] > 0.5)
            for k in range(Q):
                put8(s2, j, y, k, moved[k])
            for k in range(Q):
                cx, cy, cz = velocities[k]
                value = zs[zx + cx, Q + place[k], y + cy : y + cy + 8, :]
                put8(gp, j, y, k, z_shift(value, -cz))
        for first, count in chunks(12, 4):
            first += 2
            state = load_rows(s2, j, first, count)
            state_parts = split(state)
            hidden = forward_hidden(state_parts)
            hidden_parts = split(hidden)
            collide(p3, j, zx, first, count, state, hidden_parts)
            grad_post = load_rows(gp, j, first, count)
            back = backward(own, zx, first, count, state_parts, hidden, hidden_parts, grad_post)
            store_rows(g, j, first, count, back)
        return carry

    over_planes(2, stage2)

    for plane in range(2):
        moved = []
        for k in range(Q):
            cx, cy, cz = velocities[k]
            moved.append(z_shift(get8(p3, plane + 2 - cx, 4 - cy, k), cz))
        moved = reflect(moved, zs[plane + 4, SOLID, 4:12, :] > 0.5)
        for k in range(Q):
            final[k, plane] = moved[k]

    def run_back(g_ref, g_plane, zx, y, out_plane):
        for k in range(Q):
            cx, cy, cz = velocities[k]
            one = get8(g_ref, g_plane + cx, y + cy, k)
            if k != 0:
                other = get8(g_ref, g_plane + cx, y + cy, opposite[k])
                mask = zs[zx + cx, SOLID, y + cy : y + cy + 8, :] > 0.5
                one = jnp.where(mask, other, one)
            put8(gp, out_plane, y, k, z_shift(one, -cz))

    def stage3(own, j, carry):
        zx = j + 3
        for y in (3, 5):
            run_back(g, j + 1, zx, y, j)
        for first, count in ((3, 5), (8, 5)):
            state_parts = split(load_rows(s1, j + 2, first, count))
            hidden = forward_hidden(state_parts)
            grad_post = load_rows(gp, j, first, count)
            back = backward(own, zx, first, count, state_parts, hidden, split(hidden), grad_post)
            store_rows(p2, j, first, count, back)
        return carry

    over_planes(1, stage3)

    def stage4(own, j, carry):
        zx = j + 4
        run_back(p2, j + 1, zx, 4, j)
        for first, count in ((4, 4), (8, 4)):
            state_parts = split(load_rows(s0, j, first - 4, count))
            hidden = forward_hidden(state_parts)
            grad_post = load_rows(gp, j, first, count)
            back = backward(own, zx, first, count, state_parts, hidden, split(hidden), grad_post)
            store_rows(g, j, first, count, back)
        for k in range(Q):
            grad[k, j] = get8(g, j, 4, k)
        return carry

    over_planes(0, stage4)

    one = acc1[0:T, :] + acc1[T : 2 * T, :]
    two = acc2[0:T, :] + acc2[T : 2 * T, :]
    in_part = one[:, 0:HID] + one[:, HID : 2 * HID]
    out_part = two[:, 0:HID] + two[:, HID : 2 * HID]
    bias = one[:, 2 * HID : 2 * HID + T] + one[:, 2 * HID + T : 2 * HID + 2 * T]
    sums[...] = jnp.zeros(sums.shape, jnp.float32)
    sums[0:T, 0:HID] = in_part * scale
    sums[0:Q, HID : 2 * HID] = out_part[0:Q, :] * scale
    sums[ONE : ONE + 1, HID : HID + T] = bias[ONE : ONE + 1, :] * scale


def shift(x, axis, step):
    count = lax.axis_size(axis)
    return lax.ppermute(x, axis, [(i, (i + step) % count) for i in range(count)])


def spread(x, axis):
    count = lax.axis_size(axis)
    return lax.all_to_all(jnp.broadcast_to(x[None], (count,) + x.shape), axis, 0, 0)


F32 = jnp.float32


def shape(*dims):
    return jax.ShapeDtypeStruct(dims, F32)


PARAMS = pltpu.CompilerParams(vmem_limit_bytes=48 * 1024 * 1024)


def on_device(start, adjoint, solid, w_in, b_in, w_out, b_out):
    rows = pltpu.VMEM
    z, to_up, to_down, w1x, w2x, w2tx, w1tx, b2b = pl.pallas_call(
        first_kernel,
        out_shape=(
            shape(2, UNITS, ROWS, W),
            shape(Y_ROWS, W),
            shape(Y_ROWS, W),
            shape(HID, 80),
            shape(T, 192),
            shape(HID, 80),
            shape(T, 192),
            shape(T, W),
        ),
        scratch_shapes=[
            rows((2, 8 * T, W), F32),
            rows((2, 8 * T, W), F32),
            rows((128, 128), F32),
        ],
        compiler_params=PARAMS,
        name="first",
    )(start, adjoint, solid, w_in, b_in.reshape(1, HID), w_out, b_out.reshape(1, Q))

    from_below = shift(to_up, "gy", 1)
    from_above = shift(to_down, "gy", -1)

    z, to_right, to_left = pl.pallas_call(
        second_kernel,
        out_shape=(shape(2, UNITS, ROWS, W), shape(FAR, ROWS, W), shape(FAR, ROWS, W)),
        compiler_params=PARAMS,
        name="second",
    )(z, from_below, from_above)

    z_left = shift(z, "gx", 1)
    z_right = shift(z, "gx", -1)
    f_left = shift(to_right, "gx", 2)
    f_right = shift(to_left, "gx", -2)

    cells = 16 * W * lax.axis_size("gx") * lax.axis_size("gy")
    vmem = pl.BlockSpec(memory_space=pltpu.VMEM)
    hbm = pl.BlockSpec(memory_space=pl.ANY)
    final, grad, sums = pl.pallas_call(
        functools.partial(third_kernel, 1.0 / math.sqrt(cells)),
        out_shape=(shape(Q, 2, 8, W), shape(Q, 2, 8, W), shape(T, W)),
        in_specs=[vmem] + [hbm] * 5 + [vmem] * 5,
        scratch_shapes=[
            rows((PLANES, UNITS, ROWS, W), F32),
            rows((2, 8 * T, W), F32),
            rows((8, ROWS * T, W), F32),
            rows((8, ROWS * T, W), F32),
            rows((6, ROWS * T, W), F32),
            rows((6, ROWS * T, W), F32),
            rows((6, ROWS * T, W), F32),
            rows((6, ROWS * T, W), F32),
            rows((2 * T, 2 * HID + 2 * T), F32),
            rows((2 * T, 2 * HID), F32),
            pltpu.SemaphoreType.DMA((11,)),
        ],
        compiler_params=PARAMS,
        name="third",
    )(start, z, z_left, z_right, f_left, f_right, w1x, w2x, w2tx, w1tx, b2b)

    parts = lax.axis_size("gx")
    used = (ONE + 1) * W
    share = -(-used // parts)
    flat = jnp.pad(sums[0 : ONE + 1].reshape(-1), (0, share * parts - used))
    mine = lax.all_to_all(flat.reshape(parts, share), "gx", 0, 0).sum(0)
    mine = spread(mine, "gy").sum(0)
    total = spread(mine, "gx").reshape(-1)[:used].reshape(ONE + 1, W)
    return (
        final,
        grad,
        total[0:Q, 0:HID].T,
        total[ONE, 0:HID],
        total[0:Q, HID : 2 * HID],
        total[ONE, HID : HID + Q],
    )


def solution(mesh):
    return jax.shard_map(
        on_device,
        mesh=mesh,
        in_specs=(
            P(None, "gx", "gy", None),
            P(None, "gx", "gy", None),
            P("gx", "gy", None),
            P(),
            P(),
            P(),
            P(),
        ),
        out_specs=(P(None, "gx", "gy", None), P(None, "gx", "gy", None), P(), P(), P(), P()),
        check_vma=False,
    )
```

time: 309 us -> 132 us (0.43)
  starting transfers between devices: 122 us -> 42.1 us
  blocking collectives: 107 us -> 53.3 us
  Pallas kernels: 0 us -> 22.6 us
  local copies, waits for them, and re-layouts: 24.9 us -> 5.74 us
  waiting for transfers between devices: 24 us -> 6.6 us
  other arithmetic: 16.3 us -> 0.76 us
  matrix products: 11 us -> 0 us
    psum x1 -> x0, blocking collectives: 107 us -> none  [on_device(): lax.psum((sum_w_in, sum_b_in, sum_w_out, sum_b_out), ('gx', 'gy'))]
    ppermute x24 -> x6, starting transfers between devices: 122 us -> 42.1 us  [shift(): lax.ppermute(x, axis, [(i, (i + step) % count) for i in range(count)])]
    all_to_all x0 -> x3, blocking collectives: none -> 53.3 us  [the longest x2 33.8 us: spread(): lax.all_to_all(jnp.broadcast_to(x[None], (count,) + x.shape), axis, 0, 0)]
    pallas_call x0 -> x3, Pallas kernels: none -> 22.6 us  [the longest x1 21.4 us: on_device(): pl.pallas_call(functools.partial(third_kernel, 1.0 / math.sqrt(cells)), o...]
    ppermute x24 -> x6, waiting for transfers between devices: 24 us -> 6.6 us  [shift(): lax.ppermute(x, axis, [(i, (i + step) % count) for i in range(count)])]
    unnamed x203 -> x13, local copies, waits for them, and re-layouts: 17.4 us -> 3.28 us
    dot_general x18 -> x0, matrix products: 11 us -> none  [the longest x3 2.78 us: on_device(): grad_hidden = jnp.dot(w_out.T, grad_change, precision=lax.Precision.HIGHEST)]
    unnamed x94 -> x0, other arithmetic: 9.36 us -> none
  transfers between devices with their start and end apart: 24 -> 6, of which waited for: 6 -> 4; matrix products, arithmetic and copies ran while one was open for 3% -> 0% of each run, Pallas kernels for 0% -> 0%
where the time goes in v1:
time: 132 us
  blocking collectives  53.3 us (40%)
  starting transfers between devices  42.1 us (32%)
  Pallas kernels  22.6 us (17%)
  waiting for transfers between devices  6.6 us (5%)
  local copies, waits for them, and re-layouts  5.74 us (4%)
    ppermute x6, starting transfers between devices, shift(): lax.ppermute(x, axis, [(i, (i + step) % count) for i in range(count)])  42.1 us
    all_to_all x2, blocking collectives, spread(): lax.all_to_all(jnp.broadcast_to(x[None], (count,) + x.shape), axis, 0, 0)  33.8 us
    pallas_call x1, Pallas kernels, on_device(): pl.pallas_call(functools.partial(third_kernel, 1.0 / math.sqrt(cells)), o...  21.4 us
    all_to_all x1, blocking collectives, on_device(): mine = lax.all_to_all(flat.reshape(parts, share), 'gx', 0, 0).sum(0)  19.4 us
    ppermute x6, waiting for transfers between devices, shift(): lax.ppermute(x, axis, [(i, (i + step) % count) for i in range(count)])  6.6 us
    unnamed x13, local copies, waits for them, and re-layouts  3.28 us
  transfers between devices with their start and end apart: 6, of which 4 were waited for; matrix products, arithmetic and copies ran while one was open for 0% of the time, Pallas kernels for 0%

profile of v1, /device:TPU:1, one launch (start us, length us, event | category | flops | bytes accessed | tf_op | source)
XLA Modules:
  0.0 131.8 jit_solution(13483025176513317602)
XLA Ops:
  0.6 0.0 copy-start.2
  0.6 0.0 copy-start.3
  0.7 0.8 copy.18.w_in
  1.5 0.0 copy-start.4
  1.5 0.0 copy-start.5
  1.5 0.0 copy-done.2
  1.5 0.0 copy-done.3
  1.5 0.6 copy-done.4
  2.1 0.0 copy-done.5
  2.1 0.0 copy-start
  2.1 0.9 copy-done
  3.0 0.0 copy-start.1
  3.0 0.9 copy-done.1
  4.0 1.1 first.1
  5.0 4.0 %collective-permute-start = (f32[200,128]{1,0:T(8,128)S(1)}, f32[200,128]{1,0:T(8,128)S(1)}, u32[]{:S(2)}, u32[]{:S(2)}) collective-permute-start(f32[200,128]{1,0:T(8,128)S(1)} %get-tuple-element.21), channel_id=1, source_target_pairs={{0,1},{1,2},{2,3},{3,4},{4,5},{5,6},{6,7},{7,8},{8,9},{9,10},{10,1... | collective-permute-start | bytes 307208 | tf_op jit(solution)/shard_map/ppermute | solution.py:425
  9.1 15.9 %collective-permute-start.1 = (f32[200,128]{1,0:T(8,128)S(1)}, f32[200,128]{1,0:T(8,128)S(1)}, u32[]{:S(2)}, u32[]{:S(2)}) collective-permute-start(f32[200,128]{1,0:T(8,128)S(1)} %get-tuple-element.22), channel_id=1, source_target_pairs={{0,23},{1,0},{2,1},{3,2},{4,3},{5,4},{6,5},{7,6},{8,7},{9,8},{10,9... | collective-permute-start | bytes 307208 | tf_op jit(solution)/shard_map/ppermute | solution.py:425
  25.0 0.4 collective-permute-done.from_below
  25.4 1.3 collective-permute-done.1.from_above
  26.6 0.1 second.1
  26.8 4.9 %collective-permute-start.2 = (f32[2,39,16,128]{3,2,1,0:T(8,128)S(1)}, f32[2,39,16,128]{3,2,1,0:T(8,128)S(1)}, u32[]{:S(2)}, u32[]{:S(2)}) collective-permute-start(f32[2,39,16,128]{3,2,1,0:T(8,128)S(1)} %get-tuple-element.23.z_own), channel_id=1, source_target_pairs={{0,24},{24,48},{48,72},{72,96},{96,120},{120,144},{144,168},{168,1... | collective-permute-start | bytes 1916936 | tf_op jit(solution)/shard_map/ppermute | solution.py:425
  31.7 8.0 %collective-permute-start.3 = (f32[2,39,16,128]{3,2,1,0:T(8,128)S(1)}, f32[2,39,16,128]{3,2,1,0:T(8,128)S(1)}, u32[]{:S(2)}, u32[]{:S(2)}) collective-permute-start(f32[2,39,16,128]{3,2,1,0:T(8,128)S(1)} %get-tuple-element.23.z_own), channel_id=1, source_target_pairs={{0,744},{24,0},{48,24},{72,48},{96,72},{120,96},{144,120},{168,144... | collective-permute-start | bytes 1916936 | tf_op jit(solution)/shard_map/ppermute | solution.py:425
  39.7 1.9 %collective-permute-start.4 = (f32[25,16,128]{2,1,0:T(8,128)S(1)}, f32[25,16,128]{2,1,0:T(8,128)S(1)}, u32[]{:S(2)}, u32[]{:S(2)}) collective-permute-start(f32[25,16,128]{2,1,0:T(8,128)S(1)} %get-tuple-element.24), channel_id=1, source_target_pairs={{0,48},{24,72},{48,96},{72,120},{96,144},{120,168},{144,192},{168,... | collective-permute-start | bytes 614408 | tf_op jit(solution)/shard_map/ppermute | solution.py:425
  41.7 7.3 %collective-permute-start.5 = (f32[25,16,128]{2,1,0:T(8,128)S(1)}, f32[25,16,128]{2,1,0:T(8,128)S(1)}, u32[]{:S(2)}, u32[]{:S(2)}) collective-permute-start(f32[25,16,128]{2,1,0:T(8,128)S(1)} %get-tuple-element.25), channel_id=1, source_target_pairs={{0,720},{24,744},{48,0},{72,24},{96,48},{120,72},{144,96},{168,120... | collective-permute-start | bytes 614408 | tf_op jit(solution)/shard_map/ppermute | solution.py:425
  48.9 4.1 %collective-permute-done.4.f_left = f32[25,16,128]{2,1,0:T(8,128)S(1)} collective-permute-done((f32[25,16,128]{2,1,0:T(8,128)S(1)}, f32[25,16,128]{2,1,0:T(8,128)S(1)}, u32[]{:S(2)}, u32[]{:S(2)}) %collective-permute-start.4) | collective-permute-done | bytes 204832 | tf_op jit(solution)/shard_map/ppermute | solution.py:425
  53.0 0.8 collective-permute-done.5.f_right
  53.9 0.0 collective-permute-done.2.z_left
  53.9 0.0 collective-permute-done.3.z_right
  53.9 21.4 %third.1 = (f32[19,2,8,128]{3,2,1,0:T(8,128)}, f32[19,2,8,128]{3,2,1,0:T(8,128)}, f32[24,128]{1,0:T(8,128)S(1)}) custom-call(f32[19,2,8,128]{3,2,1,0:T(8,128)S(1)} %copy-done, f32[2,39,16,128]{3,2,1,0:T(8,128)S(1)} %get-tuple-element.23.z_own, f32[2,39,16,128]{3,2,1,0:T(8,128)S(1)} %collective-permute-done.2.z_left, ...), custom_call_target="tpu_custom_call" | custom-call | tf_op jit(solution)/shard_map/third/pallas_call | solution.py:484
  75.3 0.1 all_to_all.14
  75.3 19.4 %all_to_all.21 = f32[32,1,80]{2,1,0:T(1,128)S(1)} all-to-all(f32[32,1,80]{2,1,0:T(1,128)S(1)} %bitcast.14), channel_id=1, replica_groups=mesh['gx'=32,'gy'=24] {'gx'}, dimensions={0} | all-to-all | bytes 20480 | tf_op jit(solution)/shard_map/all_to_all | solution.py:509
  94.8 0.1 reduce_sum.18
  94.8 21.8 %all_to_all.22 = f32[24,1,80]{2,1,0:T(1,128)S(1)} all-to-all(f32[24,1,80]{2,1,0:T(1,128)S(1)} %broadcast_in_dim.4), channel_id=1, replica_groups=mesh['gx'=32,'gy'=24] {'gy'}, dimensions={0} | all-to-all | bytes 15360 | tf_op jit(solution)/shard_map/all_to_all | solution.py:430
  116.7 12.0 %all_to_all.23 = f32[32,1,80]{2,1,0:T(1,128)S(1)} all-to-all(f32[32,1,80]{2,1,0:T(1,128)S(1)} %broadcast_in_dim.5), channel_id=1, replica_groups=mesh['gx'=32,'gy'=24] {'gx'}, dimensions={0} | all-to-all | bytes 20480 | tf_op jit(solution)/shard_map/all_to_all | solution.py:430
  128.7 0.5 broadcast.9
  129.2 0.7 reduce.5
  129.9 0.1 reshape_reshape.3
  130.0 0.7 fusion
  130.7 0.6 slice_bitcast_fusion.1
  131.3 0.5 slice_bitcast_fusion.2
  (3 shorter events, 0.0 us)
Async XLA Ops:
  0.6 0.8 copy-start.2
  0.6 0.8 copy-start.3
  1.5 0.7 copy-start.4
  1.5 0.7 copy-start.5
  2.1 0.9 copy-start
  3.0 0.9 copy-start.1
  5.0 20.4 %collective-permute-start = (f32[200,128]{1,0:T(8,128)S(1)}, f32[200,128]{1,0:T(8,128)S(1)}, u32[]{:S(2)}, u32[]{:S(2)}) collective-permute-start(f32[200,128]{1,0:T(8,128)S(1)} %get-tuple-element.21), channel_id=1, source_target_pairs={{0,1},{1,2},{2,3},{3,4},{4,5},{5,6},{6,7},{7,8},{8,9},{9,10},{10,1... | collective-permute-start | bytes 307208 | tf_op jit(solution)/shard_map/ppermute | solution.py:425
  9.1 17.6 %collective-permute-start.1 = (f32[200,128]{1,0:T(8,128)S(1)}, f32[200,128]{1,0:T(8,128)S(1)}, u32[]{:S(2)}, u32[]{:S(2)}) collective-permute-start(f32[200,128]{1,0:T(8,128)S(1)} %get-tuple-element.22), channel_id=1, source_target_pairs={{0,23},{1,0},{2,1},{3,2},{4,3},{5,4},{6,5},{7,6},{8,7},{9,8},{10,9... | collective-permute-start | bytes 307208 | tf_op jit(solution)/shard_map/ppermute | solution.py:425
  26.8 27.1 %collective-permute-start.2 = (f32[2,39,16,128]{3,2,1,0:T(8,128)S(1)}, f32[2,39,16,128]{3,2,1,0:T(8,128)S(1)}, u32[]{:S(2)}, u32[]{:S(2)}) collective-permute-start(f32[2,39,16,128]{3,2,1,0:T(8,128)S(1)} %get-tuple-element.23.z_own), channel_id=1, source_target_pairs={{0,24},{24,48},{48,72},{72,96},{96,120},{120,144},{144,168},{168,1... | collective-permute-start | bytes 1916936 | tf_op jit(solution)/shard_map/ppermute | solution.py:425
  31.7 22.2 %collective-permute-start.3 = (f32[2,39,16,128]{3,2,1,0:T(8,128)S(1)}, f32[2,39,16,128]{3,2,1,0:T(8,128)S(1)}, u32[]{:S(2)}, u32[]{:S(2)}) collective-permute-start(f32[2,39,16,128]{3,2,1,0:T(8,128)S(1)} %get-tuple-element.23.z_own), channel_id=1, source_target_pairs={{0,744},{24,0},{48,24},{72,48},{96,72},{120,96},{144,120},{168,144... | collective-permute-start | bytes 1916936 | tf_op jit(solution)/shard_map/ppermute | solution.py:425
  39.7 13.3 %collective-permute-start.4 = (f32[25,16,128]{2,1,0:T(8,128)S(1)}, f32[25,16,128]{2,1,0:T(8,128)S(1)}, u32[]{:S(2)}, u32[]{:S(2)}) collective-permute-start(f32[25,16,128]{2,1,0:T(8,128)S(1)} %get-tuple-element.24), channel_id=1, source_target_pairs={{0,48},{24,72},{48,96},{72,120},{96,144},{120,168},{144,192},{168,... | collective-permute-start | bytes 614408 | tf_op jit(solution)/shard_map/ppermute | solution.py:425
  41.7 12.2 %collective-permute-start.5 = (f32[25,16,128]{2,1,0:T(8,128)S(1)}, f32[25,16,128]{2,1,0:T(8,128)S(1)}, u32[]{:S(2)}, u32[]{:S(2)}) collective-permute-start(f32[25,16,128]{2,1,0:T(8,128)S(1)} %get-tuple-element.25), channel_id=1, source_target_pairs={{0,720},{24,744},{48,0},{72,24},{96,48},{120,72},{144,96},{168,120... | collective-permute-start | bytes 614408 | tf_op jit(solution)/shard_map/ppermute | solution.py:425

commit v2 on v1

--- a/solution.py
+++ b/solution.py
@@ -77,6 +77,18 @@
     return jnp.concatenate(parts, axis=1)
 
 
+def weights2(a):
+    high, low = split(a)
+    top = jnp.concatenate([high, high], axis=1)
+    bottom = jnp.concatenate([low, jnp.zeros_like(low)], axis=1)
+    return jnp.concatenate([top, bottom], axis=0)
+
+
+def mm2(weights, parts):
+    both = mm(weights, jnp.concatenate(parts, axis=0).astype(jnp.bfloat16))
+    return both[0:T] + both[T:]
+
+
 def mm(a, b):
     return lax.dot_general(a, b, (((1,), (0,)), ((), ())), preferred_element_type=jnp.float32)
 
@@ -126,14 +138,23 @@
 
 
 def first_kernel(
-    start, adjoint, solid, w_in, b_in, w_out, b_out,
-    z, to_up, to_down, w1x, w2x, w2tx, w1tx, b2b,
-    s0, p1, sq,
+    start_hbm, adjoint_hbm, solid_hbm, w_in_t_hbm, b_in_hbm, w_out_hbm, b_out_hbm,
+    z, to_even, to_odd, s0, w1x, w2x, w2tx, w1tx, b2b,
+    p1, sq, start, adjoint, solid, w_in_t, b_in, w_out, b_out, sems,
 ):
+    pairs = (
+        (w_in_t_hbm, w_in_t), (b_in_hbm, b_in), (w_out_hbm, w_out), (b_out_hbm, b_out),
+        (start_hbm, start), (solid_hbm, solid), (adjoint_hbm, adjoint),
+    )
+    copies = [pltpu.make_async_copy(a, b, sems.at[i]) for i, (a, b) in enumerate(pairs)]
+    for copy in copies:
+        copy.start()
     sq[...] = jnp.zeros((128, 128), jnp.float32)
-    sq[0:HID, 0:Q] = w_in[...]
-    a1t = sq[...].T
-    sq[...] = a1t
+    for plane in range(2):
+        pad_rows(s0, plane, 0, 8)
+    for copy in copies[:4]:
+        copy.wait()
+    sq[0:Q, 0:HID] = w_in_t[...]
     sq[ONE : ONE + 1, 0:HID] = b_in[...]
     a1t = sq[0:T, 0:HID]
     a1 = sq[...].T[0:HID, 0:T]
@@ -145,16 +166,17 @@
     sq[0:1, 0:Q] = b_out[...]
     b2 = jnp.broadcast_to(sq[...].T[0:T, 0:1], (T, W))
     w1 = weights3(a1)
-    w2 = weights3(a2)
+    w2 = weights2(a2)
     w1x[...] = w1
     w2x[...] = w2
     w2tx[...] = weights3(a2t)
-    w1tx[...] = weights3(a1t)
+    w1tx[...] = weights2(a1t)
     b2b[...] = b2
     w1 = w1.astype(jnp.bfloat16)
     w2 = w2.astype(jnp.bfloat16)
+    for copy in copies[4:]:
+        copy.wait()
     for plane in range(2):
-        pad_rows(s0, plane, 0, 8)
         for k in range(Q):
             put8(s0, plane, 0, k, start[k, plane])
         sol = solid[plane].astype(jnp.float32)
@@ -164,21 +186,20 @@
             z[plane, Q + place[k], 4:12, :] = jnp.where(
                 mask, adjoint[opposite[k], plane], adjoint[k, plane]
             )
+    state = jnp.concatenate([load_rows(s0, plane, 0, 8) for plane in range(2)], axis=1)
+    hidden = jnp.tanh(mm(w1, stack3(*split(state))))
+    change = mm2(w2, split(hidden))
+    for i in range(16):
+        plane, y = divmod(i, 8)
+        fluid = 1.0 - solid[plane, y : y + 1, :].astype(jnp.float32)
+        p1[plane, y * T : (y + 1) * T, :] = state[:, i * W : (i + 1) * W] + fluid * (
+            change[:, i * W : (i + 1) * W] + b2
+        )
     for plane in range(2):
-        for first, count in chunks(8, 4):
-            state = load_rows(s0, plane, first, count)
-            hidden = jnp.tanh(mm(w1, stack3(*split(state))))
-            change = mm(w2, stack3(*split(hidden)))
-            for i in range(count):
-                y = first + i
-                fluid = 1.0 - solid[plane, y : y + 1, :].astype(jnp.float32)
-                p1[plane, y * T : (y + 1) * T, :] = state[:, i * W : (i + 1) * W] + fluid * (
-                    change[:, i * W : (i + 1) * W] + b2
-                )
-    for plane in range(2):
         for k in range(Q):
             z[plane, place[k], 4:12, :] = get8(p1, plane, 0, k)
-    for ref, way in ((to_up, 1), (to_down, -1)):
+
+    def pack(ref, way):
         at = 0
         for plane, unit, rows in y_pieces(way):
             begin = 12 - rows if way == 1 else 4
@@ -186,19 +207,58 @@
             at += rows
         ref[at:, :] = jnp.zeros((Y_ROWS - at, W), jnp.float32)
 
-
-def second_kernel(z_in, from_below, from_above, z, to_right, to_left):
+    odd = lax.rem(lax.axis_index("gy"), 2)
+
+    @pl.when(odd == 0)
+    def _():
+        pack(to_even, 1)
+        pack(to_odd, -1)
+
+    @pl.when(odd == 1)
+    def _():
+        pack(to_even, -1)
+        pack(to_odd, 1)
+
+
+def second_kernel(z_in, from_even, from_odd, z, to_near, to_far):
     z[...] = z_in[...]
-    for ref, way in ((from_below, 1), (from_above, -1)):
+
+    def unpack(ref, way):
         at = 0
         for plane, unit, rows in y_pieces(way):
             begin = 4 - rows if way == 1 else 12
             z[plane, unit, begin : begin + rows, :] = ref[at : at + rows, :]
             at += rows
-    for at, (plane, unit) in enumerate(far_units(1)):
-        to_right[at] = z[plane, unit]
-    for at, (plane, unit) in enumerate(far_units(-1)):
-        to_left[at] = z[plane, unit]
+
+    odd = lax.rem(lax.axis_index("gy"), 2)
+
+    @pl.when(odd == 0)
+    def _():
+        unpack(from_even, -1)
+        unpack(from_odd, 1)
+
+    @pl.when(odd == 1)
+    def _():
+        unpack(from_even, 1)
+        unpack(from_odd, -1)
+
+    def pack(ref, way):
+        at = 0
+        for count, plane, first in far_runs(way):
+            ref[at : at + count] = z[plane, first : first + count]
+            at += count
+
+    low = lax.rem(lax.axis_index("gx"), 4) < 2
+
+    @pl.when(low)
+    def _():
+        pack(to_near, 1)
+        pack(to_far, -1)
+
+    @pl.when(jnp.logical_not(low))
+    def _():
+        pack(to_near, -1)
+        pack(to_far, 1)
 
 
 def far_runs(way):
@@ -207,10 +267,6 @@
     return ((5, 1, 14), (14, 0, 5), (5, 0, Q), (1, 0, SOLID))
 
 
-def far_units(way):
-    return [(plane, first + i) for count, plane, first in far_runs(way) for i in range(count)]
-
-
 FAR = 25
 
 
@@ -220,15 +276,25 @@
 
 def third_kernel(
     scale,
-    start, z_own, z_left, z_right, f_left, f_right, w1x, w2x, w2tx, w1tx, b2b,
+    s0, z_own, z_even, z_odd, f_near, f_far, w1x, w2x, w2tx, w1tx, b2b,
     final, grad, sums,
-    zs, s0, s1, p2, s2, p3, gp, g, acc1, acc2, sems,
+    zs, s1, p2, s2, p3, gp, g, acc1, acc2, sems,
 ):
-    copies = [(z_left, zs.at[2:4]), (z_own, zs.at[4:6]), (z_right, zs.at[6:8])]
-    for ref, way, base in ((f_left, 1, 0), (f_right, -1, 8)):
+    index = lax.axis_index("gx")
+    odd = lax.rem(index, 2)
+    high = lax.rem(index, 4) // 2
+    copies = [
+        (z_even, zs.at[pl.ds(6 - 4 * odd, 2)]),
+        (z_own, zs.at[4:6]),
+        (z_odd, zs.at[pl.ds(2 + 4 * odd, 2)]),
+    ]
+    for ref, left in ((f_near, high), (f_far, 1 - high)):
         at = 0
-        for count, plane, first in far_runs(way):
-            copies.append((ref.at[at : at + count], zs.at[base + plane, first : first + count]))
+        for (count, plane, first), (_, plane_r, first_r) in zip(far_runs(1), far_runs(-1)):
+            plane_r += 8
+            x = plane_r + left * (plane - plane_r)
+            unit = first_r + left * (first - first_r)
+            copies.append((ref.at[at : at + count], zs.at[x, pl.ds(unit, count)]))
             at += count
     copies = [pltpu.make_async_copy(a, b, sems.at[i]) for i, (a, b) in enumerate(copies)]
     for copy in copies:
@@ -241,16 +307,6 @@
     b2 = b2b[...]
     acc1[...] = jnp.zeros(acc1.shape, jnp.float32)
     acc2[...] = jnp.zeros(acc2.shape, jnp.float32)
-    tile = pad_tile()
-
-    def init_pads(ref, planes, first, count):
-        for plane in range(planes):
-            pad_rows(ref, plane, first, count)
-
-    init_pads(s0, 2, 0, 8)
-    for plane in range(2):
-        for k in range(Q):
-            put8(s0, plane, 0, k, start[k, plane])
     for ref, planes in ((s1, 8), (s2, 6)):
         for plane in range(planes):
             pad_rows(ref, plane, 0, ROWS)
@@ -268,7 +324,7 @@
         return jnp.tanh(mm(w1, stack3(*state_parts)))
 
     def collide(p_ref, p_plane, zx, first, count, state, hidden_parts):
-        change = mm(w2, stack3(*hidden_parts))
+        change = mm2(w2, hidden_parts)
         for i in range(count):
             y = first + i
             p_ref[p_plane, y * T : (y + 1) * T, :] = state[:, i * W : (i + 1) * W] + fluid_rows(
@@ -287,7 +343,7 @@
         grad_hidden = mm(w2t, stack3(*change_parts))
         grad_pre = grad_hidden * (1.0 - hidden * hidden)
         pre_parts = split(grad_pre)
-        back = grad_post + mm(w1t, stack3(*pre_parts))
+        back = grad_post + mm2(w1t, pre_parts)
         low = max(first, 4)
         high = min(first + count, 12)
 
@@ -308,8 +364,9 @@
                 2 * halo,
                 lambda i, c: body(False, jnp.where(i < halo, i, i + 2), c),
                 0,
+                unroll=2 * halo,
             )
-        lax.fori_loop(0, 2, lambda i, c: body(True, i + halo, c), 0)
+        lax.fori_loop(0, 2, lambda i, c: body(True, i + halo, c), 0, unroll=2)
 
     def reflect(values, mask):
         return [jnp.where(mask, values[opposite[k]], values[k]) for k in range(Q)]
@@ -324,14 +381,14 @@
             moved = reflect(moved, zs[zx, SOLID, y : y + 8, :] > 0.5)
             for k in range(Q):
                 put8(s1, j, y, k, moved[k])
-        for first, count in chunks(14, 4):
+        for first, count in chunks(14, 14):
             first += 1
             state = load_rows(s1, j, first, count)
             hidden = forward_hidden(split(state))
             collide(p2, j, zx, first, count, state, split(hidden))
         return carry
 
-    lax.fori_loop(0, 8, stage1, 0)
+    lax.fori_loop(0, 8, stage1, 0, unroll=8)
 
     def stage2(own, j, carry):
         zx = j + 2
@@ -347,7 +404,7 @@
                 cx, cy, cz = velocities[k]
                 value = zs[zx + cx, Q + place[k], y + cy : y + cy + 8, :]
                 put8(gp, j, y, k, z_shift(value, -cz))
-        for first, count in chunks(12, 4):
+        for first, count in chunks(12, 12):
             first += 2
             state = load_rows(s2, j, first, count)
             state_parts = split(state)
@@ -384,7 +441,7 @@
         zx = j + 3
         for y in (3, 5):
             run_back(g, j + 1, zx, y, j)
-        for first, count in ((3, 5), (8, 5)):
+        for first, count in ((3, 10),):
             state_parts = split(load_rows(s1, j + 2, first, count))
             hidden = forward_hidden(state_parts)
             grad_post = load_rows(gp, j, first, count)
@@ -397,7 +454,7 @@
     def stage4(own, j, carry):
         zx = j + 4
         run_back(p2, j + 1, zx, 4, j)
-        for first, count in ((4, 4), (8, 4)):
+        for first, count in ((4, 8),):
             state_parts = split(load_rows(s0, j, first - 4, count))
             hidden = forward_hidden(state_parts)
             grad_post = load_rows(gp, j, first, count)
@@ -420,14 +477,48 @@
     sums[ONE : ONE + 1, HID : HID + T] = bias[ONE : ONE + 1, :] * scale
 
 
-def shift(x, axis, step):
+def last_kernel(parts, grad_w_in_t, grad_b_in, grad_w_out, grad_b_out):
+    total = parts[0]
+    for i in range(1, parts.shape[0]):
+        total = total + parts[i]
+    grad_w_in_t[...] = total[0:Q, 0:HID]
+    grad_b_in[...] = total[ONE : ONE + 1, 0:HID]
+    grad_w_out[...] = total[0:Q, HID : 2 * HID]
+    grad_b_out[...] = total[ONE : ONE + 1, HID : HID + Q]
+
+
+def swap_even(x, axis, step=1):
     count = lax.axis_size(axis)
-    return lax.ppermute(x, axis, [(i, (i + step) % count) for i in range(count)])
-
-
-def spread(x, axis):
+    return lax.ppermute(x, axis, [(i, i ^ step) for i in range(count)])
+
+
+def swap_odd(x, axis, step=1):
     count = lax.axis_size(axis)
-    return lax.all_to_all(jnp.broadcast_to(x[None], (count,) + x.shape), axis, 0, 0)
+    return lax.ppermute(
+        x, axis, [(i, (i + step if i & step else i - step) % count) for i in range(count)]
+    )
+
+
+def spread(x, groups):
+    count = len(groups[0])
+    return lax.all_to_all(
+        jnp.broadcast_to(x[None], (count,) + x.shape), ("gx", "gy"), 0, 0, axis_index_groups=groups
+    )
+
+
+def sum_groups():
+    gx, gy = lax.axis_size("gx"), lax.axis_size("gy")
+    nx, ny = math.gcd(gx, 8), math.gcd(gy, 8)
+    zs = [(a, b) for b in range(gy // ny) for a in range(gx // nx)]
+
+    def at(z, x, y):
+        return (z[0] * nx + x) * gy + z[1] * ny + y
+
+    return (
+        [[at(z, x, y) for x in range(nx)] for z in zs for y in range(ny)],
+        [[at(z, x, y) for z in zs] for x in range(nx) for y in range(ny)],
+        [[at(z, x, y) for y in range(ny)] for z in zs for x in range(nx)],
+    )
 
 
 F32 = jnp.float32
@@ -437,46 +528,56 @@
     return jax.ShapeDtypeStruct(dims, F32)
 
 
+FIRST_VMEM = 63 * 1024 * 1024
 PARAMS = pltpu.CompilerParams(vmem_limit_bytes=48 * 1024 * 1024)
 
 
 def on_device(start, adjoint, solid, w_in, b_in, w_out, b_out):
     rows = pltpu.VMEM
-    z, to_up, to_down, w1x, w2x, w2tx, w1tx, b2b = pl.pallas_call(
+    z, to_even, to_odd, s0, w1x, w2x, w2tx, w1tx, b2b = pl.pallas_call(
         first_kernel,
         out_shape=(
             shape(2, UNITS, ROWS, W),
             shape(Y_ROWS, W),
             shape(Y_ROWS, W),
+            shape(2, 8 * T, W),
             shape(HID, 80),
-            shape(T, 192),
+            shape(2 * T, 2 * HID),
             shape(HID, 80),
-            shape(T, 192),
+            shape(2 * T, 2 * HID),
             shape(T, W),
         ),
+        in_specs=[pl.BlockSpec(memory_space=pltpu.HBM)] * 7,
         scratch_shapes=[
             rows((2, 8 * T, W), F32),
-            rows((2, 8 * T, W), F32),
             rows((128, 128), F32),
+            rows((Q, 2, 8, W), F32),
+            rows((Q, 2, 8, W), F32),
+            rows((2, 8, W), jnp.int32),
+            rows((Q, HID), F32),
+            rows((1, HID), F32),
+            rows((Q, HID), F32),
+            rows((1, Q), F32),
+            pltpu.SemaphoreType.DMA((7,)),
         ],
-        compiler_params=PARAMS,
+        compiler_params=pltpu.CompilerParams(vmem_limit_bytes=FIRST_VMEM),
         name="first",
-    )(start, adjoint, solid, w_in, b_in.reshape(1, HID), w_out, b_out.reshape(1, Q))
-
-    from_below = shift(to_up, "gy", 1)
-    from_above = shift(to_down, "gy", -1)
-
-    z, to_right, to_left = pl.pallas_call(
+    )(start, adjoint, solid, w_in.T, b_in.reshape(1, HID), w_out, b_out.reshape(1, Q))
+
+    from_even = swap_even(to_even, "gy")
+    from_odd = swap_odd(to_odd, "gy")
+
+    z, to_near, to_far = pl.pallas_call(
         second_kernel,
         out_shape=(shape(2, UNITS, ROWS, W), shape(FAR, ROWS, W), shape(FAR, ROWS, W)),
         compiler_params=PARAMS,
         name="second",
-    )(z, from_below, from_above)
-
-    z_left = shift(z, "gx", 1)
-    z_right = shift(z, "gx", -1)
-    f_left = shift(to_right, "gx", 2)
-    f_right = shift(to_left, "gx", -2)
+    )(z, from_even, from_odd)
+
+    z_odd = swap_odd(z, "gx")
+    f_far = swap_odd(to_far, "gx", 2)
+    f_near = swap_even(to_near, "gx", 2)
+    z_even = swap_even(z, "gx")
 
     cells = 16 * W * lax.axis_size("gx") * lax.axis_size("gy")
     vmem = pl.BlockSpec(memory_space=pltpu.VMEM)
@@ -487,7 +588,6 @@
         in_specs=[vmem] + [hbm] * 5 + [vmem] * 5,
         scratch_shapes=[
             rows((PLANES, UNITS, ROWS, W), F32),
-            rows((2, 8 * T, W), F32),
             rows((8, ROWS * T, W), F32),
             rows((8, ROWS * T, W), F32),
             rows((6, ROWS * T, W), F32),
@@ -500,23 +600,18 @@
         ],
         compiler_params=PARAMS,
         name="third",
-    )(start, z, z_left, z_right, f_left, f_right, w1x, w2x, w2tx, w1tx, b2b)
-
-    parts = lax.axis_size("gx")
-    used = (ONE + 1) * W
-    share = -(-used // parts)
-    flat = jnp.pad(sums[0 : ONE + 1].reshape(-1), (0, share * parts - used))
-    mine = lax.all_to_all(flat.reshape(parts, share), "gx", 0, 0).sum(0)
-    mine = spread(mine, "gy").sum(0)
-    total = spread(mine, "gx").reshape(-1)[:used].reshape(ONE + 1, W)
-    return (
-        final,
-        grad,
-        total[0:Q, 0:HID].T,
-        total[ONE, 0:HID],
-        total[0:Q, HID : 2 * HID],
-        total[ONE, HID : HID + Q],
-    )
+    )(s0, z, z_even, z_odd, f_near, f_far, w1x, w2x, w2tx, w1tx, b2b)
+
+    along_x, along_z, along_y = sum_groups()
+    sums = spread(sums, along_x).sum(0)
+    sums = spread(sums, along_z).sum(0)
+    grad_w_in_t, grad_b_in, grad_w_out, grad_b_out = pl.pallas_call(
+        last_kernel,
+        out_shape=(shape(Q, HID), shape(1, HID), shape(Q, HID), shape(1, Q)),
+        compiler_params=PARAMS,
+        name="last",
+    )(spread(sums, along_y))
+    return final, grad, grad_w_in_t.T, grad_b_in[0], grad_w_out, grad_b_out[0]
 
 
 def solution(mesh):

time: 132 us -> 106 us (0.80)
  the two profiles are of different devices: /device:TPU:1 before, /device:TPU:2 now
where the time goes in v2:
time: 106 us
  blocking collectives  40.2 us (38%)
  starting transfers between devices  34.5 us (33%)
  waiting for transfers between devices  16 us (15%)
  Pallas kernels  12.9 us (12%)
  local copies, waits for them, and re-layouts  1.13 us (1%)
    all_to_all x3, blocking collectives, spread(): lax.all_to_all(jnp.broadcast_to(x[None], (count,) + x.shape), ('gx', 'gy'...  40.2 us
    ppermute x3, starting transfers between devices, swap_odd(): lax.ppermute(x, axis, [(i, (i + step if i & step else i - step) % count)...  21.1 us
    ppermute x3, starting transfers between devices, swap_even(): return lax.ppermute(x, axis, [(i, i ^ step) for i in range(count)])  13.4 us
    ppermute x3, waiting for transfers between devices, swap_odd(): lax.ppermute(x, axis, [(i, (i + step if i & step else i - step) % count)...  12.2 us
    pallas_call x1, Pallas kernels, on_device(): pl.pallas_call(functools.partial(third_kernel, 1.0 / math.sqrt(cells)), o...  9.51 us
    ppermute x3, waiting for transfers between devices, swap_even(): return lax.ppermute(x, axis, [(i, i ^ step) for i in range(count)])  3.8 us
    pallas_call x1, Pallas kernels, on_device(): pl.pallas_call(first_kernel, out_shape=(shape(2, UNITS, ROWS, W), shape(Y...  2.61 us
  transfers between devices with their start and end apart: 6, of which 3 were waited for; matrix products, arithmetic and copies ran while one was open for 0% of the time, Pallas kernels for 0%

profile of v2, /device:TPU:2, one launch (start us, length us, event | category | flops | bytes accessed | tf_op | source)
XLA Modules:
  0.0 105.6 jit_solution(5990423130200510355)
XLA Ops:
  0.6 2.6 %first.1 = (f32[2,39,16,128]{3,2,1,0:T(8,128)}, f32[200,128]{1,0:T(8,128)}, f32[200,128]{1,0:T(8,128)}, f32[2,192,128]{2,1,0:T(8,128)}, f32[64,80]{1,0:T(8,128)}...) custom-call(f32[19,2,8,128]{3,2,1,0:T(8,128)} %start_hbm.1, ...), custom_call_target="tpu_custom_call" | custom-call | tf_op jit(solution)/shard_map/first/pallas_call | solution.py:537
  3.2 3.5 %collective-permute-start = (f32[200,128]{1,0:T(8,128)}, f32[200,128]{1,0:T(8,128)S(1)}, u32[]{:S(2)}, u32[]{:S(2)}) collective-permute-start(f32[200,128]{1,0:T(8,128)} %get-tuple-element.27), channel_id=1, source_target_pairs={{0,1},{1,0},{2,3},{3,2},{4,5},{5,4},{6,7},{7,6},{8,9},{9,8},{10,11... | collective-permute-start | bytes 307208 | tf_op jit(solution)/shard_map/ppermute | solution.py:492
  6.7 17.2 %collective-permute-start.1 = (f32[200,128]{1,0:T(8,128)}, f32[200,128]{1,0:T(8,128)S(1)}, u32[]{:S(2)}, u32[]{:S(2)}) collective-permute-start(f32[200,128]{1,0:T(8,128)} %get-tuple-element.28), channel_id=1, source_target_pairs={{0,23},{1,2},{2,1},{3,4},{4,3},{5,6},{6,5},{7,8},{8,7},{9,10},{10,... | collective-permute-start | bytes 307208 | tf_op jit(solution)/shard_map/ppermute | solution.py:497
  24.0 0.0 collective-permute-done.from_even
  24.0 8.9 %collective-permute-done.1.from_odd = f32[200,128]{1,0:T(8,128)S(1)} collective-permute-done((f32[200,128]{1,0:T(8,128)}, f32[200,128]{1,0:T(8,128)S(1)}, u32[]{:S(2)}, u32[]{:S(2)}) %collective-permute-start.1) | collective-permute-done | bytes 102432 | tf_op jit(solution)/shard_map/ppermute | solution.py:497
  32.8 0.0 copy-start
  32.8 1.1 %copy-done = f32[2,39,16,128]{3,2,1,0:T(8,128)S(1)} copy-done((f32[2,39,16,128]{3,2,1,0:T(8,128)S(1)}, f32[2,39,16,128]{3,2,1,0:T(8,128)}, u32[]{:S(2)}) %copy-start) | copy-done | bytes 639000
  33.9 0.0 copy-start.1
  33.9 0.0 copy-start.2
  33.9 0.0 copy-start.3
  33.9 0.0 copy-start.4
  33.9 0.0 copy-start.5
  33.9 0.1 second.1
  34.1 0.0 copy-start.6
  34.1 1.9 %collective-permute-start.3 = (f32[2,39,16,128]{3,2,1,0:T(8,128)S(1)}, f32[2,39,16,128]{3,2,1,0:T(8,128)S(1)}, u32[]{:S(2)}, u32[]{:S(2)}) collective-permute-start(f32[2,39,16,128]{3,2,1,0:T(8,128)S(1)} %get-tuple-element.29.z_own), channel_id=1, source_target_pairs={{0,744},{24,48},{48,24},{72,96},{96,72},{120,144},{144,120},{168,1... | collective-permute-start | bytes 1916936 | tf_op jit(solution)/shard_map/ppermute | solution.py:497
  36.0 3.5 %collective-permute-start.2 = (f32[2,39,16,128]{3,2,1,0:T(8,128)S(1)}, f32[2,39,16,128]{3,2,1,0:T(8,128)S(1)}, u32[]{:S(2)}, u32[]{:S(2)}) collective-permute-start(f32[2,39,16,128]{3,2,1,0:T(8,128)S(1)} %get-tuple-element.29.z_own), channel_id=1, source_target_pairs={{0,24},{24,0},{48,72},{72,48},{96,120},{120,96},{144,168},{168,144... | collective-permute-start | bytes 1916936 | tf_op jit(solution)/shard_map/ppermute | solution.py:492
  39.5 6.4 %collective-permute-start.4 = (f32[25,16,128]{2,1,0:T(8,128)S(1)}, f32[25,16,128]{2,1,0:T(8,128)S(1)}, u32[]{:S(2)}, u32[]{:S(2)}) collective-permute-start(f32[25,16,128]{2,1,0:T(8,128)S(1)} %get-tuple-element.30), channel_id=1, source_target_pairs={{0,48},{24,72},{48,0},{72,24},{96,144},{120,168},{144,96},{168,120... | collective-permute-start | bytes 614408 | tf_op jit(solution)/shard_map/ppermute | solution.py:492
  46.0 1.9 %collective-permute-start.5 = (f32[25,16,128]{2,1,0:T(8,128)S(1)}, f32[25,16,128]{2,1,0:T(8,128)S(1)}, u32[]{:S(2)}, u32[]{:S(2)}) collective-permute-start(f32[25,16,128]{2,1,0:T(8,128)S(1)} %get-tuple-element.31), channel_id=1, source_target_pairs={{0,720},{24,744},{48,96},{72,120},{96,48},{120,72},{144,192},{168,... | collective-permute-start | bytes 614408 | tf_op jit(solution)/shard_map/ppermute | solution.py:497
  47.9 3.8 %collective-permute-done.4.f_near = f32[25,16,128]{2,1,0:T(8,128)S(1)} collective-permute-done((f32[25,16,128]{2,1,0:T(8,128)S(1)}, f32[25,16,128]{2,1,0:T(8,128)S(1)}, u32[]{:S(2)}, u32[]{:S(2)}) %collective-permute-start.4) | collective-permute-done | bytes 204832 | tf_op jit(solution)/shard_map/ppermute | solution.py:492
  51.7 3.4 %collective-permute-done.5.f_far = f32[25,16,128]{2,1,0:T(8,128)S(1)} collective-permute-done((f32[25,16,128]{2,1,0:T(8,128)S(1)}, f32[25,16,128]{2,1,0:T(8,128)S(1)}, u32[]{:S(2)}, u32[]{:S(2)}) %collective-permute-start.5) | collective-permute-done | bytes 204832 | tf_op jit(solution)/shard_map/ppermute | solution.py:497
  55.1 0.0 collective-permute-done.3.z_odd
  55.1 0.0 collective-permute-done.2.z_even
  55.1 0.0 copy-done.1
  55.1 0.0 copy-done.2
  55.1 0.0 copy-done.3
  55.1 0.0 copy-done.4
  55.1 0.0 copy-done.5
  55.1 0.0 copy-done.6
  55.2 9.5 %third.1 = (f32[19,2,8,128]{3,2,1,0:T(8,128)}, f32[19,2,8,128]{3,2,1,0:T(8,128)}, f32[24,128]{1,0:T(8,128)S(1)}) custom-call(f32[2,192,128]{2,1,0:T(8,128)S(1)} %copy-done.1, f32[2,39,16,128]{3,2,1,0:T(8,128)S(1)} %get-tuple-element.29.z_own, f32[2,39,16,128]{3,2,1,0:T(8,128)S(1)} %collective-permute-done.2.z_even, ...), custom_call_target="tpu_custom_call" | custom-call | tf_op jit(solution)/shard_map/third/pallas_call | solution.py:585
  64.7 10.9 %all_to_all.15 = f32[8,24,128]{2,1,0:T(8,128)S(1)} all-to-all(f32[8,24,128]{2,1,0:T(8,128)S(1)} %broadcast_in_dim.6), channel_id=1, replica_groups={{0,24,48,72,96,120,144,168},{1,25,49,73,97,121,145,169},{2,26,50,74,98,..., dimensions={0} | all-to-all | bytes 196608 | tf_op jit(solution)/shard_map/all_to_all | solution.py:504
  75.6 17.7 %all_to_all.16 = f32[12,24,128]{2,1,0:T(8,128)S(1)} all-to-all(f32[12,24,128]{2,1,0:T(8,128)S(1)} %broadcast_in_dim.7), channel_id=1, replica_groups={{0,192,384,576,8,200,392,584,16,208,400,592},{1,193,385,577,9,201,393,5..., dimensions={0} | all-to-all | bytes 294912 | tf_op jit(solution)/shard_map/all_to_all | solution.py:504
  93.4 11.5 %all_to_all.17.parts = f32[8,24,128]{2,1,0:T(8,128)S(1)} all-to-all(f32[8,24,128]{2,1,0:T(8,128)S(1)} %broadcast_in_dim.8), channel_id=1, replica_groups={{0,1,2,3,4,5,6,7},{24,25,26,27,28,29,30,31},{48,49,50,51,52,53,54,55},{..., dimensions={0} | all-to-all | bytes 196608 | tf_op jit(solution)/shard_map/all_to_all | solution.py:504
  104.9 0.7 last.1
  (5 shorter events, 0.1 us)
Async XLA Ops:
  3.2 20.7 %collective-permute-start = (f32[200,128]{1,0:T(8,128)}, f32[200,128]{1,0:T(8,128)S(1)}, u32[]{:S(2)}, u32[]{:S(2)}) collective-permute-start(f32[200,128]{1,0:T(8,128)} %get-tuple-element.27), channel_id=1, source_target_pairs={{0,1},{1,0},{2,3},{3,2},{4,5},{5,4},{6,7},{7,6},{8,9},{9,8},{10,11... | collective-permute-start | bytes 307208 | tf_op jit(solution)/shard_map/ppermute | solution.py:492
  6.7 26.1 %collective-permute-start.1 = (f32[200,128]{1,0:T(8,128)}, f32[200,128]{1,0:T(8,128)S(1)}, u32[]{:S(2)}, u32[]{:S(2)}) collective-permute-start(f32[200,128]{1,0:T(8,128)} %get-tuple-element.28), channel_id=1, source_target_pairs={{0,23},{1,2},{2,1},{3,4},{4,3},{5,6},{6,5},{7,8},{8,7},{9,10},{10,... | collective-permute-start | bytes 307208 | tf_op jit(solution)/shard_map/ppermute | solution.py:497
  32.8 1.1 %copy-start = (f32[2,39,16,128]{3,2,1,0:T(8,128)S(1)}, f32[2,39,16,128]{3,2,1,0:T(8,128)}, u32[]{:S(2)}) copy-start(f32[2,39,16,128]{3,2,1,0:T(8,128)} %get-tuple-element.26.z_in) | copy-start | bytes 1916932
  33.9 21.2 %copy-start.1 = (f32[2,192,128]{2,1,0:T(8,128)S(1)}, f32[2,192,128]{2,1,0:T(8,128)}, u32[]{:S(2)}) copy-start(f32[2,192,128]{2,1,0:T(8,128)} %get-tuple-element.25.s0) | copy-start | bytes 589828
  33.9 21.2 %copy-start.2 = (f32[64,80]{1,0:T(8,128)S(1)}, f32[64,80]{1,0:T(8,128)}, u32[]{:S(2)}) copy-start(f32[64,80]{1,0:T(8,128)} %get-tuple-element.32.w1x) | copy-start | bytes 61444
  33.9 21.2 %copy-start.3 = (f32[64,80]{1,0:T(8,128)S(1)}, f32[64,80]{1,0:T(8,128)}, u32[]{:S(2)}) copy-start(f32[64,80]{1,0:T(8,128)} %get-tuple-element.34.w2tx) | copy-start | bytes 61444
  33.9 21.2 %copy-start.4 = (f32[48,128]{1,0:T(8,128)S(1)}, f32[48,128]{1,0:T(8,128)}, u32[]{:S(2)}) copy-start(f32[48,128]{1,0:T(8,128)} %get-tuple-element.33.w2x) | copy-start | bytes 73732
  33.9 21.2 %copy-start.5 = (f32[48,128]{1,0:T(8,128)S(1)}, f32[48,128]{1,0:T(8,128)}, u32[]{:S(2)}) copy-start(f32[48,128]{1,0:T(8,128)} %get-tuple-element.35.w1tx) | copy-start | bytes 73732
  34.1 21.1 %copy-start.6 = (f32[24,128]{1,0:T(8,128)S(1)}, f32[24,128]{1,0:T(8,128)}, u32[]{:S(2)}) copy-start(f32[24,128]{1,0:T(8,128)} %get-tuple-element.36.b2b) | copy-start | bytes 36868
  34.1 21.0 %collective-permute-start.3 = (f32[2,39,16,128]{3,2,1,0:T(8,128)S(1)}, f32[2,39,16,128]{3,2,1,0:T(8,128)S(1)}, u32[]{:S(2)}, u32[]{:S(2)}) collective-permute-start(f32[2,39,16,128]{3,2,1,0:T(8,128)S(1)} %get-tuple-element.29.z_own), channel_id=1, source_target_pairs={{0,744},{24,48},{48,24},{72,96},{96,72},{120,144},{144,120},{168,1... | collective-permute-start | bytes 1916936 | tf_op jit(solution)/shard_map/ppermute | solution.py:497
  36.0 19.1 %collective-permute-start.2 = (f32[2,39,16,128]{3,2,1,0:T(8,128)S(1)}, f32[2,39,16,128]{3,2,1,0:T(8,128)S(1)}, u32[]{:S(2)}, u32[]{:S(2)}) collective-permute-start(f32[2,39,16,128]{3,2,1,0:T(8,128)S(1)} %get-tuple-element.29.z_own), channel_id=1, source_target_pairs={{0,24},{24,0},{48,72},{72,48},{96,120},{120,96},{144,168},{168,144... | collective-permute-start | bytes 1916936 | tf_op jit(solution)/shard_map/ppermute | solution.py:492
  39.5 12.2 %collective-permute-start.4 = (f32[25,16,128]{2,1,0:T(8,128)S(1)}, f32[25,16,128]{2,1,0:T(8,128)S(1)}, u32[]{:S(2)}, u32[]{:S(2)}) collective-permute-start(f32[25,16,128]{2,1,0:T(8,128)S(1)} %get-tuple-element.30), channel_id=1, source_target_pairs={{0,48},{24,72},{48,0},{72,24},{96,144},{120,168},{144,96},{168,120... | collective-permute-start | bytes 614408 | tf_op jit(solution)/shard_map/ppermute | solution.py:492
  46.0 9.1 %collective-permute-start.5 = (f32[25,16,128]{2,1,0:T(8,128)S(1)}, f32[25,16,128]{2,1,0:T(8,128)S(1)}, u32[]{:S(2)}, u32[]{:S(2)}) collective-permute-start(f32[25,16,128]{2,1,0:T(8,128)S(1)} %get-tuple-element.31), channel_id=1, source_target_pairs={{0,720},{24,744},{48,96},{72,120},{96,48},{120,72},{144,192},{168,... | collective-permute-start | bytes 614408 | tf_op jit(solution)/shard_map/ppermute | solution.py:497

commit v3 on v2

--- a/solution.py
+++ b/solution.py
@@ -180,10 +180,10 @@
         for k in range(Q):
             put8(s0, plane, 0, k, start[k, plane])
         sol = solid[plane].astype(jnp.float32)
-        z[plane, SOLID, 4:12, :] = sol
+        z[plane, SOLID] = sol
         mask = sol > 0.5
         for k in range(Q):
-            z[plane, Q + place[k], 4:12, :] = jnp.where(
+            z[plane, Q + place[k]] = jnp.where(
                 mask, adjoint[opposite[k], plane], adjoint[k, plane]
             )
     state = jnp.concatenate([load_rows(s0, plane, 0, 8) for plane in range(2)], axis=1)
@@ -197,12 +197,12 @@
         )
     for plane in range(2):
         for k in range(Q):
-            z[plane, place[k], 4:12, :] = get8(p1, plane, 0, k)
+            z[plane, place[k]] = get8(p1, plane, 0, k)
 
     def pack(ref, way):
         at = 0
         for plane, unit, rows in y_pieces(way):
-            begin = 12 - rows if way == 1 else 4
+            begin = 8 - rows if way == 1 else 0
             ref[at : at + rows, :] = z[plane, unit, begin : begin + rows, :]
             at += rows
         ref[at:, :] = jnp.zeros((Y_ROWS - at, W), jnp.float32)
@@ -220,8 +220,12 @@
         pack(to_odd, 1)
 
 
-def second_kernel(z_in, from_even, from_odd, z, to_near, to_far):
-    z[...] = z_in[...]
+def near_kernel(z_own, z):
+    z[...] = z_own[...]
+
+
+def second_kernel(z_own, from_even, from_odd, z, to_near, to_far):
+    z[:, :, 4:12, :] = z_own[...]
 
     def unpack(ref, way):
         at = 0
@@ -270,6 +274,10 @@
 FAR = 25
 
 
+def hold_kernel(f_in, f):
+    f[...] = f_in[...]
+
+
 PLANES = 10
 ROWS = 16
 
@@ -277,8 +285,8 @@
 def third_kernel(
     scale,
     s0, z_own, z_even, z_odd, f_near, f_far, w1x, w2x, w2tx, w1tx, b2b,
-    final, grad, sums,
-    zs, s1, p2, s2, p3, gp, g, acc1, acc2, sems,
+    final_hbm, grad_hbm, sums,
+    final, grad, out_sems, zs, s1, p2, s2, p3, gp, g, acc1, acc2, sems,
 ):
     index = lax.axis_index("gx")
     odd = lax.rem(index, 2)
@@ -426,6 +434,8 @@
         moved = reflect(moved, zs[plane + 4, SOLID, 4:12, :] > 0.5)
         for k in range(Q):
             final[k, plane] = moved[k]
+    final_copy = pltpu.make_async_copy(final, final_hbm, out_sems.at[0])
+    final_copy.start()
 
     def run_back(g_ref, g_plane, zx, y, out_plane):
         for k in range(Q):
@@ -465,6 +475,8 @@
         return carry
 
     over_planes(0, stage4)
+    grad_copy = pltpu.make_async_copy(grad, grad_hbm, out_sems.at[1])
+    grad_copy.start()
 
     one = acc1[0:T, :] + acc1[T : 2 * T, :]
     two = acc2[0:T, :] + acc2[T : 2 * T, :]
@@ -475,6 +487,8 @@
     sums[0:T, 0:HID] = in_part * scale
     sums[0:Q, HID : 2 * HID] = out_part[0:Q, :] * scale
     sums[ONE : ONE + 1, HID : HID + T] = bias[ONE : ONE + 1, :] * scale
+    final_copy.wait()
+    grad_copy.wait()
 
 
 def last_kernel(parts, grad_w_in_t, grad_b_in, grad_w_out, grad_b_out):
@@ -537,7 +551,7 @@
     z, to_even, to_odd, s0, w1x, w2x, w2tx, w1tx, b2b = pl.pallas_call(
         first_kernel,
         out_shape=(
-            shape(2, UNITS, ROWS, W),
+            shape(2, UNITS, 8, W),
             shape(Y_ROWS, W),
             shape(Y_ROWS, W),
             shape(2, 8 * T, W),
@@ -567,6 +581,12 @@
     from_even = swap_even(to_even, "gy")
     from_odd = swap_odd(to_odd, "gy")
 
+    z = pl.pallas_call(
+        near_kernel,
+        out_shape=shape(2, UNITS, 8, W),
+        compiler_params=PARAMS,
+        name="near",
+    )(z)
     z, to_near, to_far = pl.pallas_call(
         second_kernel,
         out_shape=(shape(2, UNITS, ROWS, W), shape(FAR, ROWS, W), shape(FAR, ROWS, W)),
@@ -578,6 +598,14 @@
     f_far = swap_odd(to_far, "gx", 2)
     f_near = swap_even(to_near, "gx", 2)
     z_even = swap_even(z, "gx")
+
+    f_far = pl.pallas_call(
+        hold_kernel,
+        out_shape=shape(FAR, ROWS, W),
+        compiler_params=PARAMS,
+        cost_estimate=pl.CostEstimate(flops=6 * 10**9, bytes_accessed=10**6, transcendentals=0),
+        name="hold",
+    )(f_far)
 
     cells = 16 * W * lax.axis_size("gx") * lax.axis_size("gy")
     vmem = pl.BlockSpec(memory_space=pltpu.VMEM)
@@ -586,7 +614,11 @@
         functools.partial(third_kernel, 1.0 / math.sqrt(cells)),
         out_shape=(shape(Q, 2, 8, W), shape(Q, 2, 8, W), shape(T, W)),
         in_specs=[vmem] + [hbm] * 5 + [vmem] * 5,
+        out_specs=(hbm, hbm, vmem),
         scratch_shapes=[
+            rows((Q, 2, 8, W), F32),
+            rows((Q, 2, 8, W), F32),
+            pltpu.SemaphoreType.DMA((2,)),
             rows((PLANES, UNITS, ROWS, W), F32),
             rows((8, ROWS * T, W), F32),
             rows((8, ROWS * T, W), F32),

time: 106 us -> 104 us (0.981)
  blocking collectives: 40.2 us -> 38.2 us
    ppermute x3, starting transfers between devices: 21.1 us -> 26.9 us  [swap_odd(): lax.ppermute(x, axis, [(i, (i + step if i & step else i - step) % count)...]
    ppermute x3, starting transfers between devices: 13.4 us -> 8.32 us  [swap_even(): return lax.ppermute(x, axis, [(i, i ^ step) for i in range(count)])]
    ppermute x3, waiting for transfers between devices: 12.2 us -> 7.86 us  [swap_odd(): lax.ppermute(x, axis, [(i, (i + step if i & step else i - step) % count)...]
    ppermute x3, waiting for transfers between devices: 3.8 us -> 7.35 us  [swap_even(): return lax.ppermute(x, axis, [(i, i ^ step) for i in range(count)])]
    all_to_all x3, blocking collectives: 40.2 us -> 38.2 us  [spread(): lax.all_to_all(jnp.broadcast_to(x[None], (count,) + x.shape), ('gx', 'gy'...]
    pallas_call x1 -> x3, Pallas kernels: 2.61 us -> 2.53 us  [the longest x1 2.49 us: on_device(): pl.pallas_call(first_kernel, out_shape=(shape(2, UNITS, 8, W), shape(Y_RO...]
  transfers between devices with their start and end apart: 6 -> 6, of which waited for: 3 -> 2; matrix products, arithmetic and copies ran while one was open for 0% -> 0% of each run, Pallas kernels for 0% -> 0%
where the time goes in v3:
time: 104 us
  blocking collectives  38.2 us (37%)
  starting transfers between devices  35.3 us (34%)
  waiting for transfers between devices  15.2 us (15%)
  Pallas kernels  12.9 us (12%)
    all_to_all x3, blocking collectives, spread(): lax.all_to_all(jnp.broadcast_to(x[None], (count,) + x.shape), ('gx', 'gy'...  38.2 us
    ppermute x3, starting transfers between devices, swap_odd(): lax.ppermute(x, axis, [(i, (i + step if i & step else i - step) % count)...  26.9 us
    pallas_call x1, Pallas kernels, on_device(): pl.pallas_call(functools.partial(third_kernel, 1.0 / math.sqrt(cells)), o...  9.57 us
    ppermute x3, starting transfers between devices, swap_even(): return lax.ppermute(x, axis, [(i, i ^ step) for i in range(count)])  8.32 us
    ppermute x3, waiting for transfers between devices, swap_odd(): lax.ppermute(x, axis, [(i, (i + step if i & step else i - step) % count)...  7.86 us
    ppermute x3, waiting for transfers between devices, swap_even(): return lax.ppermute(x, axis, [(i, i ^ step) for i in range(count)])  7.35 us
    pallas_call x1, Pallas kernels, on_device(): pl.pallas_call(first_kernel, out_shape=(shape(2, UNITS, 8, W), shape(Y_RO...  2.49 us
  transfers between devices with their start and end apart: 6, of which 2 were waited for; matrix products, arithmetic and copies ran while one was open for 0% of the time, Pallas kernels for 0%

profile of v3, /device:TPU:2, one launch (start us, length us, event | category | flops | bytes accessed | tf_op | source)
XLA Modules:
  0.0 103.5 jit_solution(3685833924824693063)
XLA Ops:
  0.6 2.5 %first.1 = (f32[2,39,8,128]{3,2,1,0:T(8,128)}, f32[200,128]{1,0:T(8,128)}, f32[200,128]{1,0:T(8,128)}, f32[2,192,128]{2,1,0:T(8,128)}, f32[64,80]{1,0:T(8,128)},...) custom-call(f32[19,2,8,128]{3,2,1,0:T(8,128)} %start_hbm.1, ...), custom_call_target="tpu_custom_call" | custom-call | tf_op jit(solution)/shard_map/first/pallas_call | solution.py:551
  3.1 3.5 %collective-permute-start = (f32[200,128]{1,0:T(8,128)}, f32[200,128]{1,0:T(8,128)S(1)}, u32[]{:S(2)}, u32[]{:S(2)}) collective-permute-start(f32[200,128]{1,0:T(8,128)} %get-tuple-element.27), channel_id=1, source_target_pairs={{0,1},{1,0},{2,3},{3,2},{4,5},{5,4},{6,7},{7,6},{8,9},{9,8},{10,11... | collective-permute-start | bytes 307208 | tf_op jit(solution)/shard_map/ppermute | solution.py:506
  6.6 17.2 %collective-permute-start.1 = (f32[200,128]{1,0:T(8,128)}, f32[200,128]{1,0:T(8,128)S(1)}, u32[]{:S(2)}, u32[]{:S(2)}) collective-permute-start(f32[200,128]{1,0:T(8,128)} %get-tuple-element.28), channel_id=1, source_target_pairs={{0,23},{1,2},{2,1},{3,4},{4,3},{5,6},{6,5},{7,8},{8,7},{9,10},{10,... | collective-permute-start | bytes 307208 | tf_op jit(solution)/shard_map/ppermute | solution.py:511
  23.9 0.0 copy-start
  23.9 1.0 copy-done
  24.9 0.0 collective-permute-done.from_even
  24.9 7.9 %collective-permute-done.1.from_odd = f32[200,128]{1,0:T(8,128)S(1)} collective-permute-done((f32[200,128]{1,0:T(8,128)}, f32[200,128]{1,0:T(8,128)S(1)}, u32[]{:S(2)}, u32[]{:S(2)}) %collective-permute-start.1) | collective-permute-done | bytes 102432 | tf_op jit(solution)/shard_map/ppermute | solution.py:511
  32.7 0.1 second.1
  32.9 3.4 %collective-permute-start.5 = (f32[25,16,128]{2,1,0:T(8,128)S(1)}, f32[25,16,128]{2,1,0:T(8,128)S(1)}, u32[]{:S(2)}, u32[]{:S(2)}) collective-permute-start(f32[25,16,128]{2,1,0:T(8,128)S(1)} %get-tuple-element.31), channel_id=1, source_target_pairs={{0,720},{24,744},{48,96},{72,120},{96,48},{120,72},{144,192},{168,... | collective-permute-start | bytes 614408 | tf_op jit(solution)/shard_map/ppermute | solution.py:511
  36.3 6.3 %collective-permute-start.3 = (f32[2,39,16,128]{3,2,1,0:T(8,128)S(1)}, f32[2,39,16,128]{3,2,1,0:T(8,128)S(1)}, u32[]{:S(2)}, u32[]{:S(2)}) collective-permute-start(f32[2,39,16,128]{3,2,1,0:T(8,128)S(1)} %get-tuple-element.29.z_own), channel_id=1, source_target_pairs={{0,744},{24,48},{48,24},{72,96},{96,72},{120,144},{144,120},{168,1... | collective-permute-start | bytes 1916936 | tf_op jit(solution)/shard_map/ppermute | solution.py:511
  42.6 1.9 %collective-permute-start.2 = (f32[2,39,16,128]{3,2,1,0:T(8,128)S(1)}, f32[2,39,16,128]{3,2,1,0:T(8,128)S(1)}, u32[]{:S(2)}, u32[]{:S(2)}) collective-permute-start(f32[2,39,16,128]{3,2,1,0:T(8,128)S(1)} %get-tuple-element.29.z_own), channel_id=1, source_target_pairs={{0,24},{24,0},{48,72},{72,48},{96,120},{120,96},{144,168},{168,144... | collective-permute-start | bytes 1916936 | tf_op jit(solution)/shard_map/ppermute | solution.py:506
  44.5 0.0 copy-start.1
  44.5 2.9 %collective-permute-start.4 = (f32[25,16,128]{2,1,0:T(8,128)S(1)}, f32[25,16,128]{2,1,0:T(8,128)S(1)}, u32[]{:S(2)}, u32[]{:S(2)}) collective-permute-start(f32[25,16,128]{2,1,0:T(8,128)S(1)} %get-tuple-element.30), channel_id=1, source_target_pairs={{0,48},{24,72},{48,0},{72,24},{96,144},{120,168},{144,96},{168,120... | collective-permute-start | bytes 614408 | tf_op jit(solution)/shard_map/ppermute | solution.py:506
  47.4 0.0 collective-permute-done.5.f_in
  47.5 0.0 copy-start.2
  47.5 0.0 copy-start.3
  47.5 0.0 copy-start.4
  47.5 0.0 copy-start.5
  47.5 0.0 copy-start.6
  47.5 7.3 %collective-permute-done.4.f_near = f32[25,16,128]{2,1,0:T(8,128)S(1)} collective-permute-done((f32[25,16,128]{2,1,0:T(8,128)S(1)}, f32[25,16,128]{2,1,0:T(8,128)S(1)}, u32[]{:S(2)}, u32[]{:S(2)}) %collective-permute-start.4) | collective-permute-done | bytes 204832 | tf_op jit(solution)/shard_map/ppermute | solution.py:506
  54.9 0.0 collective-permute-done.3.z_odd
  54.9 0.0 collective-permute-done.2.z_even
  54.9 0.0 copy-done.1
  54.9 0.0 copy-done.2
  54.9 0.0 copy-done.3
  54.9 0.0 copy-done.4
  54.9 0.0 copy-done.5
  54.9 0.0 copy-done.6
  54.9 9.6 %third.1 = (f32[19,2,8,128]{3,2,1,0:T(8,128)}, f32[19,2,8,128]{3,2,1,0:T(8,128)}, f32[24,128]{1,0:T(8,128)S(1)}) custom-call(f32[2,192,128]{2,1,0:T(8,128)S(1)} %copy-done.1, f32[2,39,16,128]{3,2,1,0:T(8,128)S(1)} %get-tuple-element.29.z_own, f32[2,39,16,128]{3,2,1,0:T(8,128)S(1)} %collective-permute-done.2.z_even, ...), custom_call_target="tpu_custom_call" | custom-call | tf_op jit(solution)/shard_map/third/pallas_call | solution.py:613
  64.5 9.2 %all_to_all.15 = f32[8,24,128]{2,1,0:T(8,128)S(1)} all-to-all(f32[8,24,128]{2,1,0:T(8,128)S(1)} %broadcast_in_dim.6), channel_id=1, replica_groups={{0,24,48,72,96,120,144,168},{1,25,49,73,97,121,145,169},{2,26,50,74,98,..., dimensions={0} | all-to-all | bytes 196608 | tf_op jit(solution)/shard_map/all_to_all | solution.py:518
  73.8 17.7 %all_to_all.16 = f32[12,24,128]{2,1,0:T(8,128)S(1)} all-to-all(f32[12,24,128]{2,1,0:T(8,128)S(1)} %broadcast_in_dim.7), channel_id=1, replica_groups={{0,192,384,576,8,200,392,584,16,208,400,592},{1,193,385,577,9,201,393,5..., dimensions={0} | all-to-all | bytes 294912 | tf_op jit(solution)/shard_map/all_to_all | solution.py:518
  91.5 11.3 %all_to_all.17.parts = f32[8,24,128]{2,1,0:T(8,128)S(1)} all-to-all(f32[8,24,128]{2,1,0:T(8,128)S(1)} %broadcast_in_dim.8), channel_id=1, replica_groups={{0,1,2,3,4,5,6,7},{24,25,26,27,28,29,30,31},{48,49,50,51,52,53,54,55},{..., dimensions={0} | all-to-all | bytes 196608 | tf_op jit(solution)/shard_map/all_to_all | solution.py:518
  102.8 0.7 last.1
  (7 shorter events, 0.1 us)
Async XLA Ops:
  3.1 21.7 %collective-permute-start = (f32[200,128]{1,0:T(8,128)}, f32[200,128]{1,0:T(8,128)S(1)}, u32[]{:S(2)}, u32[]{:S(2)}) collective-permute-start(f32[200,128]{1,0:T(8,128)} %get-tuple-element.27), channel_id=1, source_target_pairs={{0,1},{1,0},{2,3},{3,2},{4,5},{5,4},{6,7},{7,6},{8,9},{9,8},{10,11... | collective-permute-start | bytes 307208 | tf_op jit(solution)/shard_map/ppermute | solution.py:506
  6.6 26.1 %collective-permute-start.1 = (f32[200,128]{1,0:T(8,128)}, f32[200,128]{1,0:T(8,128)S(1)}, u32[]{:S(2)}, u32[]{:S(2)}) collective-permute-start(f32[200,128]{1,0:T(8,128)} %get-tuple-element.28), channel_id=1, source_target_pairs={{0,23},{1,2},{2,1},{3,4},{4,3},{5,6},{6,5},{7,8},{8,7},{9,10},{10,... | collective-permute-start | bytes 307208 | tf_op jit(solution)/shard_map/ppermute | solution.py:511
  23.9 1.0 copy-start
  32.9 14.6 %collective-permute-start.5 = (f32[25,16,128]{2,1,0:T(8,128)S(1)}, f32[25,16,128]{2,1,0:T(8,128)S(1)}, u32[]{:S(2)}, u32[]{:S(2)}) collective-permute-start(f32[25,16,128]{2,1,0:T(8,128)S(1)} %get-tuple-element.31), channel_id=1, source_target_pairs={{0,720},{24,744},{48,96},{72,120},{96,48},{120,72},{144,192},{168,... | collective-permute-start | bytes 614408 | tf_op jit(solution)/shard_map/ppermute | solution.py:511
  36.3 18.6 %collective-permute-start.3 = (f32[2,39,16,128]{3,2,1,0:T(8,128)S(1)}, f32[2,39,16,128]{3,2,1,0:T(8,128)S(1)}, u32[]{:S(2)}, u32[]{:S(2)}) collective-permute-start(f32[2,39,16,128]{3,2,1,0:T(8,128)S(1)} %get-tuple-element.29.z_own), channel_id=1, source_target_pairs={{0,744},{24,48},{48,24},{72,96},{96,72},{120,144},{144,120},{168,1... | collective-permute-start | bytes 1916936 | tf_op jit(solution)/shard_map/ppermute | solution.py:511
  42.6 12.3 %collective-permute-start.2 = (f32[2,39,16,128]{3,2,1,0:T(8,128)S(1)}, f32[2,39,16,128]{3,2,1,0:T(8,128)S(1)}, u32[]{:S(2)}, u32[]{:S(2)}) collective-permute-start(f32[2,39,16,128]{3,2,1,0:T(8,128)S(1)} %get-tuple-element.29.z_own), channel_id=1, source_target_pairs={{0,24},{24,0},{48,72},{72,48},{96,120},{120,96},{144,168},{168,144... | collective-permute-start | bytes 1916936 | tf_op jit(solution)/shard_map/ppermute | solution.py:506
  44.5 10.4 %copy-start.1 = (f32[2,192,128]{2,1,0:T(8,128)S(1)}, f32[2,192,128]{2,1,0:T(8,128)}, u32[]{:S(2)}) copy-start(f32[2,192,128]{2,1,0:T(8,128)} %get-tuple-element.25.s0) | copy-start | bytes 589828
  44.5 10.4 %collective-permute-start.4 = (f32[25,16,128]{2,1,0:T(8,128)S(1)}, f32[25,16,128]{2,1,0:T(8,128)S(1)}, u32[]{:S(2)}, u32[]{:S(2)}) collective-permute-start(f32[25,16,128]{2,1,0:T(8,128)S(1)} %get-tuple-element.30), channel_id=1, source_target_pairs={{0,48},{24,72},{48,0},{72,24},{96,144},{120,168},{144,96},{168,120... | collective-permute-start | bytes 614408 | tf_op jit(solution)/shard_map/ppermute | solution.py:506
  47.5 7.4 %copy-start.2 = (f32[64,80]{1,0:T(8,128)S(1)}, f32[64,80]{1,0:T(8,128)}, u32[]{:S(2)}) copy-start(f32[64,80]{1,0:T(8,128)} %get-tuple-element.32.w1x) | copy-start | bytes 61444
  47.5 7.4 %copy-start.3 = (f32[64,80]{1,0:T(8,128)S(1)}, f32[64,80]{1,0:T(8,128)}, u32[]{:S(2)}) copy-start(f32[64,80]{1,0:T(8,128)} %get-tuple-element.34.w2tx) | copy-start | bytes 61444
  47.5 7.4 %copy-start.4 = (f32[48,128]{1,0:T(8,128)S(1)}, f32[48,128]{1,0:T(8,128)}, u32[]{:S(2)}) copy-start(f32[48,128]{1,0:T(8,128)} %get-tuple-element.33.w2x) | copy-start | bytes 73732
  47.5 7.4 %copy-start.5 = (f32[48,128]{1,0:T(8,128)S(1)}, f32[48,128]{1,0:T(8,128)}, u32[]{:S(2)}) copy-start(f32[48,128]{1,0:T(8,128)} %get-tuple-element.35.w1tx) | copy-start | bytes 73732
  47.5 7.4 %copy-start.6 = (f32[24,128]{1,0:T(8,128)S(1)}, f32[24,128]{1,0:T(8,128)}, u32[]{:S(2)}) copy-start(f32[24,128]{1,0:T(8,128)} %get-tuple-element.36.b2b) | copy-start | bytes 36868

commit v4 on v3

--- a/solution.py
+++ b/solution.py
@@ -131,6 +131,10 @@
     tile = pad_tile()
     for i in range(count):
         ref[plane, (first + i) * T + 16 : (first + i + 1) * T, :] = tile
+
+
+def reflect(values, mask):
+    return [jnp.where(mask, values[opposite[k]], values[k]) for k in range(Q)]
 
 
 def chunks(count, size):
@@ -285,8 +289,8 @@
 def third_kernel(
     scale,
     s0, z_own, z_even, z_odd, f_near, f_far, w1x, w2x, w2tx, w1tx, b2b,
-    final_hbm, grad_hbm, sums,
-    final, grad, out_sems, zs, s1, p2, s2, p3, gp, g, acc1, acc2, sems,
+    sums, p3, g,
+    zs, s1, p2, s2, gp, acc1, acc2, sems,
 ):
     index = lax.axis_index("gx")
     odd = lax.rem(index, 2)
@@ -322,7 +326,7 @@
         for i in range(ROWS):
             gp[plane, i * T + 16 : (i + 1) * T, :] = jnp.zeros((8, W), jnp.float32)
 
-    for copy in copies:
+    for copy in copies[:3]:
         copy.wait()
 
     def fluid_rows(x, y):
@@ -375,9 +379,6 @@
                 unroll=2 * halo,
             )
         lax.fori_loop(0, 2, lambda i, c: body(True, i + halo, c), 0, unroll=2)
-
-    def reflect(values, mask):
-        return [jnp.where(mask, values[opposite[k]], values[k]) for k in range(Q)]
 
     def stage1(j, carry):
         zx = j + 1
@@ -396,7 +397,10 @@
             collide(p2, j, zx, first, count, state, split(hidden))
         return carry
 
-    lax.fori_loop(0, 8, stage1, 0, unroll=8)
+    lax.fori_loop(2, 6, stage1, 0, unroll=4)
+    for copy in copies[3:]:
+        copy.wait()
+    lax.fori_loop(0, 4, lambda i, c: stage1(jnp.where(i < 2, i, i + 4), c), 0, unroll=4)
 
     def stage2(own, j, carry):
         zx = j + 2
@@ -426,17 +430,6 @@
 
     over_planes(2, stage2)
 
-    for plane in range(2):
-        moved = []
-        for k in range(Q):
-            cx, cy, cz = velocities[k]
-            moved.append(z_shift(get8(p3, plane + 2 - cx, 4 - cy, k), cz))
-        moved = reflect(moved, zs[plane + 4, SOLID, 4:12, :] > 0.5)
-        for k in range(Q):
-            final[k, plane] = moved[k]
-    final_copy = pltpu.make_async_copy(final, final_hbm, out_sems.at[0])
-    final_copy.start()
-
     def run_back(g_ref, g_plane, zx, y, out_plane):
         for k in range(Q):
             cx, cy, cz = velocities[k]
@@ -470,13 +463,9 @@
             grad_post = load_rows(gp, j, first, count)
             back = backward(own, zx, first, count, state_parts, hidden, split(hidden), grad_post)
             store_rows(g, j, first, count, back)
-        for k in range(Q):
-            grad[k, j] = get8(g, j, 4, k)
         return carry
 
     over_planes(0, stage4)
-    grad_copy = pltpu.make_async_copy(grad, grad_hbm, out_sems.at[1])
-    grad_copy.start()
 
     one = acc1[0:T, :] + acc1[T : 2 * T, :]
     two = acc2[0:T, :] + acc2[T : 2 * T, :]
@@ -487,8 +476,18 @@
     sums[0:T, 0:HID] = in_part * scale
     sums[0:Q, HID : 2 * HID] = out_part[0:Q, :] * scale
     sums[ONE : ONE + 1, HID : HID + T] = bias[ONE : ONE + 1, :] * scale
-    final_copy.wait()
-    grad_copy.wait()
+
+
+def fourth_kernel(z, p3, g, final, grad):
+    for plane in range(2):
+        moved = []
+        for k in range(Q):
+            cx, cy, cz = velocities[k]
+            moved.append(z_shift(get8(p3, plane + 2 - cx, 4 - cy, k), cz))
+        moved = reflect(moved, z[plane, SOLID, 4:12, :] > 0.5)
+        for k in range(Q):
+            final[k, plane] = moved[k]
+            grad[k, plane] = get8(g, plane, 4, k)
 
 
 def last_kernel(parts, grad_w_in_t, grad_b_in, grad_w_out, grad_b_out):
@@ -610,20 +609,15 @@
     cells = 16 * W * lax.axis_size("gx") * lax.axis_size("gy")
     vmem = pl.BlockSpec(memory_space=pltpu.VMEM)
     hbm = pl.BlockSpec(memory_space=pl.ANY)
-    final, grad, sums = pl.pallas_call(
+    sums, p3, g = pl.pallas_call(
         functools.partial(third_kernel, 1.0 / math.sqrt(cells)),
-        out_shape=(shape(Q, 2, 8, W), shape(Q, 2, 8, W), shape(T, W)),
+        out_shape=(shape(T, W), shape(6, ROWS * T, W), shape(6, ROWS * T, W)),
         in_specs=[vmem] + [hbm] * 5 + [vmem] * 5,
-        out_specs=(hbm, hbm, vmem),
+        out_specs=(vmem, vmem, vmem),
         scratch_shapes=[
-            rows((Q, 2, 8, W), F32),
-            rows((Q, 2, 8, W), F32),
-            pltpu.SemaphoreType.DMA((2,)),
             rows((PLANES, UNITS, ROWS, W), F32),
             rows((8, ROWS * T, W), F32),
             rows((8, ROWS * T, W), F32),
-            rows((6, ROWS * T, W), F32),
-            rows((6, ROWS * T, W), F32),
             rows((6, ROWS * T, W), F32),
             rows((6, ROWS * T, W), F32),
             rows((2 * T, 2 * HID + 2 * T), F32),
@@ -633,6 +627,14 @@
         compiler_params=PARAMS,
         name="third",
     )(s0, z, z_even, z_odd, f_near, f_far, w1x, w2x, w2tx, w1tx, b2b)
+
+    final, grad = pl.pallas_call(
+        fourth_kernel,
+        out_shape=(shape(Q, 2, 8, W), shape(Q, 2, 8, W)),
+        compiler_params=PARAMS,
+        cost_estimate=pl.CostEstimate(flops=10**9, bytes_accessed=10**6, transcendentals=0),
+        name="fourth",
+    )(z, p3, g)
 
     along_x, along_z, along_y = sum_groups()
     sums = spread(sums, along_x).sum(0)

time: 104 us -> 105 us (level)
  blocking collectives: 38.2 us -> 26.9 us
  waiting for transfers between devices: 15.2 us -> 23.1 us
  starting transfers between devices: 35.3 us -> 38.6 us
    all_to_all x3 -> x2, blocking collectives: 38.2 us -> 26.9 us  [spread(): lax.all_to_all(jnp.broadcast_to(x[None], (count,) + x.shape), ('gx', 'gy'...]
    all_to_all x0 -> x1, waiting for transfers between devices: none -> 7.87 us  [spread(): lax.all_to_all(jnp.broadcast_to(x[None], (count,) + x.shape), ('gx', 'gy'...]
    all_to_all x0 -> x1, starting transfers between devices: none -> 3.36 us  [spread(): lax.all_to_all(jnp.broadcast_to(x[None], (count,) + x.shape), ('gx', 'gy'...]
  transfers between devices with their start and end apart: 6 -> 7, of which waited for: 2 -> 3; matrix products, arithmetic and copies ran while one was open for 0% -> 0% of each run, Pallas kernels for 0% -> 1%
where the time goes in v4:
time: 105 us; the launch traced here: 104 us
  starting transfers between devices  38.6 us (37%)
  blocking collectives  26.9 us (26%)
  waiting for transfers between devices  23.1 us (22%)
  Pallas kernels  13.2 us (13%)
  local copies, waits for them, and re-layouts  1.65 us (2%)
    ppermute x3, starting transfers between devices, swap_odd(): lax.ppermute(x, axis, [(i, (i + step if i & step else i - step) % count)...  26.9 us
    all_to_all x2, blocking collectives, spread(): lax.all_to_all(jnp.broadcast_to(x[None], (count,) + x.shape), ('gx', 'gy'...  26.9 us
    pallas_call x1, Pallas kernels, on_device(): pl.pallas_call(functools.partial(third_kernel, 1.0 / math.sqrt(cells)), o...  9.1 us
    ppermute x3, starting transfers between devices, swap_even(): return lax.ppermute(x, axis, [(i, i ^ step) for i in range(count)])  8.32 us
    all_to_all x1, waiting for transfers between devices, spread(): lax.all_to_all(jnp.broadcast_to(x[None], (count,) + x.shape), ('gx', 'gy'...  7.87 us
    ppermute x3, waiting for transfers between devices, swap_odd(): lax.ppermute(x, axis, [(i, (i + step if i & step else i - step) % count)...  7.86 us
    ppermute x3, waiting for transfers between devices, swap_even(): return lax.ppermute(x, axis, [(i, i ^ step) for i in range(count)])  7.35 us
    all_to_all x1, starting transfers between devices, spread(): lax.all_to_all(jnp.broadcast_to(x[None], (count,) + x.shape), ('gx', 'gy'...  3.36 us
  transfers between devices with their start and end apart: 7, of which 3 were waited for; matrix products, arithmetic and copies ran while one was open for 0% of the time, Pallas kernels for 1%

profile of v4, /device:TPU:2, one launch (start us, length us, event | category | flops | bytes accessed | tf_op | source)
XLA Modules:
  0.0 104.4 jit_solution(1230228401062836021)
XLA Ops:
  0.6 2.5 %first.1 = (f32[2,39,8,128]{3,2,1,0:T(8,128)}, f32[200,128]{1,0:T(8,128)}, f32[200,128]{1,0:T(8,128)}, f32[2,192,128]{2,1,0:T(8,128)}, f32[64,80]{1,0:T(8,128)},...) custom-call(f32[19,2,8,128]{3,2,1,0:T(8,128)} %start_hbm.1, ...), custom_call_target="tpu_custom_call" | custom-call | tf_op jit(solution)/shard_map/first/pallas_call | solution.py:550
  3.1 3.5 %collective-permute-start = (f32[200,128]{1,0:T(8,128)}, f32[200,128]{1,0:T(8,128)S(1)}, u32[]{:S(2)}, u32[]{:S(2)}) collective-permute-start(f32[200,128]{1,0:T(8,128)} %get-tuple-element.28), channel_id=1, source_target_pairs={{0,1},{1,0},{2,3},{3,2},{4,5},{5,4},{6,7},{7,6},{8,9},{9,8},{10,11... | collective-permute-start | bytes 307208 | tf_op jit(solution)/shard_map/ppermute | solution.py:505
  6.6 17.2 %collective-permute-start.1 = (f32[200,128]{1,0:T(8,128)}, f32[200,128]{1,0:T(8,128)S(1)}, u32[]{:S(2)}, u32[]{:S(2)}) collective-permute-start(f32[200,128]{1,0:T(8,128)} %get-tuple-element.29), channel_id=1, source_target_pairs={{0,23},{1,2},{2,1},{3,4},{4,3},{5,6},{6,5},{7,8},{8,7},{9,10},{10,... | collective-permute-start | bytes 307208 | tf_op jit(solution)/shard_map/ppermute | solution.py:510
  23.9 0.0 copy-start
  23.9 1.0 copy-done
  24.9 0.0 collective-permute-done.from_even
  24.9 7.9 %collective-permute-done.1.from_odd = f32[200,128]{1,0:T(8,128)S(1)} collective-permute-done((f32[200,128]{1,0:T(8,128)}, f32[200,128]{1,0:T(8,128)S(1)}, u32[]{:S(2)}, u32[]{:S(2)}) %collective-permute-start.1) | collective-permute-done | bytes 102432 | tf_op jit(solution)/shard_map/ppermute | solution.py:510
  32.7 0.1 second.1
  32.9 3.4 %collective-permute-start.5 = (f32[25,16,128]{2,1,0:T(8,128)S(1)}, f32[25,16,128]{2,1,0:T(8,128)S(1)}, u32[]{:S(2)}, u32[]{:S(2)}) collective-permute-start(f32[25,16,128]{2,1,0:T(8,128)S(1)} %get-tuple-element.33), channel_id=1, source_target_pairs={{0,720},{24,744},{48,96},{72,120},{96,48},{120,72},{144,192},{168,... | collective-permute-start | bytes 614408 | tf_op jit(solution)/shard_map/ppermute | solution.py:510
  36.3 6.3 %collective-permute-start.3 = (f32[2,39,16,128]{3,2,1,0:T(8,128)S(1)}, f32[2,39,16,128]{3,2,1,0:T(8,128)S(1)}, u32[]{:S(2)}, u32[]{:S(2)}) collective-permute-start(f32[2,39,16,128]{3,2,1,0:T(8,128)S(1)} %get-tuple-element.30.z_own.z), channel_id=1, source_target_pairs={{0,744},{24,48},{48,24},{72,96},{96,72},{120,144},{144,120},{168,1... | collective-permute-start | bytes 1916936 | tf_op jit(solution)/shard_map/ppermute | solution.py:510
  42.6 1.9 %collective-permute-start.2 = (f32[2,39,16,128]{3,2,1,0:T(8,128)S(1)}, f32[2,39,16,128]{3,2,1,0:T(8,128)S(1)}, u32[]{:S(2)}, u32[]{:S(2)}) collective-permute-start(f32[2,39,16,128]{3,2,1,0:T(8,128)S(1)} %get-tuple-element.30.z_own.z), channel_id=1, source_target_pairs={{0,24},{24,0},{48,72},{72,48},{96,120},{120,96},{144,168},{168,144... | collective-permute-start | bytes 1916936 | tf_op jit(solution)/shard_map/ppermute | solution.py:505
  44.5 0.0 copy-start.1
  44.5 0.0 copy-start.2
  44.5 0.0 copy-start.3
  44.5 0.0 copy-start.4
  44.5 0.0 copy-start.5
  44.6 0.0 copy-start.6
  44.6 2.9 %collective-permute-start.4 = (f32[25,16,128]{2,1,0:T(8,128)S(1)}, f32[25,16,128]{2,1,0:T(8,128)S(1)}, u32[]{:S(2)}, u32[]{:S(2)}) collective-permute-start(f32[25,16,128]{2,1,0:T(8,128)S(1)} %get-tuple-element.32), channel_id=1, source_target_pairs={{0,48},{24,72},{48,0},{72,24},{96,144},{120,168},{144,96},{168,120... | collective-permute-start | bytes 614408 | tf_op jit(solution)/shard_map/ppermute | solution.py:505
  47.5 0.0 collective-permute-done.5.f_in
  47.5 7.3 %collective-permute-done.4.f_near = f32[25,16,128]{2,1,0:T(8,128)S(1)} collective-permute-done((f32[25,16,128]{2,1,0:T(8,128)S(1)}, f32[25,16,128]{2,1,0:T(8,128)S(1)}, u32[]{:S(2)}, u32[]{:S(2)}) %collective-permute-start.4) | collective-permute-done | bytes 204832 | tf_op jit(solution)/shard_map/ppermute | solution.py:505
  54.9 0.0 collective-permute-done.3.z_odd
  54.9 0.0 collective-permute-done.2.z_even
  54.9 0.0 copy-done.1
  54.9 0.0 copy-done.2
  54.9 0.0 copy-done.3
  54.9 0.0 copy-done.4
  54.9 0.0 copy-done.5
  54.9 0.0 copy-done.6
  54.9 9.1 %third.1 = (f32[24,128]{1,0:T(8,128)S(1)}, f32[6,384,128]{2,1,0:T(8,128)S(1)}, f32[6,384,128]{2,1,0:T(8,128)S(1)}) custom-call(f32[2,192,128]{2,1,0:T(8,128)S(1)} %copy-done.1, f32[2,39,16,128]{3,2,1,0:T(8,128)S(1)} %get-tuple-element.30.z_own.z, f32[2,39,16,128]{3,2,1,0:T(8,128)S(1)} %collective-permute-done.2.z_even, ...), custom_call_target="tpu_custom_call" | custom-call | tf_op jit(solution)/shard_map/third/pallas_call | solution.py:612
  64.1 9.2 %all_to_all.15 = f32[8,24,128]{2,1,0:T(8,128)S(1)} all-to-all(f32[8,24,128]{2,1,0:T(8,128)S(1)} %broadcast_in_dim.6), channel_id=1, replica_groups={{0,24,48,72,96,120,144,168},{1,25,49,73,97,121,145,169},{2,26,50,74,98,..., dimensions={0} | all-to-all | bytes 196608 | tf_op jit(solution)/shard_map/all_to_all | solution.py:517
  73.3 17.7 %all_to_all.16 = f32[12,24,128]{2,1,0:T(8,128)S(1)} all-to-all(f32[12,24,128]{2,1,0:T(8,128)S(1)} %broadcast_in_dim.7), channel_id=1, replica_groups={{0,192,384,576,8,200,392,584,16,208,400,592},{1,193,385,577,9,201,393,5..., dimensions={0} | all-to-all | bytes 294912 | tf_op jit(solution)/shard_map/all_to_all | solution.py:517
  91.0 0.6 broadcast_in_dim.8
  91.7 3.4 %all-to-all-start.2 = ((f32[8,24,128]{2,1,0:T(8,128)}), f32[8,24,128]{2,1,0:T(8,128)S(1)}, u32[]{:S(2)}, u32[]{:S(2)}) async-start(f32[8,24,128]{2,1,0:T(8,128)} %broadcast_in_dim.8), calls=%async_computation.2 | async-start | bytes 196608 | tf_op jit(solution)/shard_map/all_to_all | solution.py:517
  95.0 0.8 fourth.1
  95.8 7.9 %all-to-all-done.2.parts = f32[8,24,128]{2,1,0:T(8,128)S(1)} async-done(((f32[8,24,128]{2,1,0:T(8,128)}), f32[8,24,128]{2,1,0:T(8,128)S(1)}, u32[]{:S(2)}, u32[]{:S(2)}) %all-to-all-start.2) | async-done | bytes 98336 | tf_op jit(solution)/shard_map/all_to_all | solution.py:517
  103.7 0.7 last.1
  (6 shorter events, 0.1 us)
Async XLA Ops:
  3.1 21.7 %collective-permute-start = (f32[200,128]{1,0:T(8,128)}, f32[200,128]{1,0:T(8,128)S(1)}, u32[]{:S(2)}, u32[]{:S(2)}) collective-permute-start(f32[200,128]{1,0:T(8,128)} %get-tuple-element.28), channel_id=1, source_target_pairs={{0,1},{1,0},{2,3},{3,2},{4,5},{5,4},{6,7},{7,6},{8,9},{9,8},{10,11... | collective-permute-start | bytes 307208 | tf_op jit(solution)/shard_map/ppermute | solution.py:505
  6.6 26.1 %collective-permute-start.1 = (f32[200,128]{1,0:T(8,128)}, f32[200,128]{1,0:T(8,128)S(1)}, u32[]{:S(2)}, u32[]{:S(2)}) collective-permute-start(f32[200,128]{1,0:T(8,128)} %get-tuple-element.29), channel_id=1, source_target_pairs={{0,23},{1,2},{2,1},{3,4},{4,3},{5,6},{6,5},{7,8},{8,7},{9,10},{10,... | collective-permute-start | bytes 307208 | tf_op jit(solution)/shard_map/ppermute | solution.py:510
  23.9 1.0 copy-start
  32.9 14.6 %collective-permute-start.5 = (f32[25,16,128]{2,1,0:T(8,128)S(1)}, f32[25,16,128]{2,1,0:T(8,128)S(1)}, u32[]{:S(2)}, u32[]{:S(2)}) collective-permute-start(f32[25,16,128]{2,1,0:T(8,128)S(1)} %get-tuple-element.33), channel_id=1, source_target_pairs={{0,720},{24,744},{48,96},{72,120},{96,48},{120,72},{144,192},{168,... | collective-permute-start | bytes 614408 | tf_op jit(solution)/shard_map/ppermute | solution.py:510
  36.3 18.6 %collective-permute-start.3 = (f32[2,39,16,128]{3,2,1,0:T(8,128)S(1)}, f32[2,39,16,128]{3,2,1,0:T(8,128)S(1)}, u32[]{:S(2)}, u32[]{:S(2)}) collective-permute-start(f32[2,39,16,128]{3,2,1,0:T(8,128)S(1)} %get-tuple-element.30.z_own.z), channel_id=1, source_target_pairs={{0,744},{24,48},{48,24},{72,96},{96,72},{120,144},{144,120},{168,1... | collective-permute-start | bytes 1916936 | tf_op jit(solution)/shard_map/ppermute | solution.py:510
  42.6 12.3 %collective-permute-start.2 = (f32[2,39,16,128]{3,2,1,0:T(8,128)S(1)}, f32[2,39,16,128]{3,2,1,0:T(8,128)S(1)}, u32[]{:S(2)}, u32[]{:S(2)}) collective-permute-start(f32[2,39,16,128]{3,2,1,0:T(8,128)S(1)} %get-tuple-element.30.z_own.z), channel_id=1, source_target_pairs={{0,24},{24,0},{48,72},{72,48},{96,120},{120,96},{144,168},{168,144... | collective-permute-start | bytes 1916936 | tf_op jit(solution)/shard_map/ppermute | solution.py:505
  44.5 10.4 %copy-start.1 = (f32[2,192,128]{2,1,0:T(8,128)S(1)}, f32[2,192,128]{2,1,0:T(8,128)}, u32[]{:S(2)}) copy-start(f32[2,192,128]{2,1,0:T(8,128)} %get-tuple-element.31.s0) | copy-start | bytes 589828
  44.5 10.4 %copy-start.2 = (f32[64,80]{1,0:T(8,128)S(1)}, f32[64,80]{1,0:T(8,128)}, u32[]{:S(2)}) copy-start(f32[64,80]{1,0:T(8,128)} %get-tuple-element.34.w1x) | copy-start | bytes 61444
  44.5 10.4 %copy-start.3 = (f32[64,80]{1,0:T(8,128)S(1)}, f32[64,80]{1,0:T(8,128)}, u32[]{:S(2)}) copy-start(f32[64,80]{1,0:T(8,128)} %get-tuple-element.36.w2tx) | copy-start | bytes 61444
  44.5 10.4 %copy-start.4 = (f32[48,128]{1,0:T(8,128)S(1)}, f32[48,128]{1,0:T(8,128)}, u32[]{:S(2)}) copy-start(f32[48,128]{1,0:T(8,128)} %get-tuple-element.35.w2x) | copy-start | bytes 73732
  44.5 10.4 %copy-start.5 = (f32[48,128]{1,0:T(8,128)S(1)}, f32[48,128]{1,0:T(8,128)}, u32[]{:S(2)}) copy-start(f32[48,128]{1,0:T(8,128)} %get-tuple-element.37.w1tx) | copy-start | bytes 73732
  44.6 10.4 %copy-start.6 = (f32[24,128]{1,0:T(8,128)S(1)}, f32[24,128]{1,0:T(8,128)}, u32[]{:S(2)}) copy-start(f32[24,128]{1,0:T(8,128)} %get-tuple-element.38.b2b) | copy-start | bytes 36868
  44.6 10.3 %collective-permute-start.4 = (f32[25,16,128]{2,1,0:T(8,128)S(1)}, f32[25,16,128]{2,1,0:T(8,128)S(1)}, u32[]{:S(2)}, u32[]{:S(2)}) collective-permute-start(f32[25,16,128]{2,1,0:T(8,128)S(1)} %get-tuple-element.32), channel_id=1, source_target_pairs={{0,48},{24,72},{48,0},{72,24},{96,144},{120,168},{144,96},{168,120... | collective-permute-start | bytes 614408 | tf_op jit(solution)/shard_map/ppermute | solution.py:505
  91.7 12.0 %all-to-all-start.2 = ((f32[8,24,128]{2,1,0:T(8,128)}), f32[8,24,128]{2,1,0:T(8,128)S(1)}, u32[]{:S(2)}, u32[]{:S(2)}) async-start(f32[8,24,128]{2,1,0:T(8,128)} %broadcast_in_dim.8), calls=%async_computation.2 | async-start | bytes 196608 | tf_op jit(solution)/shard_map/all_to_all | solution.py:517

commit v5 on v3

--- a/solution.py
+++ b/solution.py
@@ -224,33 +224,40 @@
     z[...] = z_own[...]
 
 
-def second_kernel(z_own, from_even, from_odd, z, to_near, to_far):
+def second_kernel(z_own, from_even, from_odd, z, next_rows, to_near, to_far):
     z[:, :, 4:12, :] = z_own[...]
 
-    def unpack(ref, way):
-        at = 0
-        for plane, unit, rows in y_pieces(way):
-            begin = 4 - rows if way == 1 else 12
-            z[plane, unit, begin : begin + rows, :] = ref[at : at + rows, :]
-            at += rows
+    def unpack(below, above):
+        for ref, way in ((below, 1), (above, -1)):
+            at = 0
+            for plane, unit, rows in y_pieces(way):
+                begin = 4 - rows if way == 1 else 12
+                z[plane, unit, begin : begin + rows, :] = ref[at : at + rows, :]
+                at += rows
+        next_rows[OWN : OWN + Y_ROWS, :] = below[...]
+        next_rows[OWN + Y_ROWS :, :] = above[...]
+
+    for plane in range(2):
+        for unit in range(UNITS):
+            at = (plane * UNITS + unit) * 8
+            next_rows[at : at + 8, :] = z_own[plane, unit]
 
     odd = lax.rem(lax.axis_index("gy"), 2)
 
     @pl.when(odd == 0)
     def _():
-        unpack(from_even, -1)
-        unpack(from_odd, 1)
+        unpack(from_odd, from_even)
 
     @pl.when(odd == 1)
     def _():
-        unpack(from_even, 1)
-        unpack(from_odd, -1)
+        unpack(from_even, from_odd)
 
     def pack(ref, way):
         at = 0
-        for count, plane, first in far_runs(way):
-            ref[at : at + count] = z[plane, first : first + count]
-            at += count
+        for plane, unit, begin, rows in far_pieces(way):
+            ref[at : at + rows, :] = z[plane, unit, begin : begin + rows, :]
+            at += rows
+        ref[at:, :] = jnp.zeros((FAR_ROWS - at, W), jnp.float32)
 
     low = lax.rem(lax.axis_index("gx"), 4) < 2
 
@@ -271,11 +278,24 @@
     return ((5, 1, 14), (14, 0, 5), (5, 0, Q), (1, 0, SOLID))
 
 
-FAR = 25
-
-
-def hold_kernel(f_in, f):
-    f[...] = f_in[...]
+def far_pieces(way):
+    below = {piece[:2]: piece[2] for piece in y_pieces(1)}
+    above = {piece[:2]: piece[2] for piece in y_pieces(-1)}
+    units = [(plane, first + i) for count, plane, first in far_runs(way) for i in range(count)]
+    pieces = [(plane, unit, 4, 8) for plane, unit in units]
+    for key in units:
+        pieces.append((*key, 4 - below[key], below[key]))
+        pieces.append((*key, 12, above[key]))
+    return pieces
+
+
+FAR_ROWS = 344
+OWN = 2 * UNITS * 8
+
+
+def hold_kernel(f_far, z_odd, token):
+    del f_far, z_odd
+    token[...] = jnp.zeros(token.shape, jnp.float32)
 
 
 PLANES = 10
@@ -284,26 +304,15 @@
 
 def third_kernel(
     scale,
-    s0, z_own, z_even, z_odd, f_near, f_far, w1x, w2x, w2tx, w1tx, b2b,
+    s0, z_own, z_even, z_odd, f_near, f_far, w1x, w2x, w2tx, w1tx, b2b, token,
     final_hbm, grad_hbm, sums,
     final, grad, out_sems, zs, s1, p2, s2, p3, gp, g, acc1, acc2, sems,
 ):
     index = lax.axis_index("gx")
     odd = lax.rem(index, 2)
-    high = lax.rem(index, 4) // 2
-    copies = [
-        (z_even, zs.at[pl.ds(6 - 4 * odd, 2)]),
-        (z_own, zs.at[4:6]),
-        (z_odd, zs.at[pl.ds(2 + 4 * odd, 2)]),
-    ]
-    for ref, left in ((f_near, high), (f_far, 1 - high)):
-        at = 0
-        for (count, plane, first), (_, plane_r, first_r) in zip(far_runs(1), far_runs(-1)):
-            plane_r += 8
-            x = plane_r + left * (plane - plane_r)
-            unit = first_r + left * (first - first_r)
-            copies.append((ref.at[at : at + count], zs.at[x, pl.ds(unit, count)]))
-            at += count
+    low = lax.rem(index, 4) < 2
+    del token
+    copies = [(z_even, zs.at[pl.ds(6 - 4 * odd, 2)]), (z_own, zs.at[4:6])]
     copies = [pltpu.make_async_copy(a, b, sems.at[i]) for i, (a, b) in enumerate(copies)]
     for copy in copies:
         copy.start()
@@ -321,6 +330,31 @@
     for plane in range(6):
         for i in range(ROWS):
             gp[plane, i * T + 16 : (i + 1) * T, :] = jnp.zeros((8, W), jnp.float32)
+
+    for plane in range(2):
+        for unit in range(UNITS):
+            at = (plane * UNITS + unit) * 8
+            zs[2 + 4 * odd + plane, unit, 4:12, :] = z_odd[at : at + 8, :]
+    for way, at in ((1, OWN), (-1, OWN + Y_ROWS)):
+        for plane, unit, count in y_pieces(way):
+            begin = 4 - count if way == 1 else 12
+            zs[2 + 4 * odd + plane, unit, begin : begin + count, :] = z_odd[at : at + count, :]
+            at += count
+
+    def unpack(left, right):
+        for ref, way, base in ((left, 1, 0), (right, -1, 8)):
+            at = 0
+            for plane, unit, begin, count in far_pieces(way):
+                zs[base + plane, unit, begin : begin + count, :] = ref[at : at + count, :]
+                at += count
+
+    @pl.when(low)
+    def _():
+        unpack(f_far, f_near)
+
+    @pl.when(jnp.logical_not(low))
+    def _():
+        unpack(f_near, f_far)
 
     for copy in copies:
         copy.wait()
@@ -587,25 +621,31 @@
         compiler_params=PARAMS,
         name="near",
     )(z)
-    z, to_near, to_far = pl.pallas_call(
+    z, next_rows, to_near, to_far = pl.pallas_call(
         second_kernel,
-        out_shape=(shape(2, UNITS, ROWS, W), shape(FAR, ROWS, W), shape(FAR, ROWS, W)),
+        out_shape=(
+            shape(2, UNITS, ROWS, W),
+            shape(OWN + 2 * Y_ROWS, W),
+            shape(FAR_ROWS, W),
+            shape(FAR_ROWS, W),
+        ),
         compiler_params=PARAMS,
         name="second",
     )(z, from_even, from_odd)
 
-    z_odd = swap_odd(z, "gx")
+    z_odd = swap_odd(next_rows, "gx")
     f_far = swap_odd(to_far, "gx", 2)
     f_near = swap_even(to_near, "gx", 2)
     z_even = swap_even(z, "gx")
 
-    f_far = pl.pallas_call(
+    token = pl.pallas_call(
         hold_kernel,
-        out_shape=shape(FAR, ROWS, W),
+        out_shape=shape(8, W),
+        in_specs=[pl.BlockSpec(memory_space=pl.ANY)] * 2,
         compiler_params=PARAMS,
         cost_estimate=pl.CostEstimate(flops=6 * 10**9, bytes_accessed=10**6, transcendentals=0),
         name="hold",
-    )(f_far)
+    )(f_far, z_odd)
 
     cells = 16 * W * lax.axis_size("gx") * lax.axis_size("gy")
     vmem = pl.BlockSpec(memory_space=pltpu.VMEM)
@@ -613,7 +653,7 @@
     final, grad, sums = pl.pallas_call(
         functools.partial(third_kernel, 1.0 / math.sqrt(cells)),
         out_shape=(shape(Q, 2, 8, W), shape(Q, 2, 8, W), shape(T, W)),
-        in_specs=[vmem] + [hbm] * 5 + [vmem] * 5,
+        in_specs=[vmem] + [hbm] * 2 + [vmem] * 8 + [hbm],
         out_specs=(hbm, hbm, vmem),
         scratch_shapes=[
             rows((Q, 2, 8, W), F32),
@@ -628,11 +668,11 @@
             rows((6, ROWS * T, W), F32),
             rows((2 * T, 2 * HID + 2 * T), F32),
             rows((2 * T, 2 * HID), F32),
-            pltpu.SemaphoreType.DMA((11,)),
+            pltpu.SemaphoreType.DMA((2,)),
         ],
         compiler_params=PARAMS,
         name="third",
-    )(s0, z, z_even, z_odd, f_near, f_far, w1x, w2x, w2tx, w1tx, b2b)
+    )(s0, z, z_even, z_odd, f_near, f_far, w1x, w2x, w2tx, w1tx, b2b, token)
 
     along_x, along_z, along_y = sum_groups()
     sums = spread(sums, along_x).sum(0)

time: 104 us -> 103 us (level)
  waiting for transfers between devices: 15.2 us -> 12.9 us
  blocking collectives: 38.2 us -> 39.8 us
    ppermute x3, starting transfers between devices: 8.32 us -> 12.9 us  [swap_even(): return lax.ppermute(x, axis, [(i, i ^ step) for i in range(count)])]
    ppermute x3, starting transfers between devices: 26.9 us -> 22.6 us  [swap_odd(): lax.ppermute(x, axis, [(i, (i + step if i & step else i - step) % count)...]
    ppermute x3, waiting for transfers between devices: 7.35 us -> 5.03 us  [swap_even(): return lax.ppermute(x, axis, [(i, i ^ step) for i in range(count)])]
    all_to_all x3, blocking collectives: 38.2 us -> 39.8 us  [spread(): lax.all_to_all(jnp.broadcast_to(x[None], (count,) + x.shape), ('gx', 'gy'...]
where the time goes in v5:
time: 103 us; the launch traced here: 102 us
  blocking collectives  39.8 us (39%)
  starting transfers between devices  35.5 us (34%)
  waiting for transfers between devices  12.9 us (13%)
  Pallas kernels  12.2 us (12%)
    all_to_all x3, blocking collectives, spread(): lax.all_to_all(jnp.broadcast_to(x[None], (count,) + x.shape), ('gx', 'gy'...  39.8 us
    ppermute x3, starting transfers between devices, swap_odd(): lax.ppermute(x, axis, [(i, (i + step if i & step else i - step) % count)...  22.6 us
    ppermute x3, starting transfers between devices, swap_even(): return lax.ppermute(x, axis, [(i, i ^ step) for i in range(count)])  12.9 us
    pallas_call x1, Pallas kernels, on_device(): pl.pallas_call(functools.partial(third_kernel, 1.0 / math.sqrt(cells)), o...  8.88 us
    ppermute x3, waiting for transfers between devices, swap_odd(): lax.ppermute(x, axis, [(i, (i + step if i & step else i - step) % count)...  7.86 us
    ppermute x3, waiting for transfers between devices, swap_even(): return lax.ppermute(x, axis, [(i, i ^ step) for i in range(count)])  5.03 us
    pallas_call x1, Pallas kernels, on_device(): pl.pallas_call(first_kernel, out_shape=(shape(2, UNITS, 8, W), shape(Y_RO...  2.49 us
  transfers between devices with their start and end apart: 6, of which 2 were waited for; matrix products, arithmetic and copies ran while one was open for 0% of the time, Pallas kernels for 0%

profile of v5, /device:TPU:2, one launch (start us, length us, event | category | flops | bytes accessed | tf_op | source)
XLA Modules:
  0.0 102.3 jit_solution(16737691834348546449)
XLA Ops:
  0.6 2.5 %first.1 = (f32[2,39,8,128]{3,2,1,0:T(8,128)}, f32[200,128]{1,0:T(8,128)}, f32[200,128]{1,0:T(8,128)}, f32[2,192,128]{2,1,0:T(8,128)}, f32[64,80]{1,0:T(8,128)},...) custom-call(f32[19,2,8,128]{3,2,1,0:T(8,128)} %start_hbm.1, ...), custom_call_target="tpu_custom_call" | custom-call | tf_op jit(solution)/shard_map/first/pallas_call | solution.py:585
  3.1 3.5 %collective-permute-start = (f32[200,128]{1,0:T(8,128)}, f32[200,128]{1,0:T(8,128)S(1)}, u32[]{:S(2)}, u32[]{:S(2)}) collective-permute-start(f32[200,128]{1,0:T(8,128)} %get-tuple-element.28), channel_id=1, source_target_pairs={{0,1},{1,0},{2,3},{3,2},{4,5},{5,4},{6,7},{7,6},{8,9},{9,8},{10,11... | collective-permute-start | bytes 307208 | tf_op jit(solution)/shard_map/ppermute | solution.py:540
  6.6 17.2 %collective-permute-start.1 = (f32[200,128]{1,0:T(8,128)}, f32[200,128]{1,0:T(8,128)S(1)}, u32[]{:S(2)}, u32[]{:S(2)}) collective-permute-start(f32[200,128]{1,0:T(8,128)} %get-tuple-element.29), channel_id=1, source_target_pairs={{0,23},{1,2},{2,1},{3,4},{4,3},{5,6},{6,5},{7,8},{8,7},{9,10},{10,... | collective-permute-start | bytes 307208 | tf_op jit(solution)/shard_map/ppermute | solution.py:545
  23.9 0.0 copy-start
  23.9 1.0 copy-done
  24.9 0.0 collective-permute-done.from_even
  24.9 7.9 %collective-permute-done.1.from_odd = f32[200,128]{1,0:T(8,128)S(1)} collective-permute-done((f32[200,128]{1,0:T(8,128)}, f32[200,128]{1,0:T(8,128)S(1)}, u32[]{:S(2)}, u32[]{:S(2)}) %collective-permute-start.1) | collective-permute-done | bytes 102432 | tf_op jit(solution)/shard_map/ppermute | solution.py:545
  32.7 0.2 second.1
  32.9 1.9 %collective-permute-start.3 = (f32[1024,128]{1,0:T(8,128)S(1)}, f32[1024,128]{1,0:T(8,128)S(1)}, u32[]{:S(2)}, u32[]{:S(2)}) collective-permute-start(f32[1024,128]{1,0:T(8,128)S(1)} %get-tuple-element.31), channel_id=1, source_target_pairs={{0,744},{24,48},{48,24},{72,96},{96,72},{120,144},{144,120},{168,1... | collective-permute-start | bytes 1572872 | tf_op jit(solution)/shard_map/ppermute | solution.py:545
  34.8 3.4 %collective-permute-start.5 = (f32[344,128]{1,0:T(8,128)S(1)}, f32[344,128]{1,0:T(8,128)S(1)}, u32[]{:S(2)}, u32[]{:S(2)}) collective-permute-start(f32[344,128]{1,0:T(8,128)S(1)} %get-tuple-element.33), channel_id=1, source_target_pairs={{0,720},{24,744},{48,96},{72,120},{96,48},{120,72},{144,192},{168,... | collective-permute-start | bytes 528392 | tf_op jit(solution)/shard_map/ppermute | solution.py:545
  38.2 2.9 %collective-permute-start.2 = (f32[2,39,16,128]{3,2,1,0:T(8,128)S(1)}, f32[2,39,16,128]{3,2,1,0:T(8,128)S(1)}, u32[]{:S(2)}, u32[]{:S(2)}) collective-permute-start(f32[2,39,16,128]{3,2,1,0:T(8,128)S(1)} %get-tuple-element.30.z_own), channel_id=1, source_target_pairs={{0,24},{24,0},{48,72},{72,48},{96,120},{120,96},{144,168},{168,144... | collective-permute-start | bytes 1916936 | tf_op jit(solution)/shard_map/ppermute | solution.py:540
  41.2 0.0 copy-start.1
  41.2 6.5 %collective-permute-start.4 = (f32[344,128]{1,0:T(8,128)S(1)}, f32[344,128]{1,0:T(8,128)S(1)}, u32[]{:S(2)}, u32[]{:S(2)}) collective-permute-start(f32[344,128]{1,0:T(8,128)S(1)} %get-tuple-element.32), channel_id=1, source_target_pairs={{0,48},{24,72},{48,0},{72,24},{96,144},{120,168},{144,96},{168,120... | collective-permute-start | bytes 528392 | tf_op jit(solution)/shard_map/ppermute | solution.py:540
  47.7 0.0 collective-permute-done.5.f_far
  47.7 0.0 collective-permute-done.3.z_odd
  47.7 0.0 copy-start.2
  47.7 0.0 copy-start.3
  47.7 0.0 copy-start.4
  47.7 0.0 copy-start.5
  47.7 0.0 copy-start.6
  47.8 5.0 %collective-permute-done.4.f_near = f32[344,128]{1,0:T(8,128)S(1)} collective-permute-done((f32[344,128]{1,0:T(8,128)S(1)}, f32[344,128]{1,0:T(8,128)S(1)}, u32[]{:S(2)}, u32[]{:S(2)}) %collective-permute-start.4) | collective-permute-done | bytes 176160 | tf_op jit(solution)/shard_map/ppermute | solution.py:540
  52.8 0.0 collective-permute-done.2.z_even
  52.8 0.0 copy-done.1
  52.8 0.0 copy-done.2
  52.8 0.0 copy-done.3
  52.8 0.0 copy-done.4
  52.8 0.0 copy-done.5
  52.8 0.0 copy-done.6
  52.8 8.9 %third.1 = (f32[19,2,8,128]{3,2,1,0:T(8,128)}, f32[19,2,8,128]{3,2,1,0:T(8,128)}, f32[24,128]{1,0:T(8,128)S(1)}) custom-call(f32[2,192,128]{2,1,0:T(8,128)S(1)} %copy-done.1, f32[2,39,16,128]{3,2,1,0:T(8,128)S(1)} %get-tuple-element.30.z_own, f32[2,39,16,128]{3,2,1,0:T(8,128)S(1)} %collective-permute-done.2.z_even, ...), custom_call_target="tpu_custom_call" | custom-call | tf_op jit(solution)/shard_map/third/pallas_call | solution.py:653
  61.7 8.5 %all_to_all.15 = f32[8,24,128]{2,1,0:T(8,128)S(1)} all-to-all(f32[8,24,128]{2,1,0:T(8,128)S(1)} %broadcast_in_dim.6), channel_id=1, replica_groups={{0,24,48,72,96,120,144,168},{1,25,49,73,97,121,145,169},{2,26,50,74,98,..., dimensions={0} | all-to-all | bytes 196608 | tf_op jit(solution)/shard_map/all_to_all | solution.py:552
  70.2 18.8 %all_to_all.16 = f32[12,24,128]{2,1,0:T(8,128)S(1)} all-to-all(f32[12,24,128]{2,1,0:T(8,128)S(1)} %broadcast_in_dim.7), channel_id=1, replica_groups={{0,192,384,576,8,200,392,584,16,208,400,592},{1,193,385,577,9,201,393,5..., dimensions={0} | all-to-all | bytes 294912 | tf_op jit(solution)/shard_map/all_to_all | solution.py:552
  89.1 12.5 %all_to_all.17.parts = f32[8,24,128]{2,1,0:T(8,128)S(1)} all-to-all(f32[8,24,128]{2,1,0:T(8,128)S(1)} %broadcast_in_dim.8), channel_id=1, replica_groups={{0,1,2,3,4,5,6,7},{24,25,26,27,28,29,30,31},{48,49,50,51,52,53,54,55},{..., dimensions={0} | all-to-all | bytes 196608 | tf_op jit(solution)/shard_map/all_to_all | solution.py:552
  101.6 0.7 last.1
  (7 shorter events, 0.1 us)
Async XLA Ops:
  3.1 21.7 %collective-permute-start = (f32[200,128]{1,0:T(8,128)}, f32[200,128]{1,0:T(8,128)S(1)}, u32[]{:S(2)}, u32[]{:S(2)}) collective-permute-start(f32[200,128]{1,0:T(8,128)} %get-tuple-element.28), channel_id=1, source_target_pairs={{0,1},{1,0},{2,3},{3,2},{4,5},{5,4},{6,7},{7,6},{8,9},{9,8},{10,11... | collective-permute-start | bytes 307208 | tf_op jit(solution)/shard_map/ppermute | solution.py:540
  6.6 26.1 %collective-permute-start.1 = (f32[200,128]{1,0:T(8,128)}, f32[200,128]{1,0:T(8,128)S(1)}, u32[]{:S(2)}, u32[]{:S(2)}) collective-permute-start(f32[200,128]{1,0:T(8,128)} %get-tuple-element.29), channel_id=1, source_target_pairs={{0,23},{1,2},{2,1},{3,4},{4,3},{5,6},{6,5},{7,8},{8,7},{9,10},{10,... | collective-permute-start | bytes 307208 | tf_op jit(solution)/shard_map/ppermute | solution.py:545
  23.9 1.0 copy-start
  32.9 14.8 %collective-permute-start.3 = (f32[1024,128]{1,0:T(8,128)S(1)}, f32[1024,128]{1,0:T(8,128)S(1)}, u32[]{:S(2)}, u32[]{:S(2)}) collective-permute-start(f32[1024,128]{1,0:T(8,128)S(1)} %get-tuple-element.31), channel_id=1, source_target_pairs={{0,744},{24,48},{48,24},{72,96},{96,72},{120,144},{144,120},{168,1... | collective-permute-start | bytes 1572872 | tf_op jit(solution)/shard_map/ppermute | solution.py:545
  34.8 12.9 %collective-permute-start.5 = (f32[344,128]{1,0:T(8,128)S(1)}, f32[344,128]{1,0:T(8,128)S(1)}, u32[]{:S(2)}, u32[]{:S(2)}) collective-permute-start(f32[344,128]{1,0:T(8,128)S(1)} %get-tuple-element.33), channel_id=1, source_target_pairs={{0,720},{24,744},{48,96},{72,120},{96,48},{120,72},{144,192},{168,... | collective-permute-start | bytes 528392 | tf_op jit(solution)/shard_map/ppermute | solution.py:545
  38.2 14.6 %collective-permute-start.2 = (f32[2,39,16,128]{3,2,1,0:T(8,128)S(1)}, f32[2,39,16,128]{3,2,1,0:T(8,128)S(1)}, u32[]{:S(2)}, u32[]{:S(2)}) collective-permute-start(f32[2,39,16,128]{3,2,1,0:T(8,128)S(1)} %get-tuple-element.30.z_own), channel_id=1, source_target_pairs={{0,24},{24,0},{48,72},{72,48},{96,120},{120,96},{144,168},{168,144... | collective-permute-start | bytes 1916936 | tf_op jit(solution)/shard_map/ppermute | solution.py:540
  41.2 11.6 %copy-start.1 = (f32[2,192,128]{2,1,0:T(8,128)S(1)}, f32[2,192,128]{2,1,0:T(8,128)}, u32[]{:S(2)}) copy-start(f32[2,192,128]{2,1,0:T(8,128)} %get-tuple-element.26.s0) | copy-start | bytes 589828
  41.2 11.6 %collective-permute-start.4 = (f32[344,128]{1,0:T(8,128)S(1)}, f32[344,128]{1,0:T(8,128)S(1)}, u32[]{:S(2)}, u32[]{:S(2)}) collective-permute-start(f32[344,128]{1,0:T(8,128)S(1)} %get-tuple-element.32), channel_id=1, source_target_pairs={{0,48},{24,72},{48,0},{72,24},{96,144},{120,168},{144,96},{168,120... | collective-permute-start | bytes 528392 | tf_op jit(solution)/shard_map/ppermute | solution.py:540
  47.7 5.1 %copy-start.2 = (f32[64,80]{1,0:T(8,128)S(1)}, f32[64,80]{1,0:T(8,128)}, u32[]{:S(2)}) copy-start(f32[64,80]{1,0:T(8,128)} %get-tuple-element.34.w1x) | copy-start | bytes 61444
  47.7 5.1 %copy-start.3 = (f32[64,80]{1,0:T(8,128)S(1)}, f32[64,80]{1,0:T(8,128)}, u32[]{:S(2)}) copy-start(f32[64,80]{1,0:T(8,128)} %get-tuple-element.36.w2tx) | copy-start | bytes 61444
  47.7 5.1 %copy-start.4 = (f32[48,128]{1,0:T(8,128)S(1)}, f32[48,128]{1,0:T(8,128)}, u32[]{:S(2)}) copy-start(f32[48,128]{1,0:T(8,128)} %get-tuple-element.35.w2x) | copy-start | bytes 73732
  47.7 5.1 %copy-start.5 = (f32[48,128]{1,0:T(8,128)S(1)}, f32[48,128]{1,0:T(8,128)}, u32[]{:S(2)}) copy-start(f32[48,128]{1,0:T(8,128)} %get-tuple-element.37.w1tx) | copy-start | bytes 73732
  47.7 5.1 %copy-start.6 = (f32[24,128]{1,0:T(8,128)S(1)}, f32[24,128]{1,0:T(8,128)}, u32[]{:S(2)}) copy-start(f32[24,128]{1,0:T(8,128)} %get-tuple-element.38.b2b) | copy-start | bytes 36868

commit v6 on v5

--- a/solution.py
+++ b/solution.py
@@ -306,7 +306,7 @@
     scale,
     s0, z_own, z_even, z_odd, f_near, f_far, w1x, w2x, w2tx, w1tx, b2b, token,
     final_hbm, grad_hbm, sums,
-    final, grad, out_sems, zs, s1, p2, s2, p3, gp, g, acc1, acc2, sems,
+    packed, final, grad, out_sems, zs, s1, p2, s2, p3, gp, g, acc1, acc2, sems,
 ):
     index = lax.axis_index("gx")
     odd = lax.rem(index, 2)
@@ -517,22 +517,27 @@
     in_part = one[:, 0:HID] + one[:, HID : 2 * HID]
     out_part = two[:, 0:HID] + two[:, HID : 2 * HID]
     bias = one[:, 2 * HID : 2 * HID + T] + one[:, 2 * HID + T : 2 * HID + 2 * T]
-    sums[...] = jnp.zeros(sums.shape, jnp.float32)
-    sums[0:T, 0:HID] = in_part * scale
-    sums[0:Q, HID : 2 * HID] = out_part[0:Q, :] * scale
-    sums[ONE : ONE + 1, HID : HID + T] = bias[ONE : ONE + 1, :] * scale
+    packed[...] = jnp.zeros(packed.shape, jnp.float32)
+    packed[0:T, 0:HID] = in_part * scale
+    packed[0:Q, HID : 2 * HID] = out_part[0:Q, :] * scale
+    packed[ONE : ONE + 1, HID : HID + T] = bias[ONE : ONE + 1, :] * scale
+    for i in range(ONE + 1):
+        sums[i] = packed[i : i + 1, :]
     final_copy.wait()
     grad_copy.wait()
 
 
 def last_kernel(parts, grad_w_in_t, grad_b_in, grad_w_out, grad_b_out):
-    total = parts[0]
-    for i in range(1, parts.shape[0]):
-        total = total + parts[i]
-    grad_w_in_t[...] = total[0:Q, 0:HID]
-    grad_b_in[...] = total[ONE : ONE + 1, 0:HID]
-    grad_w_out[...] = total[0:Q, HID : 2 * HID]
-    grad_b_out[...] = total[ONE : ONE + 1, HID : HID + Q]
+    for row in range(ONE + 1):
+        total = parts[0, row]
+        for i in range(1, parts.shape[0]):
+            total = total + parts[i, row]
+        if row < Q:
+            grad_w_in_t[row : row + 1, :] = total[:, 0:HID]
+            grad_w_out[row : row + 1, :] = total[:, HID : 2 * HID]
+        else:
+            grad_b_in[...] = total[:, 0:HID]
+            grad_b_out[...] = total[:, HID : HID + Q]
 
 
 def swap_even(x, axis, step=1):
@@ -652,10 +657,11 @@
     hbm = pl.BlockSpec(memory_space=pl.ANY)
     final, grad, sums = pl.pallas_call(
         functools.partial(third_kernel, 1.0 / math.sqrt(cells)),
-        out_shape=(shape(Q, 2, 8, W), shape(Q, 2, 8, W), shape(T, W)),
+        out_shape=(shape(Q, 2, 8, W), shape(Q, 2, 8, W), shape(ONE + 1, 1, W)),
         in_specs=[vmem] + [hbm] * 2 + [vmem] * 8 + [hbm],
         out_specs=(hbm, hbm, vmem),
         scratch_shapes=[
+            rows((T, W), F32),
             rows((Q, 2, 8, W), F32),
             rows((Q, 2, 8, W), F32),
             pltpu.SemaphoreType.DMA((2,)),

time: 103 us -> 102 us (level)
  blocking collectives: 39.8 us -> 38.7 us
    all_to_all x3, blocking collectives: 39.8 us -> 38.7 us  [spread(): lax.all_to_all(jnp.broadcast_to(x[None], (count,) + x.shape), ('gx', 'gy'...]
where the time goes in v6:
time: 102 us
  blocking collectives  38.7 us (38%)
  starting transfers between devices  35.5 us (35%)
  waiting for transfers between devices  12.9 us (13%)
  Pallas kernels  12.3 us (12%)
  local copies, waits for them, and re-layouts  1.15 us (1%)
    all_to_all x3, blocking collectives, spread(): lax.all_to_all(jnp.broadcast_to(x[None], (count,) + x.shape), ('gx', 'gy'...  38.7 us
    ppermute x3, starting transfers between devices, swap_odd(): lax.ppermute(x, axis, [(i, (i + step if i & step else i - step) % count)...  22.6 us
    ppermute x3, starting transfers between devices, swap_even(): return lax.ppermute(x, axis, [(i, i ^ step) for i in range(count)])  12.9 us
    pallas_call x1, Pallas kernels, on_device(): pl.pallas_call(functools.partial(third_kernel, 1.0 / math.sqrt(cells)), o...  8.93 us
    ppermute x3, waiting for transfers between devices, swap_odd(): lax.ppermute(x, axis, [(i, (i + step if i & step else i - step) % count)...  7.86 us
    ppermute x3, waiting for transfers between devices, swap_even(): return lax.ppermute(x, axis, [(i, i ^ step) for i in range(count)])  5.03 us
    pallas_call x1, Pallas kernels, on_device(): pl.pallas_call(first_kernel, out_shape=(shape(2, UNITS, 8, W), shape(Y_RO...  2.49 us
  transfers between devices with their start and end apart: 6, of which 2 were waited for; matrix products, arithmetic and copies ran while one was open for 0% of the time, Pallas kernels for 0%

profile of v6, /device:TPU:2, one launch (start us, length us, event | category | flops | bytes accessed | tf_op | source)
XLA Modules:
  0.0 101.6 jit_solution(1301825994822750187)
XLA Ops:
  0.6 2.5 %first.1 = (f32[2,39,8,128]{3,2,1,0:T(8,128)}, f32[200,128]{1,0:T(8,128)}, f32[200,128]{1,0:T(8,128)}, f32[2,192,128]{2,1,0:T(8,128)}, f32[64,80]{1,0:T(8,128)},...) custom-call(f32[19,2,8,128]{3,2,1,0:T(8,128)} %start_hbm.1, ...), custom_call_target="tpu_custom_call" | custom-call | tf_op jit(solution)/shard_map/first/pallas_call | solution.py:590
  3.1 3.5 %collective-permute-start = (f32[200,128]{1,0:T(8,128)}, f32[200,128]{1,0:T(8,128)S(1)}, u32[]{:S(2)}, u32[]{:S(2)}) collective-permute-start(f32[200,128]{1,0:T(8,128)} %get-tuple-element.28), channel_id=1, source_target_pairs={{0,1},{1,0},{2,3},{3,2},{4,5},{5,4},{6,7},{7,6},{8,9},{9,8},{10,11... | collective-permute-start | bytes 307208 | tf_op jit(solution)/shard_map/ppermute | solution.py:545
  6.6 17.2 %collective-permute-start.1 = (f32[200,128]{1,0:T(8,128)}, f32[200,128]{1,0:T(8,128)S(1)}, u32[]{:S(2)}, u32[]{:S(2)}) collective-permute-start(f32[200,128]{1,0:T(8,128)} %get-tuple-element.29), channel_id=1, source_target_pairs={{0,23},{1,2},{2,1},{3,4},{4,3},{5,6},{6,5},{7,8},{8,7},{9,10},{10,... | collective-permute-start | bytes 307208 | tf_op jit(solution)/shard_map/ppermute | solution.py:550
  23.9 0.0 copy-start
  23.9 1.0 copy-done
  24.9 0.0 collective-permute-done.from_even
  24.9 7.9 %collective-permute-done.1.from_odd = f32[200,128]{1,0:T(8,128)S(1)} collective-permute-done((f32[200,128]{1,0:T(8,128)}, f32[200,128]{1,0:T(8,128)S(1)}, u32[]{:S(2)}, u32[]{:S(2)}) %collective-permute-start.1) | collective-permute-done | bytes 102432 | tf_op jit(solution)/shard_map/ppermute | solution.py:550
  32.7 0.2 second.1
  32.9 1.9 %collective-permute-start.3 = (f32[1024,128]{1,0:T(8,128)S(1)}, f32[1024,128]{1,0:T(8,128)S(1)}, u32[]{:S(2)}, u32[]{:S(2)}) collective-permute-start(f32[1024,128]{1,0:T(8,128)S(1)} %get-tuple-element.31), channel_id=1, source_target_pairs={{0,744},{24,48},{48,24},{72,96},{96,72},{120,144},{144,120},{168,1... | collective-permute-start | bytes 1572872 | tf_op jit(solution)/shard_map/ppermute | solution.py:550
  34.8 3.4 %collective-permute-start.5 = (f32[344,128]{1,0:T(8,128)S(1)}, f32[344,128]{1,0:T(8,128)S(1)}, u32[]{:S(2)}, u32[]{:S(2)}) collective-permute-start(f32[344,128]{1,0:T(8,128)S(1)} %get-tuple-element.33), channel_id=1, source_target_pairs={{0,720},{24,744},{48,96},{72,120},{96,48},{120,72},{144,192},{168,... | collective-permute-start | bytes 528392 | tf_op jit(solution)/shard_map/ppermute | solution.py:550
  38.2 2.9 %collective-permute-start.2 = (f32[2,39,16,128]{3,2,1,0:T(8,128)S(1)}, f32[2,39,16,128]{3,2,1,0:T(8,128)S(1)}, u32[]{:S(2)}, u32[]{:S(2)}) collective-permute-start(f32[2,39,16,128]{3,2,1,0:T(8,128)S(1)} %get-tuple-element.30.z_own), channel_id=1, source_target_pairs={{0,24},{24,0},{48,72},{72,48},{96,120},{120,96},{144,168},{168,144... | collective-permute-start | bytes 1916936 | tf_op jit(solution)/shard_map/ppermute | solution.py:545
  41.2 0.0 copy-start.1
  41.2 6.5 %collective-permute-start.4 = (f32[344,128]{1,0:T(8,128)S(1)}, f32[344,128]{1,0:T(8,128)S(1)}, u32[]{:S(2)}, u32[]{:S(2)}) collective-permute-start(f32[344,128]{1,0:T(8,128)S(1)} %get-tuple-element.32), channel_id=1, source_target_pairs={{0,48},{24,72},{48,0},{72,24},{96,144},{120,168},{144,96},{168,120... | collective-permute-start | bytes 528392 | tf_op jit(solution)/shard_map/ppermute | solution.py:545
  47.7 0.0 collective-permute-done.5.f_far
  47.7 0.0 collective-permute-done.3.z_odd
  47.7 0.0 copy-start.2
  47.7 0.0 copy-start.3
  47.7 0.0 copy-start.4
  47.7 0.0 copy-start.5
  47.7 0.0 copy-start.6
  47.8 5.0 %collective-permute-done.4.f_near = f32[344,128]{1,0:T(8,128)S(1)} collective-permute-done((f32[344,128]{1,0:T(8,128)S(1)}, f32[344,128]{1,0:T(8,128)S(1)}, u32[]{:S(2)}, u32[]{:S(2)}) %collective-permute-start.4) | collective-permute-done | bytes 176160 | tf_op jit(solution)/shard_map/ppermute | solution.py:545
  52.8 0.0 collective-permute-done.2.z_even
  52.8 0.0 copy-done.1
  52.8 0.0 copy-done.2
  52.8 0.0 copy-done.3
  52.8 0.0 copy-done.4
  52.8 0.0 copy-done.5
  52.8 0.0 copy-done.6
  52.8 8.9 %third.1 = (f32[19,2,8,128]{3,2,1,0:T(8,128)}, f32[19,2,8,128]{3,2,1,0:T(8,128)}, f32[20,1,128]{2,1,0:T(1,128)S(1)}) custom-call(f32[2,192,128]{2,1,0:T(8,128)S(1)} %copy-done.1, f32[2,39,16,128]{3,2,1,0:T(8,128)S(1)} %get-tuple-element.30.z_own, f32[2,39,16,128]{3,2,1,0:T(8,128)S(1)} %collective-permute-done.2.z_even, ...), custom_call_target="tpu_custom_call" | custom-call | tf_op jit(solution)/shard_map/third/pallas_call | solution.py:658
  61.8 8.4 %all_to_all.15 = f32[8,20,1,128]{3,2,1,0:T(1,128)S(1)} all-to-all(f32[8,20,1,128]{3,2,1,0:T(1,128)S(1)} %broadcast_in_dim.9), channel_id=1, replica_groups={{0,24,48,72,96,120,144,168},{1,25,49,73,97,121,145,169},{2,26,50,74,98,..., dimensions={0} | all-to-all | bytes 163840 | tf_op jit(solution)/shard_map/all_to_all | solution.py:557
  70.2 0.1 reduce_sum.18
  70.3 0.1 broadcast_in_dim.10
  70.4 18.0 %all_to_all.16 = f32[12,20,1,128]{3,2,1,0:T(1,128)S(1)} all-to-all(f32[12,20,1,128]{3,2,1,0:T(1,128)S(1)} %broadcast_in_dim.10), channel_id=1, replica_groups={{0,192,384,576,8,200,392,584,16,208,400,592},{1,193,385,577,9,201,393,5..., dimensions={0} | all-to-all | bytes 245760 | tf_op jit(solution)/shard_map/all_to_all | solution.py:557
  88.4 0.1 reduce_sum.19
  88.5 12.4 %all_to_all.17.parts = f32[8,20,1,128]{3,2,1,0:T(1,128)S(1)} all-to-all(f32[8,20,1,128]{3,2,1,0:T(1,128)S(1)} %broadcast_in_dim.11), channel_id=1, replica_groups={{0,1,2,3,4,5,6,7},{24,25,26,27,28,29,30,31},{48,49,50,51,52,53,54,55},{..., dimensions={0} | all-to-all | bytes 163840 | tf_op jit(solution)/shard_map/all_to_all | solution.py:557
  100.9 0.7 last.1
  (5 shorter events, 0.1 us)
Async XLA Ops:
  3.1 21.7 %collective-permute-start = (f32[200,128]{1,0:T(8,128)}, f32[200,128]{1,0:T(8,128)S(1)}, u32[]{:S(2)}, u32[]{:S(2)}) collective-permute-start(f32[200,128]{1,0:T(8,128)} %get-tuple-element.28), channel_id=1, source_target_pairs={{0,1},{1,0},{2,3},{3,2},{4,5},{5,4},{6,7},{7,6},{8,9},{9,8},{10,11... | collective-permute-start | bytes 307208 | tf_op jit(solution)/shard_map/ppermute | solution.py:545
  6.6 26.1 %collective-permute-start.1 = (f32[200,128]{1,0:T(8,128)}, f32[200,128]{1,0:T(8,128)S(1)}, u32[]{:S(2)}, u32[]{:S(2)}) collective-permute-start(f32[200,128]{1,0:T(8,128)} %get-tuple-element.29), channel_id=1, source_target_pairs={{0,23},{1,2},{2,1},{3,4},{4,3},{5,6},{6,5},{7,8},{8,7},{9,10},{10,... | collective-permute-start | bytes 307208 | tf_op jit(solution)/shard_map/ppermute | solution.py:550
  23.9 1.0 copy-start
  32.9 14.8 %collective-permute-start.3 = (f32[1024,128]{1,0:T(8,128)S(1)}, f32[1024,128]{1,0:T(8,128)S(1)}, u32[]{:S(2)}, u32[]{:S(2)}) collective-permute-start(f32[1024,128]{1,0:T(8,128)S(1)} %get-tuple-element.31), channel_id=1, source_target_pairs={{0,744},{24,48},{48,24},{72,96},{96,72},{120,144},{144,120},{168,1... | collective-permute-start | bytes 1572872 | tf_op jit(solution)/shard_map/ppermute | solution.py:550
  34.8 12.9 %collective-permute-start.5 = (f32[344,128]{1,0:T(8,128)S(1)}, f32[344,128]{1,0:T(8,128)S(1)}, u32[]{:S(2)}, u32[]{:S(2)}) collective-permute-start(f32[344,128]{1,0:T(8,128)S(1)} %get-tuple-element.33), channel_id=1, source_target_pairs={{0,720},{24,744},{48,96},{72,120},{96,48},{120,72},{144,192},{168,... | collective-permute-start | bytes 528392 | tf_op jit(solution)/shard_map/ppermute | solution.py:550
  38.2 14.6 %collective-permute-start.2 = (f32[2,39,16,128]{3,2,1,0:T(8,128)S(1)}, f32[2,39,16,128]{3,2,1,0:T(8,128)S(1)}, u32[]{:S(2)}, u32[]{:S(2)}) collective-permute-start(f32[2,39,16,128]{3,2,1,0:T(8,128)S(1)} %get-tuple-element.30.z_own), channel_id=1, source_target_pairs={{0,24},{24,0},{48,72},{72,48},{96,120},{120,96},{144,168},{168,144... | collective-permute-start | bytes 1916936 | tf_op jit(solution)/shard_map/ppermute | solution.py:545
  41.2 11.6 %copy-start.1 = (f32[2,192,128]{2,1,0:T(8,128)S(1)}, f32[2,192,128]{2,1,0:T(8,128)}, u32[]{:S(2)}) copy-start(f32[2,192,128]{2,1,0:T(8,128)} %get-tuple-element.26.s0) | copy-start | bytes 589828
  41.2 11.6 %collective-permute-start.4 = (f32[344,128]{1,0:T(8,128)S(1)}, f32[344,128]{1,0:T(8,128)S(1)}, u32[]{:S(2)}, u32[]{:S(2)}) collective-permute-start(f32[344,128]{1,0:T(8,128)S(1)} %get-tuple-element.32), channel_id=1, source_target_pairs={{0,48},{24,72},{48,0},{72,24},{96,144},{120,168},{144,96},{168,120... | collective-permute-start | bytes 528392 | tf_op jit(solution)/shard_map/ppermute | solution.py:545
  47.7 5.1 %copy-start.2 = (f32[64,80]{1,0:T(8,128)S(1)}, f32[64,80]{1,0:T(8,128)}, u32[]{:S(2)}) copy-start(f32[64,80]{1,0:T(8,128)} %get-tuple-element.34.w1x) | copy-start | bytes 61444
  47.7 5.1 %copy-start.3 = (f32[64,80]{1,0:T(8,128)S(1)}, f32[64,80]{1,0:T(8,128)}, u32[]{:S(2)}) copy-start(f32[64,80]{1,0:T(8,128)} %get-tuple-element.36.w2tx) | copy-start | bytes 61444
  47.7 5.1 %copy-start.4 = (f32[48,128]{1,0:T(8,128)S(1)}, f32[48,128]{1,0:T(8,128)}, u32[]{:S(2)}) copy-start(f32[48,128]{1,0:T(8,128)} %get-tuple-element.35.w2x) | copy-start | bytes 73732
  47.7 5.1 %copy-start.5 = (f32[48,128]{1,0:T(8,128)S(1)}, f32[48,128]{1,0:T(8,128)}, u32[]{:S(2)}) copy-start(f32[48,128]{1,0:T(8,128)} %get-tuple-element.37.w1tx) | copy-start | bytes 73732
  47.7 5.1 %copy-start.6 = (f32[24,128]{1,0:T(8,128)S(1)}, f32[24,128]{1,0:T(8,128)}, u32[]{:S(2)}) copy-start(f32[24,128]{1,0:T(8,128)} %get-tuple-element.38.b2b) | copy-start | bytes 36868

commit v7 on v6

--- a/solution.py
+++ b/solution.py
@@ -681,14 +681,14 @@
     )(s0, z, z_even, z_odd, f_near, f_far, w1x, w2x, w2tx, w1tx, b2b, token)
 
     along_x, along_z, along_y = sum_groups()
-    sums = spread(sums, along_x).sum(0)
+    sums = spread(sums, along_y).sum(0)
     sums = spread(sums, along_z).sum(0)
     grad_w_in_t, grad_b_in, grad_w_out, grad_b_out = pl.pallas_call(
         last_kernel,
         out_shape=(shape(Q, HID), shape(1, HID), shape(Q, HID), shape(1, Q)),
         compiler_params=PARAMS,
         name="last",
-    )(spread(sums, along_y))
+    )(spread(sums, along_x))
     return final, grad, grad_w_in_t.T, grad_b_in[0], grad_w_out, grad_b_out[0]
 
 

time: 102 us -> 103 us (level)
  the two profiles are of different devices: /device:TPU:2 before, /device:TPU:1 now
where the time goes in v7:
time: 103 us
  starting transfers between devices  42.7 us (41%)
  blocking collectives  38 us (37%)
  Pallas kernels  12.3 us (12%)
  waiting for transfers between devices  7.54 us (7%)
  local copies, waits for them, and re-layouts  1.15 us (1%)
    all_to_all x3, blocking collectives, spread(): lax.all_to_all(jnp.broadcast_to(x[None], (count,) + x.shape), ('gx', 'gy'...  38 us
    ppermute x3, starting transfers between devices, swap_odd(): lax.ppermute(x, axis, [(i, (i + step if i & step else i - step) % count)...  33.6 us
    ppermute x3, starting transfers between devices, swap_even(): return lax.ppermute(x, axis, [(i, i ^ step) for i in range(count)])  9.16 us
    pallas_call x1, Pallas kernels, on_device(): pl.pallas_call(functools.partial(third_kernel, 1.0 / math.sqrt(cells)), o...  8.93 us
    ppermute x3, waiting for transfers between devices, swap_even(): return lax.ppermute(x, axis, [(i, i ^ step) for i in range(count)])  4.65 us
    ppermute x3, waiting for transfers between devices, swap_odd(): lax.ppermute(x, axis, [(i, (i + step if i & step else i - step) % count)...  2.9 us
    pallas_call x1, Pallas kernels, on_device(): pl.pallas_call(first_kernel, out_shape=(shape(2, UNITS, 8, W), shape(Y_RO...  2.49 us
  transfers between devices with their start and end apart: 6, of which 3 were waited for; matrix products, arithmetic and copies ran while one was open for 0% of the time, Pallas kernels for 0%

profile of v7, /device:TPU:1, one launch (start us, length us, event | category | flops | bytes accessed | tf_op | source)
XLA Modules:
  0.0 102.8 jit_solution(13869931836157547886)
XLA Ops:
  0.6 2.5 %first.1 = (f32[2,39,8,128]{3,2,1,0:T(8,128)}, f32[200,128]{1,0:T(8,128)}, f32[200,128]{1,0:T(8,128)}, f32[2,192,128]{2,1,0:T(8,128)}, f32[64,80]{1,0:T(8,128)},...) custom-call(f32[19,2,8,128]{3,2,1,0:T(8,128)} %start_hbm.1, ...), custom_call_target="tpu_custom_call" | custom-call | tf_op jit(solution)/shard_map/first/pallas_call | solution.py:590
  3.1 4.0 %collective-permute-start = (f32[200,128]{1,0:T(8,128)}, f32[200,128]{1,0:T(8,128)S(1)}, u32[]{:S(2)}, u32[]{:S(2)}) collective-permute-start(f32[200,128]{1,0:T(8,128)} %get-tuple-element.28), channel_id=1, source_target_pairs={{0,1},{1,0},{2,3},{3,2},{4,5},{5,4},{6,7},{7,6},{8,9},{9,8},{10,11... | collective-permute-start | bytes 307208 | tf_op jit(solution)/shard_map/ppermute | solution.py:545
  7.2 17.0 %collective-permute-start.1 = (f32[200,128]{1,0:T(8,128)}, f32[200,128]{1,0:T(8,128)S(1)}, u32[]{:S(2)}, u32[]{:S(2)}) collective-permute-start(f32[200,128]{1,0:T(8,128)} %get-tuple-element.29), channel_id=1, source_target_pairs={{0,23},{1,2},{2,1},{3,4},{4,3},{5,6},{6,5},{7,8},{8,7},{9,10},{10,... | collective-permute-start | bytes 307208 | tf_op jit(solution)/shard_map/ppermute | solution.py:550
  24.1 0.0 copy-start
  24.1 1.0 copy-done
  25.1 0.0 collective-permute-done.from_even
  25.1 1.5 %collective-permute-done.1.from_odd = f32[200,128]{1,0:T(8,128)S(1)} collective-permute-done((f32[200,128]{1,0:T(8,128)}, f32[200,128]{1,0:T(8,128)S(1)}, u32[]{:S(2)}, u32[]{:S(2)}) %collective-permute-start.1) | collective-permute-done | bytes 102432 | tf_op jit(solution)/shard_map/ppermute | solution.py:550
  26.7 0.2 second.1
  26.8 10.6 %collective-permute-start.3 = (f32[1024,128]{1,0:T(8,128)S(1)}, f32[1024,128]{1,0:T(8,128)S(1)}, u32[]{:S(2)}, u32[]{:S(2)}) collective-permute-start(f32[1024,128]{1,0:T(8,128)S(1)} %get-tuple-element.31), channel_id=1, source_target_pairs={{0,744},{24,48},{48,24},{72,96},{96,72},{120,144},{144,120},{168,1... | collective-permute-start | bytes 1572872 | tf_op jit(solution)/shard_map/ppermute | solution.py:550
  37.4 6.1 %collective-permute-start.5 = (f32[344,128]{1,0:T(8,128)S(1)}, f32[344,128]{1,0:T(8,128)S(1)}, u32[]{:S(2)}, u32[]{:S(2)}) collective-permute-start(f32[344,128]{1,0:T(8,128)S(1)} %get-tuple-element.33), channel_id=1, source_target_pairs={{0,720},{24,744},{48,96},{72,120},{96,48},{120,72},{144,192},{168,... | collective-permute-start | bytes 528392 | tf_op jit(solution)/shard_map/ppermute | solution.py:550
  43.5 3.1 %collective-permute-start.2 = (f32[2,39,16,128]{3,2,1,0:T(8,128)S(1)}, f32[2,39,16,128]{3,2,1,0:T(8,128)S(1)}, u32[]{:S(2)}, u32[]{:S(2)}) collective-permute-start(f32[2,39,16,128]{3,2,1,0:T(8,128)S(1)} %get-tuple-element.30.z_own), channel_id=1, source_target_pairs={{0,24},{24,0},{48,72},{72,48},{96,120},{120,96},{144,168},{168,144... | collective-permute-start | bytes 1916936 | tf_op jit(solution)/shard_map/ppermute | solution.py:545
  46.6 0.0 copy-start.1
  46.6 2.1 %collective-permute-start.4 = (f32[344,128]{1,0:T(8,128)S(1)}, f32[344,128]{1,0:T(8,128)S(1)}, u32[]{:S(2)}, u32[]{:S(2)}) collective-permute-start(f32[344,128]{1,0:T(8,128)S(1)} %get-tuple-element.32), channel_id=1, source_target_pairs={{0,48},{24,72},{48,0},{72,24},{96,144},{120,168},{144,96},{168,120... | collective-permute-start | bytes 528392 | tf_op jit(solution)/shard_map/ppermute | solution.py:545
  48.6 1.4 %collective-permute-done.5.f_far = f32[344,128]{1,0:T(8,128)S(1)} collective-permute-done((f32[344,128]{1,0:T(8,128)S(1)}, f32[344,128]{1,0:T(8,128)S(1)}, u32[]{:S(2)}, u32[]{:S(2)}) %collective-permute-start.5) | collective-permute-done | bytes 176160 | tf_op jit(solution)/shard_map/ppermute | solution.py:550
  50.0 0.0 collective-permute-done.3.z_odd
  50.0 0.0 copy-start.2
  50.0 0.0 copy-start.3
  50.0 0.0 copy-start.4
  50.0 0.0 copy-start.5
  50.0 0.0 copy-start.6
  50.1 4.6 %collective-permute-done.4.f_near = f32[344,128]{1,0:T(8,128)S(1)} collective-permute-done((f32[344,128]{1,0:T(8,128)S(1)}, f32[344,128]{1,0:T(8,128)S(1)}, u32[]{:S(2)}, u32[]{:S(2)}) %collective-permute-start.4) | collective-permute-done | bytes 176160 | tf_op jit(solution)/shard_map/ppermute | solution.py:545
  54.7 0.0 collective-permute-done.2.z_even
  54.7 0.0 copy-done.1
  54.7 0.0 copy-done.2
  54.7 0.0 copy-done.3
  54.7 0.0 copy-done.4
  54.7 0.0 copy-done.5
  54.7 0.0 copy-done.6
  54.7 8.9 %third.1 = (f32[19,2,8,128]{3,2,1,0:T(8,128)}, f32[19,2,8,128]{3,2,1,0:T(8,128)}, f32[20,1,128]{2,1,0:T(1,128)S(1)}) custom-call(f32[2,192,128]{2,1,0:T(8,128)S(1)} %copy-done.1, f32[2,39,16,128]{3,2,1,0:T(8,128)S(1)} %get-tuple-element.30.z_own, f32[2,39,16,128]{3,2,1,0:T(8,128)S(1)} %collective-permute-done.2.z_even, ...), custom_call_target="tpu_custom_call" | custom-call | tf_op jit(solution)/shard_map/third/pallas_call | solution.py:658
  63.8 9.8 %all_to_all.15 = f32[8,20,1,128]{3,2,1,0:T(1,128)S(1)} all-to-all(f32[8,20,1,128]{3,2,1,0:T(1,128)S(1)} %broadcast_in_dim.9), channel_id=1, replica_groups={{0,1,2,3,4,5,6,7},{24,25,26,27,28,29,30,31},{48,49,50,51,52,53,54,55},{..., dimensions={0} | all-to-all | bytes 163840 | tf_op jit(solution)/shard_map/all_to_all | solution.py:557
  73.6 0.1 reduce_sum.18
  73.6 0.1 broadcast_in_dim.10
  73.7 16.9 %all_to_all.16 = f32[12,20,1,128]{3,2,1,0:T(1,128)S(1)} all-to-all(f32[12,20,1,128]{3,2,1,0:T(1,128)S(1)} %broadcast_in_dim.10), channel_id=1, replica_groups={{0,192,384,576,8,200,392,584,16,208,400,592},{1,193,385,577,9,201,393,5..., dimensions={0} | all-to-all | bytes 245760 | tf_op jit(solution)/shard_map/all_to_all | solution.py:557
  90.6 0.1 reduce_sum.19
  90.7 11.4 %all_to_all.17.parts = f32[8,20,1,128]{3,2,1,0:T(1,128)S(1)} all-to-all(f32[8,20,1,128]{3,2,1,0:T(1,128)S(1)} %broadcast_in_dim.11), channel_id=1, replica_groups={{0,24,48,72,96,120,144,168},{1,25,49,73,97,121,145,169},{2,26,50,74,98,..., dimensions={0} | all-to-all | bytes 163840 | tf_op jit(solution)/shard_map/all_to_all | solution.py:557
  102.1 0.7 last.1
  (5 shorter events, 0.1 us)
Async XLA Ops:
  3.1 22.0 %collective-permute-start = (f32[200,128]{1,0:T(8,128)}, f32[200,128]{1,0:T(8,128)S(1)}, u32[]{:S(2)}, u32[]{:S(2)}) collective-permute-start(f32[200,128]{1,0:T(8,128)} %get-tuple-element.28), channel_id=1, source_target_pairs={{0,1},{1,0},{2,3},{3,2},{4,5},{5,4},{6,7},{7,6},{8,9},{9,8},{10,11... | collective-permute-start | bytes 307208 | tf_op jit(solution)/shard_map/ppermute | solution.py:545
  7.2 19.5 %collective-permute-start.1 = (f32[200,128]{1,0:T(8,128)}, f32[200,128]{1,0:T(8,128)S(1)}, u32[]{:S(2)}, u32[]{:S(2)}) collective-permute-start(f32[200,128]{1,0:T(8,128)} %get-tuple-element.29), channel_id=1, source_target_pairs={{0,23},{1,2},{2,1},{3,4},{4,3},{5,6},{6,5},{7,8},{8,7},{9,10},{10,... | collective-permute-start | bytes 307208 | tf_op jit(solution)/shard_map/ppermute | solution.py:550
  24.1 1.0 copy-start
  26.8 23.2 %collective-permute-start.3 = (f32[1024,128]{1,0:T(8,128)S(1)}, f32[1024,128]{1,0:T(8,128)S(1)}, u32[]{:S(2)}, u32[]{:S(2)}) collective-permute-start(f32[1024,128]{1,0:T(8,128)S(1)} %get-tuple-element.31), channel_id=1, source_target_pairs={{0,744},{24,48},{48,24},{72,96},{96,72},{120,144},{144,120},{168,1... | collective-permute-start | bytes 1572872 | tf_op jit(solution)/shard_map/ppermute | solution.py:550
  37.4 12.6 %collective-permute-start.5 = (f32[344,128]{1,0:T(8,128)S(1)}, f32[344,128]{1,0:T(8,128)S(1)}, u32[]{:S(2)}, u32[]{:S(2)}) collective-permute-start(f32[344,128]{1,0:T(8,128)S(1)} %get-tuple-element.33), channel_id=1, source_target_pairs={{0,720},{24,744},{48,96},{72,120},{96,48},{120,72},{144,192},{168,... | collective-permute-start | bytes 528392 | tf_op jit(solution)/shard_map/ppermute | solution.py:550
  43.5 11.2 %collective-permute-start.2 = (f32[2,39,16,128]{3,2,1,0:T(8,128)S(1)}, f32[2,39,16,128]{3,2,1,0:T(8,128)S(1)}, u32[]{:S(2)}, u32[]{:S(2)}) collective-permute-start(f32[2,39,16,128]{3,2,1,0:T(8,128)S(1)} %get-tuple-element.30.z_own), channel_id=1, source_target_pairs={{0,24},{24,0},{48,72},{72,48},{96,120},{120,96},{144,168},{168,144... | collective-permute-start | bytes 1916936 | tf_op jit(solution)/shard_map/ppermute | solution.py:545
  46.6 8.1 %copy-start.1 = (f32[2,192,128]{2,1,0:T(8,128)S(1)}, f32[2,192,128]{2,1,0:T(8,128)}, u32[]{:S(2)}) copy-start(f32[2,192,128]{2,1,0:T(8,128)} %get-tuple-element.26.s0) | copy-start | bytes 589828
  46.6 8.1 %collective-permute-start.4 = (f32[344,128]{1,0:T(8,128)S(1)}, f32[344,128]{1,0:T(8,128)S(1)}, u32[]{:S(2)}, u32[]{:S(2)}) collective-permute-start(f32[344,128]{1,0:T(8,128)S(1)} %get-tuple-element.32), channel_id=1, source_target_pairs={{0,48},{24,72},{48,0},{72,24},{96,144},{120,168},{144,96},{168,120... | collective-permute-start | bytes 528392 | tf_op jit(solution)/shard_map/ppermute | solution.py:545
  50.0 4.7 %copy-start.2 = (f32[64,80]{1,0:T(8,128)S(1)}, f32[64,80]{1,0:T(8,128)}, u32[]{:S(2)}) copy-start(f32[64,80]{1,0:T(8,128)} %get-tuple-element.34.w1x) | copy-start | bytes 61444
  50.0 4.7 %copy-start.3 = (f32[64,80]{1,0:T(8,128)S(1)}, f32[64,80]{1,0:T(8,128)}, u32[]{:S(2)}) copy-start(f32[64,80]{1,0:T(8,128)} %get-tuple-element.36.w2tx) | copy-start | bytes 61444
  50.0 4.7 %copy-start.4 = (f32[48,128]{1,0:T(8,128)S(1)}, f32[48,128]{1,0:T(8,128)}, u32[]{:S(2)}) copy-start(f32[48,128]{1,0:T(8,128)} %get-tuple-element.35.w2x) | copy-start | bytes 73732
  50.0 4.7 %copy-start.5 = (f32[48,128]{1,0:T(8,128)S(1)}, f32[48,128]{1,0:T(8,128)}, u32[]{:S(2)}) copy-start(f32[48,128]{1,0:T(8,128)} %get-tuple-element.37.w1tx) | copy-start | bytes 73732
  50.0 4.7 %copy-start.6 = (f32[24,128]{1,0:T(8,128)S(1)}, f32[24,128]{1,0:T(8,128)}, u32[]{:S(2)}) copy-start(f32[24,128]{1,0:T(8,128)} %get-tuple-element.38.b2b) | copy-start | bytes 36868
